TPU v7x, 1024 devices: a whole 4x4x32 slice. The times are simulated.
1024 devices in a mesh: seq: 128 (over z, y), head: 8 (over x, core).
Axes of the slice: x: 4, y: 4, z: 32, core: 2. Of those that a mesh axis runs over, the one named last changes fastest.
Arguments:
- query: bfloat16 [8192, 2048], P('seq', 'head'), may hold values from -16 to 16
- key_states: bfloat16 [8192, 2048], P('seq', 'head'), may hold values from -16 to 16
- value_states: bfloat16 [8192, 2048], P('seq', 'head'), may hold values from -6 to 6
- doc_ids: int32 [8192], P('seq'), may hold values from 0 to 3, never falling along the last dimension, each value on 1 to 4096 neighbouring positions
- out_weight: bfloat16 [2048, 4096], P('head', 'seq'), may hold values from -0.5 to 0.5
- residual: bfloat16 [8192, 4096], P('seq', 'head'), may hold values from -6 to 6
Outputs:
- mixed: bfloat16 [8192, 4096], P('seq', 'head')
Inputs may be any that keep to these rules, and one draw needn't show every extreme that they name: doc_ids never fall along the sequence; every document has 1 to 4096 positions, and one has exactly 4096.
All inputs are finite; a program needn't handle non-finite values.
Results may differ from a plain program's by a relative error of at most 0.0055.
Values may be sent and summed in bfloat16 or wider, within the bound.
No kernel may reach another device: no remote copies, remote signals or barrier semaphores. Data moves between devices by JAX's collectives and lax.ppermute only.
A program may use at most 64 MiB of HBM per device.

v0:
```python
import jax
import jax.numpy as jnp
from jax import lax
from jax.sharding import PartitionSpec as P

HEAD_DIM = 128


masked_score = -1e30


def in_one_piece(arrays, axis, dim, along):
    widths = [a.shape[along] for a in arrays]
    both = jnp.concatenate(arrays, axis=along)
    out = lax.all_gather(both, axis, axis=dim, tiled=True)
    return tuple(jnp.split(out, [sum(widths[:k]) for k in range(1, len(widths))], axis=along))


def split_up(x, dim, count):
    before, after = (x.shape[:dim], x.shape[dim + 1 :])
    return jnp.moveaxis(x.reshape(*before, count, -1, *after), dim, 0)


def sum_at_owner(x, axis, dim):
    tiles = split_up(x, dim, lax.axis_size(axis))
    arrived = lax.all_to_all(tiles, axis, split_axis=0, concat_axis=0, tiled=True)
    return arrived.sum(axis=0)


def to_heads(block):
    return block.reshape(block.shape[0], block.shape[1] // HEAD_DIM, HEAD_DIM)


def attend_block(state, queries, query_pos, query_docs, keys, values, key_pos, key_docs):
    run_max, run_sum, run_acc = state
    scores = jnp.einsum(
        "qhd,khd->hqk", queries, keys, preferred_element_type=jnp.float32
    ) * HEAD_DIM ** (-0.5)
    allowed = (key_pos[None, :] <= query_pos[:, None]) & (key_docs[None, :] == query_docs[:, None])
    scores = jnp.where(allowed[None], scores, masked_score)
    new_max = jnp.maximum(run_max, jnp.max(scores, axis=-1))
    weights = jnp.where(allowed[None], jnp.exp(scores - new_max[..., None]), 0.0)
    run_sum = jnp.sum(weights, axis=-1)
    run_acc = jnp.einsum(
        "hqk,khd->hqd", weights.astype(jnp.bfloat16), values, preferred_element_type=jnp.float32
    )
    return (new_max, run_sum, run_acc)


def shards(query, key_states, value_states, doc_ids, out_weight, residual):
    tok_rows = query.shape[0]
    heads = query.shape[1] // HEAD_DIM
    shard_index = lax.axis_index("seq")
    first_pos = shard_index * tok_rows
    groups = [(query, first_pos + jnp.arange(tok_rows, dtype=jnp.int32), doc_ids)]
    prepared = [(to_heads(block), block_pos, block_docs) for block, block_pos, block_docs in groups]
    initial = tuple(
        (
            (
                jnp.full((heads, block_pos.shape[0]), masked_score, jnp.float32),
                jnp.zeros((heads, block_pos.shape[0]), jnp.float32),
                jnp.zeros((heads, block_pos.shape[0], HEAD_DIM), jnp.float32),
            )
            for block, block_pos, block_docs in groups
        )
    )
    first_row = jnp.int32(0)
    keys, values, key_docs = (
        *in_one_piece((key_states, value_states), "seq", 0, 1),
        lax.all_gather(doc_ids, "seq", axis=0, tiled=True),
    )
    key_pos = jnp.arange(keys.shape[0], dtype=jnp.int32)
    key_heads = to_heads(keys)
    value_heads = to_heads(values)
    updated = []
    for member, state in zip(prepared, initial):
        queries, query_pos, query_docs = member

        def advance(inner, queries=queries, query_pos=query_pos, query_docs=query_docs):
            return attend_block(
                inner, queries, query_pos, query_docs, key_heads, value_heads, key_pos, key_docs
            )

        def unchanged(inner):
            return inner

        updated.append(lax.cond(first_row <= jnp.max(query_pos), advance, unchanged, state))
    finals = tuple(updated)
    outputs = []
    for run_max, run_sum, run_acc in finals:
        normed = run_acc / run_sum[..., None]
        outputs.append(
            jnp.transpose(normed, (1, 0, 2))
            .reshape(normed.shape[1], heads * HEAD_DIM)
            .astype(jnp.bfloat16)
        )
    attended = outputs[0]
    mapped = jnp.dot(
        attended,
        lax.all_gather(out_weight, "seq", axis=1, tiled=True),
        preferred_element_type=jnp.float32,
    )
    summed = sum_at_owner(mapped, "head", 1)
    return (residual.astype(jnp.float32) + summed).astype(jnp.bfloat16)


def solution(mesh):
    placed = (
        P("seq", "head"),
        P("seq", "head"),
        P("seq", "head"),
        P("seq"),
        P("head", "seq"),
        P("seq", "head"),
    )
    return jax.shard_map(
        shards, mesh=mesh, in_specs=placed, out_specs=P("seq", "head"), check_vma=False
    )
```

profile of v0, /device:TPU:1, one launch (start us, length us, event | category | flops | bytes accessed | tf_op | source)
XLA Modules:
  0.0 630.2 jit_solution(3303185766306719611)
XLA Ops:
  6.5 0.0 all-gather.3.cloned.1.call-start
  6.5 1.4 pad_maximum_fusion
  7.9 0.0 all-gather.3.cloned.1.call-update
  8.0 0.0 all-gather.5.cloned.1.call-start
  8.0 0.7 all-gather.5.cloned.1.call-update
  8.7 0.6 fusion.12
  9.9 1.2 dynamic-slice
  11.8 0.9 dynamic-update-slice
  12.6 458.4 %all-reduce = s32[8192]{0:T(1024)S(1)} all-reduce(s32[8192]{0:T(1024)S(1)} %dynamic-update-slice), channel_id=1, replica_groups=mesh['seq'=128,'head'=8] {'seq'}, use_global_device_ids=true, to_apply=%add | all-reduce | flops 8192 | bytes 65536
  471.0 0.0 all-gather.3.cloned.1.call-done
  471.0 20.2 %conditional.1 = (f32[2,64]{1,0:T(2,128)S(1)}, f32[2,64,128]{2,1,0:T(8,128)S(1)}) conditional(s32[]{:T(128)} %convert_element_type.22, () %tuple.13, (s32[8192]{0:T(1024)S(1)}, s32[64]{0:T(128)S(1)}, s32[8192]{0:T(1024)S(1)}, s32[64]{0:T(128)}, bf16[64,256]{1,0:T(8,128)(2,1)}, /*index=5*/bf16[8192,512]{1,0:T(8,128)(2,1)}) %tuple.14), branch_computations={%region_1.0_spmd, %region_2.5_spmd} | conditional | flops 547880832 | bytes 56922696 | solution.py:87
  471.1 11.4 %copy.18 = bf16[8192,512]{0,1:T(8,128)(2,1)} copy(bf16[8192,512]{1,0:T(8,128)(2,1)} %get-tuple-element.40) | data formatting | bytes 16777216 | tf_op jit(solution)/shard_map
  482.4 0.0 copy-start.2
  482.4 0.0 copy-start.1
  482.4 3.9 fusion.13
  486.4 0.0 copy-done.2
  486.4 0.5 compare_and_fusion
  486.8 0.0 copy-done.1
  486.9 1.5 fusion.14
  488.4 1.2 fusion.2
  489.6 1.6 fusion.3
  491.2 0.0 copy-start
  491.2 0.1 fusion.11
  491.4 55.0 %all-gather.5.cloned.1.call-done = bf16[256,4096]{0,1:T(8,128)(2,1)} async-done(((bf16[256,32]{0,1:T(8,128)(2,1)}), bf16[256,4096]{0,1:T(8,128)(2,1)}) %all-gather.5.cloned.1.call-update) | async-done | bytes 2097168 | tf_op jit(solution)/shard_map/all_gather | solution.py:100
  546.4 2.3 convolution_bitcast_fusion
  548.7 73.9 %all_to_all.5 = f32[8,64,512]{2,1,0:T(8,128)S(1)} all-to-all(f32[8,64,512]{2,1,0:T(8,128)S(1)} %convolution_bitcast_fusion), channel_id=1, replica_groups=mesh['seq'=128,'head'=8] {'head'}, dimensions={0} | all-to-all | bytes 2097152 | tf_op jit(solution)/shard_map/all_to_all | solution.py:26
  622.6 0.1 reduce_sum.18
  622.7 0.0 copy-done
  622.7 0.6 add_convert_fusion
  (6 shorter events, 0.1 us)
Async XLA Ops:
  6.5 464.5 %all-gather.3.cloned.1.call-start = ((), (), s32[]{:S(2)}) async-start(), calls=%async_computation.1 | async-start | bytes 8454144 | tf_op jit(solution)/shard_map/all_gather | solution.py:15
  8.0 538.4 %all-gather.5.cloned.1.call-start = ((), (), s32[]{:S(2)}) async-start(), calls=%async_computation.2 | async-start | bytes 2113536 | tf_op jit(solution)/shard_map/all_gather | solution.py:100
  482.4 3.9 copy-start.2
  482.4 4.4 copy-start.1
  491.2 131.5 %copy-start = (bf16[64,512]{1,0:T(8,128)(2,1)S(1)}, bf16[64,512]{1,0:T(8,128)(2,1)}, u32[]{:S(2)}) copy-start(bf16[64,512]{1,0:T(8,128)(2,1)} %param.13) | copy-start | bytes 196612
Sparse Core Ops, SparseCore 0:
  11.5 276.1 all-gather.2
  291.8 254.5 all-gather.4
where the time goes:
time: 631 us; the launch traced here: 630 us
  blocking collectives  532 us (84%)
  waiting for transfers between devices  55.7 us (9%)
  local copies, waits for them, and re-layouts  17.5 us (3%)
  between operations  14.6 us (2%)
    unnamed x1, blocking collectives  458 us
    all_to_all x1, blocking collectives, sum_at_owner(): lax.all_to_all(tiles, axis, split_axis=0, concat_axis=0, tiled=True)  73.9 us
    all_gather x1, waiting for transfers between devices, shards(): lax.all_gather(out_weight, 'seq', axis=1, tiled=True)  55 us
  transfers between devices with their start and end apart: 2, of which 1 were waited for; matrix products, arithmetic and copies ran while one was open for 4% of the time, Pallas kernels for 0%

commit v1 on v0

v1 whole, which is shorter than its diff:
```python
import jax
import jax.numpy as jnp
from jax import lax
from jax.experimental import pallas as pl
from jax.experimental.pallas import tpu as pltpu
from jax.sharding import Mesh, PartitionSpec as P

HEAD_DIM = 128
BLOCK = 64
LANES = 128
ROWS = 128
HIDDEN = -1e30
LOWEST = -1e29
LOG2_E = 1.4426950408889634

AXES = (("zh", 8), ("zp", 2), ("z2", 2), ("y", 4), ("x", 4), ("c", 2))
SEQ_AXES = ("zh", "zp", "z2", "y")
HEAD_AXES = ("x", "c")
PLANES = ("zh", "zp")
KEY_AXES = ("y", "x")
QUERY_AXES = ("z2", "c")


def exchange(tiles, axes):
    return lax.all_to_all(tiles, axes, split_axis=0, concat_axis=0, tiled=True)


def gather(block, axes):
    return exchange(jnp.broadcast_to(block[None], (lax.axis_size(axes), *block.shape)), axes)


def transposed(row):
    return jnp.broadcast_to(row, (LANES, LANES)).T


def attend_kernel(place_ref, query_ref, key_ref, out_ref, score_ref):
    z2, y, x, c = (place_ref[k] for k in range(4))
    stripe = 2 * BLOCK * 4

    def positions(z2, y, x, c, dim):
        index = lax.broadcasted_iota(jnp.int32, (ROWS, LANES), dim)
        return (z2 * 4 + y) * BLOCK + 16 * x + 8 * c + (index >> 3) * stripe + (index & 7)

    sources = key_ref.shape[0]
    factor = HEAD_DIM ** (-0.5) * LOG2_E
    for r in range(query_ref.shape[0]):
        queries = query_ref[r, 0:ROWS, :]
        query_docs = transposed(query_ref[r, ROWS : ROWS + 16, :].astype(jnp.float32)[0:1])
        query_pos = positions(r // 2, y, x, r % 2, 0)
        highest = jnp.full((ROWS, LANES), HIDDEN, jnp.float32)
        for s in range(sources):
            scores = lax.dot_general(
                queries,
                key_ref[s, 0:ROWS, :],
                (((1,), (1,)), ((), ())),
                preferred_element_type=jnp.float32,
            )
            key_docs = key_ref[s, 2 * ROWS : 2 * ROWS + 16, :].astype(jnp.float32)[0:1]
            key_pos = positions(z2, s // 4, s % 4, c, 1)
            visible = (key_pos <= query_pos) & (key_docs == query_docs)
            scores = jnp.where(visible, scores, HIDDEN)
            score_ref[s] = scores
            highest = jnp.maximum(highest, scores)
        row_max = jnp.maximum(jnp.max(highest, axis=1, keepdims=True), LOWEST)
        row_max = jnp.broadcast_to(row_max, (ROWS, LANES))
        total = jnp.zeros((ROWS, LANES), jnp.float32)
        mixed = jnp.zeros((ROWS, HEAD_DIM), jnp.float32)
        for s in range(sources):
            weights = jnp.exp2((score_ref[s] - row_max) * factor)
            total = total + weights
            mixed = mixed + jnp.dot(
                weights.astype(jnp.bfloat16),
                key_ref[s, ROWS : 2 * ROWS, :],
                preferred_element_type=jnp.float32,
            )
        row_sum = jnp.broadcast_to(jnp.sum(total, axis=1, keepdims=True), (ROWS, LANES))
        out_ref[r, 0:ROWS, :] = mixed
        out_ref[r, ROWS : ROWS + 8, :] = jnp.concatenate([row_max.T[0:4], row_sum.T[0:4]], axis=0)


def combine_kernel(part_ref, out_ref):
    parts = part_ref.shape[0]
    factor = HEAD_DIM ** (-0.5) * LOG2_E
    maxima = [part_ref[r, ROWS : ROWS + 1, :] for r in range(parts)]
    sums = [part_ref[r, ROWS + 4 : ROWS + 5, :] for r in range(parts)]
    row_max = maxima[0]
    for m in maxima[1:]:
        row_max = jnp.maximum(row_max, m)
    scales = [jnp.exp2((m - row_max) * factor) for m in maxima]
    row_sum = sum(scale * s for scale, s in zip(scales, sums))
    mixed = jnp.zeros((ROWS, HEAD_DIM), jnp.float32)
    for r in range(parts):
        mixed = mixed + part_ref[r, 0:ROWS, :] * transposed(scales[r] / row_sum)
    out_ref[...] = mixed.astype(out_ref.dtype)


def attend(place, queries, keys):
    parts = queries.shape[0]
    vmem = pl.BlockSpec(memory_space=pltpu.VMEM)
    return pl.pallas_call(
        attend_kernel,
        out_shape=jax.ShapeDtypeStruct((parts, ROWS + 8, LANES), jnp.float32),
        in_specs=[pl.BlockSpec(memory_space=pltpu.SMEM), vmem, vmem],
        out_specs=vmem,
        scratch_shapes=[pltpu.VMEM((keys.shape[0], ROWS, LANES), jnp.float32)],
        compiler_params=pltpu.CompilerParams(vmem_limit_bytes=24 << 20),
        cost_estimate=pl.CostEstimate(
            flops=4 * parts * ROWS * keys.shape[0] * ROWS * HEAD_DIM,
            bytes_accessed=4 << 20,
            transcendentals=parts * ROWS * keys.shape[0] * ROWS,
        ),
        name="attend",
    )(place, queries, keys)


def combine(parts):
    vmem = pl.BlockSpec(memory_space=pltpu.VMEM)
    return pl.pallas_call(
        combine_kernel,
        out_shape=jax.ShapeDtypeStruct((ROWS, HEAD_DIM), jnp.bfloat16),
        in_specs=[vmem],
        out_specs=vmem,
        compiler_params=pltpu.CompilerParams(vmem_limit_bytes=8 << 20),
        name="combine",
    )(parts)


def weight_columns(out_weight):
    own = out_weight.T
    columns, rows = own.shape
    by_zh = gather(own, "zh")
    by_head = exchange(by_zh, HEAD_AXES)
    by_zl = gather(by_head, ("zp", "z2"))
    zl, groups = by_zl.shape[:2]
    block = by_zl.transpose(0, 2, 1, 3).reshape(zl * columns, groups * rows)
    by_y = gather(block, "y").reshape(4, zl, columns, groups * rows)
    return by_y.transpose(1, 0, 2, 3).reshape(zl * 4 * columns, groups * rows)


def shards(query, key_states, value_states, doc_ids, out_weight, residual):
    groups = lax.axis_size(HEAD_AXES)
    planes = lax.axis_size(PLANES)
    each = BLOCK // groups
    x, c = lax.axis_index("x"), lax.axis_index("c")
    place = jnp.stack([lax.axis_index("z2"), lax.axis_index("y"), x, c])

    cut = [a.reshape(groups, each, -1) for a in (query, key_states, value_states)]
    by_rows = exchange(jnp.concatenate(cut, axis=1), HEAD_AXES)
    by_rows = by_rows.reshape(groups, 3 * each, 2, HEAD_DIM).transpose(0, 2, 1, 3)
    lane = jnp.arange(LANES, dtype=jnp.int32)
    chosen = jnp.arange(BLOCK)[:, None] == ((2 * x + c) * each + lane % each)[None, :]
    docs = jnp.sum(jnp.where(chosen, doc_ids[:, None], 0), axis=0).astype(jnp.bfloat16)
    docs = jnp.broadcast_to(docs, (planes, each, LANES))
    sent = jnp.concatenate([by_rows.reshape(planes, 3 * each, HEAD_DIM), docs], axis=1)
    by_head = exchange(sent, PLANES)
    queries, keys, values = (
        by_head[:, k * each : (k + 1) * each].reshape(ROWS, HEAD_DIM) for k in range(3)
    )
    mine = (lane // each)[None, :] == jnp.arange(planes)[:, None]
    row_docs = jnp.sum(
        jnp.where(mine, by_head[:, 3 * each].astype(jnp.float32), 0.0), axis=0
    ).astype(jnp.bfloat16)
    row_docs = jnp.broadcast_to(row_docs, (16, LANES))

    all_keys = gather(jnp.concatenate([keys, values, row_docs], axis=0), KEY_AXES)
    all_queries = gather(jnp.concatenate([queries, row_docs], axis=0), QUERY_AXES)
    parts = attend(place, all_queries, all_keys)
    attended = combine(exchange(parts, QUERY_AXES))

    back = exchange(attended.reshape(planes, each, HEAD_DIM), PLANES)
    everyone = gather(back, HEAD_AXES)
    everyone = everyone.transpose(0, 2, 1, 3).reshape(BLOCK, planes * HEAD_DIM)
    weight = weight_columns(out_weight)
    summed = lax.dot_general(
        everyone, weight, (((1,), (1,)), ((), ())), preferred_element_type=jnp.float32
    )
    return (residual.astype(jnp.float32) + summed).astype(jnp.bfloat16)


def solution(mesh):
    names, sizes = zip(*AXES)
    fine = Mesh(mesh.devices.reshape(sizes), names)
    seq, head = SEQ_AXES, HEAD_AXES
    placed = (P(seq, head), P(seq, head), P(seq, head), P(seq), P(head, seq), P(seq, head))
    return jax.shard_map(
        shards, mesh=fine, in_specs=placed, out_specs=P(seq, head), check_vma=False
    )
```

time: 631 us -> 245 us (0.39)
  blocking collectives: 532 us -> 64.2 us
  starting transfers between devices: 0.04 us -> 69.1 us
  waiting for transfers between devices: 55.7 us -> 92.7 us
  between operations: 14.6 us -> 0.12 us
  local copies, waits for them, and re-layouts: 17.5 us -> 6.72 us
    unnamed x1 -> x0, blocking collectives: 458 us -> none
    all_to_all x0 -> x9, waiting for transfers between devices: none -> 92.7 us  [exchange(): return lax.all_to_all(tiles, axes, split_axis=0, concat_axis=0, tiled=True)]
    all_to_all x0 -> x9, starting transfers between devices: none -> 69.1 us  [exchange(): return lax.all_to_all(tiles, axes, split_axis=0, concat_axis=0, tiled=True)]
    all_gather x2 -> x0, waiting for transfers between devices: 55 us -> none  [the longest x1 55 us: shards(): lax.all_gather(out_weight, 'seq', axis=1, tiled=True)]
    another operation x1 -> x0, local copies, waits for them, and re-layouts: 11.4 us -> none
    all_to_all x1 -> x2, blocking collectives: 73.9 us -> 64.2 us  [exchange(): return lax.all_to_all(tiles, axes, split_axis=0, concat_axis=0, tiled=True)]
  transfers between devices with their start and end apart: 2 -> 9, of which waited for: 1 -> 9; matrix products, arithmetic and copies ran while one was open for 4% -> 1% of each run, Pallas kernels for 0% -> 2%
where the time goes in v1:
time: 245 us; the launch traced here: 243 us
  waiting for transfers between devices  92.7 us (38%)
  starting transfers between devices  69.1 us (28%)
  blocking collectives  64.2 us (26%)
  local copies, waits for them, and re-layouts  6.72 us (3%)
  Pallas kernels  5.21 us (2%)
  matrix products  2.99 us (1%)
    all_to_all x9, waiting for transfers between devices, exchange(): return lax.all_to_all(tiles, axes, split_axis=0, concat_axis=0, tiled=True)  92.7 us
    all_to_all x9, starting transfers between devices, exchange(): return lax.all_to_all(tiles, axes, split_axis=0, concat_axis=0, tiled=True)  69.1 us
    all_to_all x2, blocking collectives, exchange(): return lax.all_to_all(tiles, axes, split_axis=0, concat_axis=0, tiled=True)  64.2 us
    broadcast_in_dim x6, local copies, waits for them, and re-layouts, gather(): jnp.broadcast_to(block[None], (lax.axis_size(axes), *block.shape))  5.01 us
  transfers between devices with their start and end apart: 9, of which 9 were waited for; matrix products, arithmetic and copies ran while one was open for 1% of the time, Pallas kernels for 2%

profile of v1, /device:TPU:1, one launch (start us, length us, event | category | flops | bytes accessed | tf_op | source)
XLA Modules:
  0.0 243.4 jit_solution(12329664285305439097)
XLA Ops:
  0.0 1.4 pad_maximum_fusion.1
  1.4 17.4 %all-to-all-start = ((bf16[8,24,256]{2,1,0:T(8,128)(2,1)}), bf16[8,24,256]{2,1,0:T(8,128)(2,1)S(1)}, u32[]{:S(2)}, u32[]{:S(2)}) async-start(bf16[8,24,256]{2,1,0:T(8,128)(2,1)} %pad_maximum_fusion.1), calls=%async_computation | async-start | bytes 196608 | tf_op jit(solution)/shard_map/all_to_all | solution.py:25
  18.9 0.7 select_reduce_fusion
  19.6 4.2 %all-to-all-done = bf16[8,24,256]{2,1,0:T(8,128)(2,1)S(1)} async-done(((bf16[8,24,256]{2,1,0:T(8,128)(2,1)}), bf16[8,24,256]{2,1,0:T(8,128)(2,1)S(1)}, u32[]{:S(2)}, u32[]{:S(2)}) %all-to-all-start) | async-done | bytes 98336 | tf_op jit(solution)/shard_map/all_to_all | solution.py:25
  23.9 38.6 %all_to_all.55 = bf16[16,32,128]{2,1,0:T(8,128)(2,1)S(1)} all-to-all(bf16[16,32,128]{2,1,0:T(8,128)(2,1)S(1)} %pad_maximum_fusion), channel_id=1, replica_groups=mesh['zh'=8,'zp'=2,'z2'=2,'y'=4,'x'=4,'c'=2] {'zh','zp'}, dimensions={0} | all-to-all | bytes 262144 | tf_op jit(solution)/shard_map/all_to_all | solution.py:25
  62.6 1.4 broadcast_in_dim.72
  64.0 10.7 %all-to-all-start.7 = ((bf16[8,32,256]{2,1,0:T(8,128)(2,1)}), bf16[8,32,256]{2,1,0:T(8,128)(2,1)}, u32[]{:S(2)}, u32[]{:S(2)}) async-start(bf16[8,32,256]{2,1,0:T(8,128)(2,1)} %broadcast_in_dim.72), calls=%async_computation.7 | async-start | bytes 262144 | tf_op jit(solution)/shard_map/all_to_all | solution.py:25
  74.7 23.3 %all-to-all-done.7 = bf16[8,32,256]{2,1,0:T(8,128)(2,1)} async-done(((bf16[8,32,256]{2,1,0:T(8,128)(2,1)}), bf16[8,32,256]{2,1,0:T(8,128)(2,1)}, u32[]{:S(2)}, u32[]{:S(2)}) %all-to-all-start.7) | async-done | bytes 131104 | tf_op jit(solution)/shard_map/all_to_all | solution.py:25
  98.0 0.7 broadcast_in_dim.39
  98.7 10.0 %all-to-all-start.2 = ((bf16[4,144,128]{2,1,0:T(8,128)(2,1)}), bf16[4,144,128]{2,1,0:T(8,128)(2,1)S(1)}, u32[]{:S(2)}, u32[]{:S(2)}) async-start(bf16[4,144,128]{2,1,0:T(8,128)(2,1)} %broadcast_in_dim.39), calls=%async_computation.2 | async-start | bytes 294912 | tf_op jit(solution)/shard_map/all_to_all | solution.py:25
  108.7 3.7 %all-to-all-done.2.query_ref = bf16[4,144,128]{2,1,0:T(8,128)(2,1)S(1)} async-done(((bf16[4,144,128]{2,1,0:T(8,128)(2,1)}), bf16[4,144,128]{2,1,0:T(8,128)(2,1)S(1)}, u32[]{:S(2)}, u32[]{:S(2)}) %all-to-all-start.2) | async-done | bytes 147488 | tf_op jit(solution)/shard_map/all_to_all | solution.py:25
  112.5 1.1 broadcast_in_dim.70
  113.6 5.4 %all-to-all-start.3 = ((bf16[16,272,128]{2,1,0:T(8,128)(2,1)}), bf16[16,272,128]{2,1,0:T(8,128)(2,1)S(1)}, u32[]{:S(2)}, u32[]{:S(2)}) async-start(bf16[16,272,128]{2,1,0:T(8,128)(2,1)} %broadcast_in_dim.70), calls=%async_computation.3 | async-start | bytes 2228224 | tf_op jit(solution)/shard_map/all_to_all | solution.py:25
  119.0 16.3 %all-to-all-done.3.key_ref = bf16[16,272,128]{2,1,0:T(8,128)(2,1)S(1)} async-done(((bf16[16,272,128]{2,1,0:T(8,128)(2,1)}), bf16[16,272,128]{2,1,0:T(8,128)(2,1)S(1)}, u32[]{:S(2)}, u32[]{:S(2)}) %all-to-all-start.3) | async-done | bytes 1114144 | tf_op jit(solution)/shard_map/all_to_all | solution.py:25
  135.3 6.3 %all-to-all-start.8 = ((bf16[8,32,256]{2,1,0:T(8,128)(2,1)}), bf16[8,32,256]{2,1,0:T(8,128)(2,1)S(1)}, u32[]{:S(2)}, u32[]{:S(2)}) async-start(bf16[8,32,256]{2,1,0:T(8,128)(2,1)} %all-to-all-done.7), calls=%async_computation.8 | async-start | bytes 262144 | tf_op jit(solution)/shard_map/all_to_all | solution.py:25
  141.6 0.1 pad_add_fusion.place_ref
  141.7 4.4 %attend.1 = f32[4,136,128]{2,1,0:T(8,128)} custom-call(s32[4]{0:T(128)S(1)} %pad_add_fusion.place_ref, bf16[4,144,128]{2,1,0:T(8,128)(2,1)S(1)} %all-to-all-done.2.query_ref, bf16[16,272,128]{2,1,0:T(8,128)(2,1)S(1)} %all-to-all-done.3.key_ref), custom_call_target="tpu_custom_call" | custom-call | flops 536870912 | bytes 4194304 | tf_op jit(solution)/shard_map/attend/pallas_call | solution.py:100
  146.1 0.8 all-to-all-done.8
  146.9 4.3 %all-to-all-start.4 = ((f32[4,136,128]{2,1,0:T(8,128)}), f32[4,136,128]{2,1,0:T(8,128)S(1)}, u32[]{:S(2)}, u32[]{:S(2)}) async-start(f32[4,136,128]{2,1,0:T(8,128)} %attend.1), calls=%async_computation.4 | async-start | bytes 557056 | tf_op jit(solution)/shard_map/all_to_all | solution.py:25
  151.2 0.1 copy.10
  151.3 5.3 %all-to-all-done.4.part_ref = f32[4,136,128]{2,1,0:T(8,128)S(1)} async-done(((f32[4,136,128]{2,1,0:T(8,128)}), f32[4,136,128]{2,1,0:T(8,128)S(1)}, u32[]{:S(2)}, u32[]{:S(2)}) %all-to-all-start.4) | async-done | bytes 278560 | tf_op jit(solution)/shard_map/all_to_all | solution.py:25
  156.5 0.8 broadcast_in_dim.73
  157.4 3.5 %all-to-all-start.9 = ((bf16[4,8,32,256]{3,1,2,0:T(8,128)(2,1)}), bf16[4,8,32,256]{3,1,2,0:T(8,128)(2,1)S(1)}, u32[]{:S(2)}, u32[]{:S(2)}) async-start(bf16[4,8,32,256]{3,1,2,0:T(8,128)(2,1)} %broadcast_in_dim.73), calls=%async_computation.9 | async-start | bytes 1048576 | tf_op jit(solution)/shard_map/all_to_all | solution.py:25
  160.8 0.8 combine.1
  161.6 13.2 %all-to-all-done.9 = bf16[4,8,32,256]{3,1,2,0:T(8,128)(2,1)S(1)} async-done(((bf16[4,8,32,256]{3,1,2,0:T(8,128)(2,1)}), bf16[4,8,32,256]{3,1,2,0:T(8,128)(2,1)S(1)}, u32[]{:S(2)}, u32[]{:S(2)}) %all-to-all-start.9) | async-done | bytes 524320 | tf_op jit(solution)/shard_map/all_to_all | solution.py:25
  174.8 4.1 %all-to-all-start.5 = ((bf16[16,8,128]{2,1,0:T(8,128)(2,1)}), bf16[16,8,128]{2,1,0:T(8,128)(2,1)S(1)}, u32[]{:S(2)}, u32[]{:S(2)}) async-start(bf16[16,8,128]{2,1,0:T(8,128)(2,1)} %bitcast.12), calls=%async_computation.5 | async-start | bytes 65536 | tf_op jit(solution)/shard_map/all_to_all | solution.py:25
  178.9 0.1 copy.12
  179.0 20.8 %all-to-all-done.5 = bf16[16,8,128]{2,1,0:T(8,128)(2,1)S(1)} async-done(((bf16[16,8,128]{2,1,0:T(8,128)(2,1)}), bf16[16,8,128]{2,1,0:T(8,128)(2,1)S(1)}, u32[]{:S(2)}, u32[]{:S(2)}) %all-to-all-start.5) | async-done | bytes 32800 | tf_op jit(solution)/shard_map/all_to_all | solution.py:25
  199.8 0.2 broadcast_in_dim.75
  200.1 25.6 %all_to_all.56 = bf16[4,128,2048]{2,1,0:T(8,128)(2,1)S(1)} all-to-all(bf16[4,128,2048]{2,1,0:T(8,128)(2,1)S(1)} %broadcast_in_dim.75), channel_id=1, replica_groups=mesh['zh'=8,'zp'=2,'z2'=2,'y'=4,'x'=4,'c'=2] {'y'}, dimensions={0} | all-to-all | bytes 4194304 | tf_op jit(solution)/shard_map/all_to_all | solution.py:25
  225.7 0.7 broadcast_in_dim.71
  226.4 7.5 %all-to-all-start.6 = ((bf16[8,16,8,128]{3,2,1,0:T(8,128)(2,1)}), bf16[8,16,8,128]{3,2,1,0:T(8,128)(2,1)S(1)}, u32[]{:S(2)}, u32[]{:S(2)}) async-start(bf16[8,16,8,128]{3,2,1,0:T(8,128)(2,1)} %broadcast_in_dim.71), calls=%async_computation.6 | async-start | bytes 524288 | tf_op jit(solution)/shard_map/all_to_all | solution.py:25
  233.9 0.0 copy-start
  233.9 1.5 copy.11
  235.4 5.0 %all-to-all-done.6 = bf16[8,16,8,128]{3,2,1,0:T(8,128)(2,1)S(1)} async-done(((bf16[8,16,8,128]{3,2,1,0:T(8,128)(2,1)}), bf16[8,16,8,128]{3,2,1,0:T(8,128)(2,1)S(1)}, u32[]{:S(2)}, u32[]{:S(2)}) %all-to-all-start.6) | async-done | bytes 262176 | tf_op jit(solution)/shard_map/all_to_all | solution.py:25
  240.4 0.0 copy-done
  240.4 3.0 %fusion = bf16[64,512]{1,0:T(8,128)(2,1)} fusion(bf16[512,2048]{1,0:T(8,128)(2,1)} %bitcast.32, bf16[8,16,8,128]{3,2,1,0:T(8,128)(2,1)S(1)} %all-to-all-done.6, bf16[64,512]{1,0:T(8,128)(2,1)S(1)} %copy-done), kind=kOutput, calls=%fused_computation.1 | convolution fusion | flops 134316032 | bytes 2490368 | tf_op jit(solution)/shard_map/dot_general | solution.py:174
  (13 shorter events, 0.1 us)
Async XLA Ops:
  1.4 22.4 %all-to-all-start = ((bf16[8,24,256]{2,1,0:T(8,128)(2,1)}), bf16[8,24,256]{2,1,0:T(8,128)(2,1)S(1)}, u32[]{:S(2)}, u32[]{:S(2)}) async-start(bf16[8,24,256]{2,1,0:T(8,128)(2,1)} %pad_maximum_fusion.1), calls=%async_computation | async-start | bytes 196608 | tf_op jit(solution)/shard_map/all_to_all | solution.py:25
  64.0 34.1 %all-to-all-start.7 = ((bf16[8,32,256]{2,1,0:T(8,128)(2,1)}), bf16[8,32,256]{2,1,0:T(8,128)(2,1)}, u32[]{:S(2)}, u32[]{:S(2)}) async-start(bf16[8,32,256]{2,1,0:T(8,128)(2,1)} %broadcast_in_dim.72), calls=%async_computation.7 | async-start | bytes 262144 | tf_op jit(solution)/shard_map/all_to_all | solution.py:25
  98.7 13.7 %all-to-all-start.2 = ((bf16[4,144,128]{2,1,0:T(8,128)(2,1)}), bf16[4,144,128]{2,1,0:T(8,128)(2,1)S(1)}, u32[]{:S(2)}, u32[]{:S(2)}) async-start(bf16[4,144,128]{2,1,0:T(8,128)(2,1)} %broadcast_in_dim.39), calls=%async_computation.2 | async-start | bytes 294912 | tf_op jit(solution)/shard_map/all_to_all | solution.py:25
  113.6 21.7 %all-to-all-start.3 = ((bf16[16,272,128]{2,1,0:T(8,128)(2,1)}), bf16[16,272,128]{2,1,0:T(8,128)(2,1)S(1)}, u32[]{:S(2)}, u32[]{:S(2)}) async-start(bf16[16,272,128]{2,1,0:T(8,128)(2,1)} %broadcast_in_dim.70), calls=%async_computation.3 | async-start | bytes 2228224 | tf_op jit(solution)/shard_map/all_to_all | solution.py:25
  135.3 11.6 %all-to-all-start.8 = ((bf16[8,32,256]{2,1,0:T(8,128)(2,1)}), bf16[8,32,256]{2,1,0:T(8,128)(2,1)S(1)}, u32[]{:S(2)}, u32[]{:S(2)}) async-start(bf16[8,32,256]{2,1,0:T(8,128)(2,1)} %all-to-all-done.7), calls=%async_computation.8 | async-start | bytes 262144 | tf_op jit(solution)/shard_map/all_to_all | solution.py:25
  146.9 9.6 %all-to-all-start.4 = ((f32[4,136,128]{2,1,0:T(8,128)}), f32[4,136,128]{2,1,0:T(8,128)S(1)}, u32[]{:S(2)}, u32[]{:S(2)}) async-start(f32[4,136,128]{2,1,0:T(8,128)} %attend.1), calls=%async_computation.4 | async-start | bytes 557056 | tf_op jit(solution)/shard_map/all_to_all | solution.py:25
  157.4 17.4 %all-to-all-start.9 = ((bf16[4,8,32,256]{3,1,2,0:T(8,128)(2,1)}), bf16[4,8,32,256]{3,1,2,0:T(8,128)(2,1)S(1)}, u32[]{:S(2)}, u32[]{:S(2)}) async-start(bf16[4,8,32,256]{3,1,2,0:T(8,128)(2,1)} %broadcast_in_dim.73), calls=%async_computation.9 | async-start | bytes 1048576 | tf_op jit(solution)/shard_map/all_to_all | solution.py:25
  174.8 25.0 %all-to-all-start.5 = ((bf16[16,8,128]{2,1,0:T(8,128)(2,1)}), bf16[16,8,128]{2,1,0:T(8,128)(2,1)S(1)}, u32[]{:S(2)}, u32[]{:S(2)}) async-start(bf16[16,8,128]{2,1,0:T(8,128)(2,1)} %bitcast.12), calls=%async_computation.5 | async-start | bytes 65536 | tf_op jit(solution)/shard_map/all_to_all | solution.py:25
  226.4 14.0 %all-to-all-start.6 = ((bf16[8,16,8,128]{3,2,1,0:T(8,128)(2,1)}), bf16[8,16,8,128]{3,2,1,0:T(8,128)(2,1)S(1)}, u32[]{:S(2)}, u32[]{:S(2)}) async-start(bf16[8,16,8,128]{3,2,1,0:T(8,128)(2,1)} %broadcast_in_dim.71), calls=%async_computation.6 | async-start | bytes 524288 | tf_op jit(solution)/shard_map/all_to_all | solution.py:25
  233.9 6.5 %copy-start = (bf16[64,512]{1,0:T(8,128)(2,1)S(1)}, bf16[64,512]{1,0:T(8,128)(2,1)}, u32[]{:S(2)}) copy-start(bf16[64,512]{1,0:T(8,128)(2,1)} %param.11) | copy-start | bytes 196612

commit v2 on v1

v2 whole, which is shorter than its diff:
```python
import itertools

import jax
import jax.numpy as jnp
from jax import lax
from jax.experimental import pallas as pl
from jax.experimental.pallas import tpu as pltpu
from jax.sharding import Mesh, PartitionSpec as P

HEAD_DIM = 128
BLOCK = 64
LANES = 128
EACH = 8
ROWS = 128
COLUMNS = 32
HIDDEN = -1e30
LOWEST = -1e29
FACTOR = HEAD_DIM ** (-0.5) * 1.4426950408889634

AXES = (("zh", 8), ("zp", 2), ("z2", 2), ("y", 4), ("x", 4), ("c", 2))
SEQ_AXES = ("zh", "zp", "z2", "y")
HEAD_AXES = ("x", "c")
PLANES = ("zh", "zp")
QUERY_AXES = ("z2", "y")

VMEM = pl.BlockSpec(memory_space=pltpu.VMEM)
SMEM = pl.BlockSpec(memory_space=pltpu.SMEM)


def exchange(tiles, axes):
    return lax.all_to_all(tiles, axes, split_axis=0, concat_axis=0, tiled=True)


def moved(block, where):
    sizes = (32, 4, 4, 2)
    places = itertools.product(*map(range, sizes))

    def flat(z, y, x, c):
        return ((z * 4 + y) * 4 + x) * 2 + c

    names = tuple(name for name, _ in AXES)
    return lax.ppermute(block, names, [(flat(*p), flat(*where(*p))) for p in places])


def transposed(row):
    return jnp.broadcast_to(row, (LANES, LANES)).T


def call(kernel, out_shape, in_specs, name, scratch=(), flops=0, moved_bytes=1 << 20):
    many = isinstance(out_shape, (list, tuple))
    return pl.pallas_call(
        kernel,
        out_shape=out_shape,
        in_specs=in_specs,
        out_specs=[VMEM] * len(out_shape) if many else VMEM,
        scratch_shapes=list(scratch),
        compiler_params=pltpu.CompilerParams(vmem_limit_bytes=24 << 20),
        cost_estimate=pl.CostEstimate(flops=flops, bytes_accessed=moved_bytes, transcendentals=0),
        name=name,
    )


WEIGHT_AT = 4 * EACH
SENT = WEIGHT_AT + 2 * COLUMNS


def send_kernel(rows_ref, docs_ref, weight_ref, out_ref):
    docs = jnp.broadcast_to(docs_ref[...].astype(jnp.float32), (EACH, LANES))
    weight = [weight_ref[:, k * LANES : (k + 1) * LANES] for k in range(2)]
    for group in range(rows_ref.shape[0]):
        for j in range(2):
            lanes = slice(j * LANES, (j + 1) * LANES)
            values = rows_ref[group, 2 * EACH : 3 * EACH, lanes].astype(jnp.float32)
            tile = out_ref.at[2 * group + j]
            tile[0 : 2 * EACH, :] = rows_ref[group, 0 : 2 * EACH, lanes]
            tile[2 * EACH : 4 * EACH, :] = jnp.concatenate([values, docs], axis=0).astype(
                jnp.bfloat16
            )
            for k in range(2):
                at = WEIGHT_AT + k * COLUMNS
                tile[at : at + COLUMNS, :] = weight[k]


DOCS_AT = 2 * ROWS
COLUMNS_AT = DOCS_AT + 16
GATHERED = COLUMNS_AT + 4 * COLUMNS


def gather_kernel(place_ref, came_ref, query_ref, key_ref):
    planes = came_ref.shape[0]
    first = [came_ref[i, 0 : 2 * EACH, :].astype(jnp.float32) for i in range(planes)]
    second = [came_ref[i, 2 * EACH : 4 * EACH, :].astype(jnp.float32) for i in range(planes)]
    queries, keys = (
        jnp.concatenate([t[k * EACH : (k + 1) * EACH] for t in first], axis=0).astype(jnp.bfloat16)
        for k in range(2)
    )
    values = jnp.concatenate([t[0:EACH] for t in second], axis=0).astype(jnp.bfloat16)
    lane = lax.broadcasted_iota(jnp.int32, (EACH, LANES), 1)
    docs = jnp.zeros((EACH, LANES), jnp.float32)
    for i, tile in enumerate(second):
        own = pltpu.roll(tile[EACH:], EACH * i, 1)
        docs = jnp.where(lane // EACH == i, own, docs)
    docs = jnp.concatenate([docs, docs], axis=0).astype(jnp.bfloat16)
    for s in range(query_ref.shape[0]):
        query_ref[s, 0:ROWS, :] = queries
        query_ref[s, ROWS : ROWS + 16, :] = docs
    for s in range(key_ref.shape[0]):
        key_ref[s, 0:ROWS, :] = keys
        key_ref[s, ROWS:DOCS_AT, :] = values
        key_ref[s, DOCS_AT:COLUMNS_AT, :] = docs
        for k in range(2):
            at = COLUMNS_AT + k * 2 * COLUMNS
            key_ref[s, at : at + 2 * COLUMNS, :] = came_ref[2 * s + k, WEIGHT_AT:SENT, :]


def attend_kernel(place_ref, query_ref, key_ref, out_ref, score_ref):
    z2, y, x, c = (place_ref[k] for k in range(1, 5))
    stripe = 2 * BLOCK * 4

    def positions(z2, y, x, c, dim):
        index = lax.broadcasted_iota(jnp.int32, (ROWS, LANES), dim)
        first = (z2 * 4 + y) * BLOCK + EACH * (2 * x + c)
        return first + (index >> 3) * stripe + (index & 7)

    sources = key_ref.shape[0]
    for r in range(query_ref.shape[0]):
        queries = query_ref[r, 0:ROWS, :]
        query_docs = transposed(query_ref[r, ROWS : ROWS + 16, :].astype(jnp.float32)[0:1])
        query_pos = positions(r // 4, r % 4, x, c, 0)
        highest = jnp.full((ROWS, LANES), HIDDEN, jnp.float32)
        for s in range(sources):
            scores = lax.dot_general(
                queries,
                key_ref[s, 0:ROWS, :],
                (((1,), (1,)), ((), ())),
                preferred_element_type=jnp.float32,
            )
            key_docs = key_ref[s, DOCS_AT:COLUMNS_AT, :].astype(jnp.float32)[0:1]
            key_pos = positions(z2, y, s // 2, s % 2, 1)
            visible = (key_pos <= query_pos) & (key_docs == query_docs)
            scores = jnp.where(visible, scores, HIDDEN)
            score_ref[s] = scores
            highest = jnp.maximum(highest, scores)
        row_max = jnp.maximum(jnp.max(highest, axis=1, keepdims=True), LOWEST)
        row_max = jnp.broadcast_to(row_max, (ROWS, LANES))
        total = jnp.zeros((ROWS, LANES), jnp.float32)
        mixed = jnp.zeros((ROWS, HEAD_DIM), jnp.float32)
        for s in range(sources):
            weights = jnp.exp2((score_ref[s] - row_max) * FACTOR)
            total = total + weights
            mixed = mixed + jnp.dot(
                weights.astype(jnp.bfloat16),
                key_ref[s, ROWS:DOCS_AT, :],
                preferred_element_type=jnp.float32,
            )
        row_sum = jnp.broadcast_to(jnp.sum(total, axis=1, keepdims=True), (ROWS, LANES))
        out_ref[r, 0:ROWS, :] = mixed
        out_ref[r, ROWS : ROWS + 8, :] = jnp.concatenate([row_max.T[0:4], row_sum.T[0:4]], axis=0)


def combine_kernel(part_ref, out_ref):
    parts = part_ref.shape[0]
    maxima = [part_ref[r, ROWS : ROWS + 1, :] for r in range(parts)]
    sums = [part_ref[r, ROWS + 4 : ROWS + 5, :] for r in range(parts)]
    row_max = maxima[0]
    for m in maxima[1:]:
        row_max = jnp.maximum(row_max, m)
    scales = [jnp.exp2((m - row_max) * FACTOR) for m in maxima]
    row_sum = sum(scale * s for scale, s in zip(scales, sums))
    mixed = jnp.zeros((ROWS, HEAD_DIM), jnp.float32)
    for r in range(parts):
        mixed = mixed + part_ref[r, 0:ROWS, :] * transposed(scales[r] / row_sum)
    out_ref[...] = mixed.astype(out_ref.dtype)


def product_kernel(place_ref, attended_ref, w0, w1, w2, w3, residual_ref, out_ref):
    z2, y = place_ref[1], place_ref[2]
    total = jnp.zeros(out_ref.shape, jnp.float32)
    for p in range(attended_ref.shape[0]):
        heads = [
            attended_ref[:, 2 * p + j].astype(jnp.float32).reshape(BLOCK, HEAD_DIM)
            for j in range(2)
        ]
        left = jnp.concatenate(heads, axis=1).astype(jnp.bfloat16)
        blocks = []
        for zl in range(4):
            own = (zl & 1) ^ z2
            for w in (w0, w1, w2, w3):
                halves = []
                for k in range(2):
                    at = ((zl >> 1) * 2 + k) * COLUMNS
                    halves.append(w[own, p, at : at + COLUMNS, :])
                blocks.append(jnp.concatenate(halves, axis=1))
        total = total + lax.dot_general(
            left,
            jnp.concatenate(blocks, axis=0),
            (((1,), (1,)), ((), ())),
            preferred_element_type=jnp.float32,
        )
    for zl in range(4):
        columns = slice(zl * LANES, (zl + 1) * LANES)
        summed = pltpu.roll(total[:, columns], y * COLUMNS, 1)
        out_ref[:, columns] = (residual_ref[:, columns].astype(jnp.float32) + summed).astype(
            out_ref.dtype
        )


def shards(query, key_states, value_states, doc_ids, out_weight, residual):
    groups = lax.axis_size(HEAD_AXES)
    planes = lax.axis_size(PLANES)
    spread = lax.axis_size(QUERY_AXES)
    bf16, f32 = jnp.bfloat16, jnp.float32
    index = [lax.axis_index(a) for a in (PLANES, "z2", "y", "x", "c")]
    place = jnp.stack(index)

    cut = [a.reshape(groups, EACH, -1) for a in (query, key_states, value_states)]
    by_rows = exchange(jnp.concatenate(cut, axis=1), HEAD_AXES)
    first = (2 * lax.axis_index("x") + lax.axis_index("c")) * EACH
    docs = jnp.roll(doc_ids, -first)
    docs = jnp.concatenate([docs, docs]).astype(bf16).reshape(1, LANES)
    sent = call(
        send_kernel, jax.ShapeDtypeStruct((planes, SENT, LANES), bf16), [VMEM] * 3, "send"
    )(by_rows, docs, out_weight.T)
    came = exchange(sent, PLANES)
    queries, keys = call(
        gather_kernel,
        [
            jax.ShapeDtypeStruct((spread, ROWS + 16, LANES), bf16),
            jax.ShapeDtypeStruct((groups, GATHERED, LANES), bf16),
        ],
        [SMEM, VMEM],
        "spread",
    )(place, came)
    keys = exchange(keys, HEAD_AXES)
    queries = exchange(queries, QUERY_AXES)

    columns = keys[:, COLUMNS_AT:]
    columns = jnp.stack([columns, moved(columns, lambda z, y, x, c: (z ^ 1, y, x, c))])
    weights = [columns]
    weights += [moved(columns, lambda z, y, x, c: (z, (y - k) % 4, x, c)) for k in (1, 2, 3)]

    parts = call(
        attend_kernel,
        jax.ShapeDtypeStruct((spread, ROWS + 8, LANES), f32),
        [SMEM, VMEM, VMEM],
        "attend",
        [pltpu.VMEM((groups, ROWS, LANES), f32)],
        4 * spread * ROWS * groups * ROWS * HEAD_DIM,
        2 << 20,
    )(place, queries, keys)
    parts = exchange(parts, QUERY_AXES)
    attended = call(
        combine_kernel, jax.ShapeDtypeStruct((ROWS, HEAD_DIM), bf16), [VMEM], "combine"
    )(parts)

    back = exchange(attended.reshape(planes, EACH, HEAD_DIM), PLANES)
    everyone = exchange(jnp.broadcast_to(back[None], (groups, *back.shape)), HEAD_AXES)
    return call(
        product_kernel,
        jax.ShapeDtypeStruct(residual.shape, residual.dtype),
        [SMEM] + [VMEM] * 6,
        "product",
        (),
        2 * BLOCK * 2048 * 512,
        3 << 20,
    )(place, everyone, *weights, residual)


def solution(mesh):
    names, sizes = zip(*AXES)
    fine = Mesh(mesh.devices.reshape(sizes), names)
    seq, head = SEQ_AXES, HEAD_AXES
    placed = (P(seq, head), P(seq, head), P(seq, head), P(seq), P(head, seq), P(seq, head))
    return jax.shard_map(
        shards, mesh=fine, in_specs=placed, out_specs=P(seq, head), check_vma=False
    )
```

time: 245 us -> 197 us (0.80)
  waiting for transfers between devices: 92.7 us -> 56.7 us
  starting transfers between devices: 69.1 us -> 60 us
  local copies, waits for them, and re-layouts: 6.72 us -> 1.58 us
  Pallas kernels: 5.21 us -> 8.98 us
  matrix products: 2.99 us -> 0 us
    all_to_all x9 -> x4, waiting for transfers between devices: 92.7 us -> 48.3 us  [exchange(): return lax.all_to_all(tiles, axes, split_axis=0, concat_axis=0, tiled=True)]
    all_to_all x9 -> x4, starting transfers between devices: 69.1 us -> 46.2 us  [exchange(): return lax.all_to_all(tiles, axes, split_axis=0, concat_axis=0, tiled=True)]
    ppermute x0 -> x4, starting transfers between devices: none -> 13.8 us  [moved(): lax.ppermute(block, names, [(flat(*p), flat(*where(*p))) for p in places])]
    ppermute x0 -> x4, waiting for transfers between devices: none -> 8.44 us  [moved(): lax.ppermute(block, names, [(flat(*p), flat(*where(*p))) for p in places])]
    broadcast_in_dim x8 -> x1, local copies, waits for them, and re-layouts: 5.02 us -> 0.73 us  [shards(): jnp.broadcast_to(back[None], (groups, *back.shape))]
    pallas_call x2 -> x5, Pallas kernels: 5.21 us -> 8.98 us  [the longest x1 5.26 us: shards(): call(attend_kernel, jax.ShapeDtypeStruct((spread, ROWS + 8, LANES), f32),...]
    dot_general x1 -> x0, matrix products: 2.99 us -> none  [shards(): lax.dot_general(everyone, weight, (((1,), (1,)), ((), ())), preferred_ele...]
    all_to_all x2 -> x3, blocking collectives: 64.2 us -> 66.6 us  [exchange(): return lax.all_to_all(tiles, axes, split_axis=0, concat_axis=0, tiled=True)]
  transfers between devices with their start and end apart: 9 -> 8, of which waited for: 9 -> 4; matrix products, arithmetic and copies ran while one was open for 1% -> 1% of each run, Pallas kernels for 2% -> 0%
where the time goes in v2:
time: 197 us; the launch traced here: 196 us
  blocking collectives  66.6 us (34%)
  starting transfers between devices  60 us (30%)
  waiting for transfers between devices  56.7 us (29%)
  Pallas kernels  8.98 us (5%)
    all_to_all x3, blocking collectives, exchange(): return lax.all_to_all(tiles, axes, split_axis=0, concat_axis=0, tiled=True)  66.6 us
    all_to_all x4, waiting for transfers between devices, exchange(): return lax.all_to_all(tiles, axes, split_axis=0, concat_axis=0, tiled=True)  48.3 us
    all_to_all x4, starting transfers between devices, exchange(): return lax.all_to_all(tiles, axes, split_axis=0, concat_axis=0, tiled=True)  46.2 us
    ppermute x4, starting transfers between devices, moved(): lax.ppermute(block, names, [(flat(*p), flat(*where(*p))) for p in places])  13.8 us
    ppermute x4, waiting for transfers between devices, moved(): lax.ppermute(block, names, [(flat(*p), flat(*where(*p))) for p in places])  8.44 us
    pallas_call x1, Pallas kernels, shards(): call(attend_kernel, jax.ShapeDtypeStruct((spread, ROWS + 8, LANES), f32),...  5.26 us
  transfers between devices with their start and end apart: 8, of which 4 were waited for; matrix products, arithmetic and copies ran while one was open for 1% of the time, Pallas kernels for 0%

profile of v2, /device:TPU:1, one launch (start us, length us, event | category | flops | bytes accessed | tf_op | source)
XLA Modules:
  0.0 195.7 jit_solution(6418371414513980266)
XLA Ops:
  0.0 1.4 pad_maximum_fusion.1
  1.4 17.4 %all-to-all-start = ((bf16[8,24,256]{2,1,0:T(8,128)(2,1)}), bf16[8,24,256]{2,1,0:T(8,128)(2,1)S(1)}, u32[]{:S(2)}, u32[]{:S(2)}) async-start(bf16[8,24,256]{2,1,0:T(8,128)(2,1)} %pad_maximum_fusion.1), calls=%async_computation | async-start | bytes 196608 | tf_op jit(solution)/shard_map/all_to_all | solution.py:31
  18.9 0.0 copy-start.1
  18.9 0.0 copy-start.2
  18.9 0.7 copy-done.2
  19.5 0.1 pad_add_fusion
  19.6 0.1 convert_bitcast_fusion
  19.7 0.1 pad_maximum_fusion.2.docs_ref
  19.8 4.1 %all-to-all-done.rows_ref = bf16[8,24,256]{2,1,0:T(8,128)(2,1)S(1)} async-done(((bf16[8,24,256]{2,1,0:T(8,128)(2,1)}), bf16[8,24,256]{2,1,0:T(8,128)(2,1)S(1)}, u32[]{:S(2)}, u32[]{:S(2)}) %all-to-all-start) | async-done | bytes 98336 | tf_op jit(solution)/shard_map/all_to_all | solution.py:31
  23.9 0.0 copy-done.1
  23.9 0.8 send.1
  24.7 16.5 %all-to-all-start.1 = ((bf16[16,96,128]{2,1,0:T(8,128)(2,1)}), bf16[16,96,128]{2,1,0:T(8,128)(2,1)S(1)}, u32[]{:S(2)}, u32[]{:S(2)}) async-start(bf16[16,96,128]{2,1,0:T(8,128)(2,1)} %send.1), calls=%async_computation.1 | async-start | bytes 786432 | tf_op jit(solution)/shard_map/all_to_all | solution.py:31
  41.2 0.1 stack.32.place_ref
  41.3 37.7 %all-to-all-done.1.came_ref = bf16[16,96,128]{2,1,0:T(8,128)(2,1)S(1)} async-done(((bf16[16,96,128]{2,1,0:T(8,128)(2,1)}), bf16[16,96,128]{2,1,0:T(8,128)(2,1)S(1)}, u32[]{:S(2)}, u32[]{:S(2)}) %all-to-all-start.1) | async-done | bytes 393248 | tf_op jit(solution)/shard_map/all_to_all | solution.py:31
  79.0 0.7 spread.1
  79.7 20.2 %all_to_all.35.key_ref = bf16[8,400,128]{2,1,0:T(8,128)(2,1)S(1)} all-to-all(bf16[8,400,128]{2,1,0:T(8,128)(2,1)S(1)} %get-tuple-element.8), channel_id=1, replica_groups=mesh['zh'=8,'zp'=2,'z2'=2,'y'=4,'x'=4,'c'=2] {'x','c'}, dimensions={0} | all-to-all | bytes 1638400 | tf_op jit(solution)/shard_map/all_to_all | solution.py:31
  99.9 16.8 %all_to_all.36.query_ref = bf16[8,144,128]{2,1,0:T(8,128)(2,1)S(1)} all-to-all(bf16[8,144,128]{2,1,0:T(8,128)(2,1)S(1)} %get-tuple-element.7), channel_id=1, replica_groups=mesh['zh'=8,'zp'=2,'z2'=2,'y'=4,'x'=4,'c'=2] {'z2','y'}, dimensions={0} | all-to-all | bytes 589824 | tf_op jit(solution)/shard_map/all_to_all | solution.py:31
  116.6 5.3 %attend.1 = f32[8,136,128]{2,1,0:T(8,128)} custom-call(s32[5]{0:T(128)S(1)} %stack.32.place_ref, bf16[8,144,128]{2,1,0:T(8,128)(2,1)S(1)} %all_to_all.36.query_ref, bf16[8,400,128]{2,1,0:T(8,128)(2,1)S(1)} %all_to_all.35.key_ref), custom_call_target="tpu_custom_call" | custom-call | flops 536870912 | bytes 2097152 | tf_op jit(solution)/shard_map/attend/pallas_call | solution.py:242
  121.9 3.5 %all-to-all-start.4 = ((f32[8,136,128]{2,1,0:T(8,128)}), f32[8,136,128]{2,1,0:T(8,128)S(1)}, u32[]{:S(2)}, u32[]{:S(2)}) async-start(f32[8,136,128]{2,1,0:T(8,128)} %attend.1), calls=%async_computation.4 | async-start | bytes 1114112 | tf_op jit(solution)/shard_map/all_to_all | solution.py:31
  125.4 0.1 slice_bitcast_fusion
  125.5 3.3 %collective-permute-start = (bf16[8,128,128]{2,1,0:T(8,128)(2,1)S(1)}, bf16[8,128,128]{2,1,0:T(8,128)(2,1)S(1)}, u32[]{:S(2)}, u32[]{:S(2)}) collective-permute-start(bf16[8,128,128]{2,1,0:T(8,128)(2,1)S(1)} %get-tuple-element.10), channel_id=1, source_target_pairs={{0,32},{1,33},{2,34},{3,35},{4,36},{5,37},{6,38},{7,39},{8,40},{9,... | collective-permute-start | bytes 786440 | tf_op jit(solution)/shard_map/ppermute | solution.py:42
  128.8 8.4 %collective-permute-done = bf16[8,128,128]{2,1,0:T(8,128)(2,1)S(1)} collective-permute-done((bf16[8,128,128]{2,1,0:T(8,128)(2,1)S(1)}, bf16[8,128,128]{2,1,0:T(8,128)(2,1)S(1)}, u32[]{:S(2)}, u32[]{:S(2)}) %collective-permute-start) | collective-permute-done | bytes 262176 | tf_op jit(solution)/shard_map/ppermute | solution.py:42
  137.3 0.1 pad_maximum_fusion.w0
  137.3 3.2 %collective-permute-start.3 = (bf16[2,8,128,128]{3,2,1,0:T(8,128)(2,1)S(1)}, bf16[2,8,128,128]{3,2,1,0:T(8,128)(2,1)S(1)}, u32[]{:S(2)}, u32[]{:S(2)}) collective-permute-start(bf16[2,8,128,128]{3,2,1,0:T(8,128)(2,1)S(1)} %pad_maximum_fusion.w0), channel_id=1, source_target_pairs={{0,8},{1,9},{2,10},{3,11},{4,12},{5,13},{6,14},{7,15},{8,16},{9,17... | collective-permute-start | bytes 1572872 | tf_op jit(solution)/shard_map/ppermute | solution.py:42
  140.5 4.3 %collective-permute-start.2 = (bf16[2,8,128,128]{3,2,1,0:T(8,128)(2,1)S(1)}, bf16[2,8,128,128]{3,2,1,0:T(8,128)(2,1)S(1)}, u32[]{:S(2)}, u32[]{:S(2)}) collective-permute-start(bf16[2,8,128,128]{3,2,1,0:T(8,128)(2,1)S(1)} %pad_maximum_fusion.w0), channel_id=1, source_target_pairs={{0,16},{1,17},{2,18},{3,19},{4,20},{5,21},{6,22},{7,23},{8,24},{9,... | collective-permute-start | bytes 1572872 | tf_op jit(solution)/shard_map/ppermute | solution.py:42
  144.8 3.0 %collective-permute-start.1 = (bf16[2,8,128,128]{3,2,1,0:T(8,128)(2,1)S(1)}, bf16[2,8,128,128]{3,2,1,0:T(8,128)(2,1)S(1)}, u32[]{:S(2)}, u32[]{:S(2)}) collective-permute-start(bf16[2,8,128,128]{3,2,1,0:T(8,128)(2,1)S(1)} %pad_maximum_fusion.w0), channel_id=1, source_target_pairs={{0,24},{1,25},{2,26},{3,27},{4,28},{5,29},{6,30},{7,31},{8,0},{9,1... | collective-permute-start | bytes 1572872 | tf_op jit(solution)/shard_map/ppermute | solution.py:42
  147.8 0.0 all-to-all-done.4.part_ref
  147.8 0.2 combine.1
  148.1 29.6 %all_to_all.37 = bf16[16,8,128]{2,1,0:T(8,128)(2,1)S(1)} all-to-all(bf16[16,8,128]{2,1,0:T(8,128)(2,1)S(1)} %bitcast.15), channel_id=1, replica_groups=mesh['zh'=8,'zp'=2,'z2'=2,'y'=4,'x'=4,'c'=2] {'zh','zp'}, dimensions={0} | all-to-all | bytes 65536 | tf_op jit(solution)/shard_map/all_to_all | solution.py:31
  177.7 0.7 broadcast_in_dim.2
  178.4 0.0 copy-start
  178.4 8.7 %all-to-all-start.6 = ((bf16[8,16,8,128]{3,2,1,0:T(8,128)(2,1)}), bf16[8,16,8,128]{3,2,1,0:T(8,128)(2,1)S(1)}, u32[]{:S(2)}, u32[]{:S(2)}) async-start(bf16[8,16,8,128]{3,2,1,0:T(8,128)(2,1)} %broadcast_in_dim.2), calls=%async_computation.6 | async-start | bytes 524288 | tf_op jit(solution)/shard_map/all_to_all | solution.py:31
  187.1 0.0 collective-permute-done.3.w3
  187.2 0.0 collective-permute-done.2.w2
  187.2 0.0 collective-permute-done.1.w1
  187.2 6.5 %all-to-all-done.6.attended_ref = bf16[8,16,8,128]{3,2,1,0:T(8,128)(2,1)S(1)} async-done(((bf16[8,16,8,128]{3,2,1,0:T(8,128)(2,1)}), bf16[8,16,8,128]{3,2,1,0:T(8,128)(2,1)S(1)}, u32[]{:S(2)}, u32[]{:S(2)}) %all-to-all-start.6) | async-done | bytes 262176 | tf_op jit(solution)/shard_map/all_to_all | solution.py:31
  193.7 0.0 copy-done
  193.7 2.0 %product.1 = bf16[64,512]{1,0:T(8,128)(2,1)} custom-call(s32[5]{0:T(128)S(1)} %stack.32.place_ref, bf16[8,16,8,128]{3,2,1,0:T(8,128)(2,1)S(1)} %all-to-all-done.6.attended_ref, bf16[2,8,128,128]{3,2,1,0:T(8,128)(2,1)S(1)} %pad_maximum_fusion.w0, bf16[2,8,128,128]{3,2,1,0:T(8,128)(2,1)S(1)} %collective-permute-done.1.w1, ...), custom_call_target="tpu_custom_call" | custom-call | flops 134217728 | bytes 3145728 | tf_op jit(solution)/shard_map/product/pallas_call | solution.py:258
Async XLA Ops:
  1.4 22.4 %all-to-all-start = ((bf16[8,24,256]{2,1,0:T(8,128)(2,1)}), bf16[8,24,256]{2,1,0:T(8,128)(2,1)S(1)}, u32[]{:S(2)}, u32[]{:S(2)}) async-start(bf16[8,24,256]{2,1,0:T(8,128)(2,1)} %pad_maximum_fusion.1), calls=%async_computation | async-start | bytes 196608 | tf_op jit(solution)/shard_map/all_to_all | solution.py:31
  18.9 5.0 %copy-start.1 = (bf16[256,32]{0,1:T(8,128)(2,1)S(1)}, bf16[256,32]{0,1:T(8,128)(2,1)}, u32[]{:S(2)}) copy-start(bf16[256,32]{0,1:T(8,128)(2,1)} %param.10) | copy-start | bytes 49156
  18.9 0.7 copy-start.2
  24.7 54.3 %all-to-all-start.1 = ((bf16[16,96,128]{2,1,0:T(8,128)(2,1)}), bf16[16,96,128]{2,1,0:T(8,128)(2,1)S(1)}, u32[]{:S(2)}, u32[]{:S(2)}) async-start(bf16[16,96,128]{2,1,0:T(8,128)(2,1)} %send.1), calls=%async_computation.1 | async-start | bytes 786432 | tf_op jit(solution)/shard_map/all_to_all | solution.py:31
  121.9 25.9 %all-to-all-start.4 = ((f32[8,136,128]{2,1,0:T(8,128)}), f32[8,136,128]{2,1,0:T(8,128)S(1)}, u32[]{:S(2)}, u32[]{:S(2)}) async-start(f32[8,136,128]{2,1,0:T(8,128)} %attend.1), calls=%async_computation.4 | async-start | bytes 1114112 | tf_op jit(solution)/shard_map/all_to_all | solution.py:31
  125.5 11.7 %collective-permute-start = (bf16[8,128,128]{2,1,0:T(8,128)(2,1)S(1)}, bf16[8,128,128]{2,1,0:T(8,128)(2,1)S(1)}, u32[]{:S(2)}, u32[]{:S(2)}) collective-permute-start(bf16[8,128,128]{2,1,0:T(8,128)(2,1)S(1)} %get-tuple-element.10), channel_id=1, source_target_pairs={{0,32},{1,33},{2,34},{3,35},{4,36},{5,37},{6,38},{7,39},{8,40},{9,... | collective-permute-start | bytes 786440 | tf_op jit(solution)/shard_map/ppermute | solution.py:42
  137.3 49.8 %collective-permute-start.3 = (bf16[2,8,128,128]{3,2,1,0:T(8,128)(2,1)S(1)}, bf16[2,8,128,128]{3,2,1,0:T(8,128)(2,1)S(1)}, u32[]{:S(2)}, u32[]{:S(2)}) collective-permute-start(bf16[2,8,128,128]{3,2,1,0:T(8,128)(2,1)S(1)} %pad_maximum_fusion.w0), channel_id=1, source_target_pairs={{0,8},{1,9},{2,10},{3,11},{4,12},{5,13},{6,14},{7,15},{8,16},{9,17... | collective-permute-start | bytes 1572872 | tf_op jit(solution)/shard_map/ppermute | solution.py:42
  140.5 46.7 %collective-permute-start.2 = (bf16[2,8,128,128]{3,2,1,0:T(8,128)(2,1)S(1)}, bf16[2,8,128,128]{3,2,1,0:T(8,128)(2,1)S(1)}, u32[]{:S(2)}, u32[]{:S(2)}) collective-permute-start(bf16[2,8,128,128]{3,2,1,0:T(8,128)(2,1)S(1)} %pad_maximum_fusion.w0), channel_id=1, source_target_pairs={{0,16},{1,17},{2,18},{3,19},{4,20},{5,21},{6,22},{7,23},{8,24},{9,... | collective-permute-start | bytes 1572872 | tf_op jit(solution)/shard_map/ppermute | solution.py:42
  144.8 42.3 %collective-permute-start.1 = (bf16[2,8,128,128]{3,2,1,0:T(8,128)(2,1)S(1)}, bf16[2,8,128,128]{3,2,1,0:T(8,128)(2,1)S(1)}, u32[]{:S(2)}, u32[]{:S(2)}) collective-permute-start(bf16[2,8,128,128]{3,2,1,0:T(8,128)(2,1)S(1)} %pad_maximum_fusion.w0), channel_id=1, source_target_pairs={{0,24},{1,25},{2,26},{3,27},{4,28},{5,29},{6,30},{7,31},{8,0},{9,1... | collective-permute-start | bytes 1572872 | tf_op jit(solution)/shard_map/ppermute | solution.py:42
  178.4 15.2 %copy-start = (bf16[64,512]{1,0:T(8,128)(2,1)S(1)}, bf16[64,512]{1,0:T(8,128)(2,1)}, u32[]{:S(2)}) copy-start(bf16[64,512]{1,0:T(8,128)(2,1)} %residual_ref.1) | copy-start | bytes 196612
  178.4 15.2 %all-to-all-start.6 = ((bf16[8,16,8,128]{3,2,1,0:T(8,128)(2,1)}), bf16[8,16,8,128]{3,2,1,0:T(8,128)(2,1)S(1)}, u32[]{:S(2)}, u32[]{:S(2)}) async-start(bf16[8,16,8,128]{3,2,1,0:T(8,128)(2,1)} %broadcast_in_dim.2), calls=%async_computation.6 | async-start | bytes 524288 | tf_op jit(solution)/shard_map/all_to_all | solution.py:31

commit v3 on v2

--- a/solution.py
+++ b/solution.py
@@ -61,7 +61,7 @@
 
 
 WEIGHT_AT = 4 * EACH
-SENT = WEIGHT_AT + 2 * COLUMNS
+SENT = WEIGHT_AT + COLUMNS
 
 
 def send_kernel(rows_ref, docs_ref, weight_ref, out_ref):
@@ -76,14 +76,12 @@
             tile[2 * EACH : 4 * EACH, :] = jnp.concatenate([values, docs], axis=0).astype(
                 jnp.bfloat16
             )
-            for k in range(2):
-                at = WEIGHT_AT + k * COLUMNS
-                tile[at : at + COLUMNS, :] = weight[k]
+            tile[WEIGHT_AT:SENT, :] = weight[j]
 
 
 DOCS_AT = 2 * ROWS
 COLUMNS_AT = DOCS_AT + 16
-GATHERED = COLUMNS_AT + 4 * COLUMNS
+GATHERED = COLUMNS_AT + 2 * COLUMNS
 
 
 def gather_kernel(place_ref, came_ref, query_ref, key_ref):
@@ -109,12 +107,14 @@
         key_ref[s, ROWS:DOCS_AT, :] = values
         key_ref[s, DOCS_AT:COLUMNS_AT, :] = docs
         for k in range(2):
-            at = COLUMNS_AT + k * 2 * COLUMNS
-            key_ref[s, at : at + 2 * COLUMNS, :] = came_ref[2 * s + k, WEIGHT_AT:SENT, :]
-
-
-def attend_kernel(place_ref, query_ref, key_ref, out_ref, score_ref):
-    z2, y, x, c = (place_ref[k] for k in range(1, 5))
+            at = COLUMNS_AT + k * COLUMNS
+            key_ref[s, at : at + COLUMNS, :] = came_ref[2 * s + k, WEIGHT_AT:SENT, :]
+
+
+def attend_kernel(place_ref, query_ref, key_ref, other_ref, out_ref, columns_ref, score_ref):
+    columns_ref[0] = key_ref[:, COLUMNS_AT:GATHERED, :]
+    columns_ref[1] = other_ref[...]
+    z2, y, x, c = (place_ref[k] for k in range(4))
     stripe = 2 * BLOCK * 4
 
     def positions(z2, y, x, c, dim):
@@ -158,7 +158,8 @@
         out_ref[r, ROWS : ROWS + 8, :] = jnp.concatenate([row_max.T[0:4], row_sum.T[0:4]], axis=0)
 
 
-def combine_kernel(part_ref, out_ref):
+def combine_kernel(part_ref, columns_ref, out_ref, same_ref):
+    same_ref[...] = columns_ref[...]
     parts = part_ref.shape[0]
     maxima = [part_ref[r, ROWS : ROWS + 1, :] for r in range(parts)]
     sums = [part_ref[r, ROWS + 4 : ROWS + 5, :] for r in range(parts)]
@@ -173,8 +174,9 @@
     out_ref[...] = mixed.astype(out_ref.dtype)
 
 
-def product_kernel(place_ref, attended_ref, w0, w1, w2, w3, residual_ref, out_ref):
-    z2, y = place_ref[1], place_ref[2]
+def product_kernel(place_ref, attended_ref, *refs):
+    weights, (residual_ref, out_ref) = refs[:8], refs[8:]
+    z2, y, zp = place_ref[0], place_ref[1], place_ref[4]
     total = jnp.zeros(out_ref.shape, jnp.float32)
     for p in range(attended_ref.shape[0]):
         heads = [
@@ -183,13 +185,10 @@
         ]
         left = jnp.concatenate(heads, axis=1).astype(jnp.bfloat16)
         blocks = []
-        for zl in range(4):
-            own = (zl & 1) ^ z2
-            for w in (w0, w1, w2, w3):
-                halves = []
-                for k in range(2):
-                    at = ((zl >> 1) * 2 + k) * COLUMNS
-                    halves.append(w[own, p, at : at + COLUMNS, :])
+        for k in range(2):
+            rows = slice(k * COLUMNS, (k + 1) * COLUMNS)
+            for w in weights:
+                halves = [w[zp ^ j, p, rows, :] for j in range(2)]
                 blocks.append(jnp.concatenate(halves, axis=1))
         total = total + lax.dot_general(
             left,
@@ -197,12 +196,17 @@
             (((1,), (1,)), ((), ())),
             preferred_element_type=jnp.float32,
         )
-    for zl in range(4):
-        columns = slice(zl * LANES, (zl + 1) * LANES)
-        summed = pltpu.roll(total[:, columns], y * COLUMNS, 1)
-        out_ref[:, columns] = (residual_ref[:, columns].astype(jnp.float32) + summed).astype(
-            out_ref.dtype
+    for k in range(2):
+        own, other = (
+            pltpu.roll(total[:, at : at + LANES], y * COLUMNS, 1)
+            for at in (2 * k * LANES, (2 * k + 1) * LANES)
         )
+        for j in range(2):
+            columns = slice((2 * k + j) * LANES, (2 * k + j + 1) * LANES)
+            summed = jnp.where(z2 == j, own, other)
+            out_ref[:, columns] = (residual_ref[:, columns].astype(jnp.float32) + summed).astype(
+                out_ref.dtype
+            )
 
 
 def shards(query, key_states, value_states, doc_ids, out_weight, residual):
@@ -210,7 +214,7 @@
     planes = lax.axis_size(PLANES)
     spread = lax.axis_size(QUERY_AXES)
     bf16, f32 = jnp.bfloat16, jnp.float32
-    index = [lax.axis_index(a) for a in (PLANES, "z2", "y", "x", "c")]
+    index = [lax.axis_index(a) for a in ("z2", "y", "x", "c", "zp")]
     place = jnp.stack(index)
 
     cut = [a.reshape(groups, EACH, -1) for a in (query, key_states, value_states)]
@@ -235,30 +239,39 @@
     queries = exchange(queries, QUERY_AXES)
 
     columns = keys[:, COLUMNS_AT:]
-    columns = jnp.stack([columns, moved(columns, lambda z, y, x, c: (z ^ 1, y, x, c))])
-    weights = [columns]
-    weights += [moved(columns, lambda z, y, x, c: (z, (y - k) % 4, x, c)) for k in (1, 2, 3)]
-
-    parts = call(
+    columns = moved(columns, lambda z, y, x, c: (z ^ 2, y, x, c))
+    held = jax.ShapeDtypeStruct((2, *columns.shape), bf16)
+
+    def every_y(block):
+        return [block] + [
+            moved(block, lambda z, y, x, c: (z, (y - k) % 4, x, c)) for k in (1, 2, 3)
+        ]
+
+    parts, columns = call(
         attend_kernel,
-        jax.ShapeDtypeStruct((spread, ROWS + 8, LANES), f32),
-        [SMEM, VMEM, VMEM],
+        [jax.ShapeDtypeStruct((spread, ROWS + 8, LANES), f32), held],
+        [SMEM] + [VMEM] * 3,
         "attend",
         [pltpu.VMEM((groups, ROWS, LANES), f32)],
         4 * spread * ROWS * groups * ROWS * HEAD_DIM,
         2 << 20,
-    )(place, queries, keys)
+    )(place, queries, keys, columns)
     parts = exchange(parts, QUERY_AXES)
-    attended = call(
-        combine_kernel, jax.ShapeDtypeStruct((ROWS, HEAD_DIM), bf16), [VMEM], "combine"
-    )(parts)
+    weights = every_y(columns)
+    attended, columns = call(
+        combine_kernel,
+        [jax.ShapeDtypeStruct((ROWS, HEAD_DIM), bf16), held],
+        [VMEM] * 2,
+        "combine",
+    )(parts, moved(columns, lambda z, y, x, c: (z ^ 1, y, x, c)))
+    weights += every_y(columns)
 
     back = exchange(attended.reshape(planes, EACH, HEAD_DIM), PLANES)
     everyone = exchange(jnp.broadcast_to(back[None], (groups, *back.shape)), HEAD_AXES)
     return call(
         product_kernel,
         jax.ShapeDtypeStruct(residual.shape, residual.dtype),
-        [SMEM] + [VMEM] * 6,
+        [SMEM] + [VMEM] * 10,
         "product",
         (),
         2 * BLOCK * 2048 * 512,

time: 197 us -> 179 us (0.909)
  blocking collectives: 66.6 us -> 20.4 us
  starting transfers between devices: 60 us -> 95.7 us
  waiting for transfers between devices: 56.7 us -> 48.6 us
    all_to_all x3 -> x1, blocking collectives: 66.6 us -> 20.4 us  [exchange(): return lax.all_to_all(tiles, axes, split_axis=0, concat_axis=0, tiled=True)]
    all_to_all x4 -> x6, starting transfers between devices: 46.2 us -> 66.4 us  [exchange(): return lax.all_to_all(tiles, axes, split_axis=0, concat_axis=0, tiled=True)]
    ppermute x4 -> x8, starting transfers between devices: 13.8 us -> 29.4 us  [moved(): lax.ppermute(block, names, [(flat(*p), flat(*where(*p))) for p in places])]
    all_to_all x4 -> x6, waiting for transfers between devices: 48.3 us -> 39.3 us  [exchange(): return lax.all_to_all(tiles, axes, split_axis=0, concat_axis=0, tiled=True)]
    ppermute x4 -> x8, waiting for transfers between devices: 8.44 us -> 9.33 us  [moved(): lax.ppermute(block, names, [(flat(*p), flat(*where(*p))) for p in places])]
  transfers between devices with their start and end apart: 8 -> 14, of which waited for: 4 -> 6; matrix products, arithmetic and copies ran while one was open for 1% -> 1% of each run, Pallas kernels for 0% -> 0%
where the time goes in v3:
time: 179 us; the launch traced here: 178 us
  starting transfers between devices  95.7 us (53%)
  waiting for transfers between devices  48.6 us (27%)
  blocking collectives  20.4 us (11%)
  Pallas kernels  10.3 us (6%)
    all_to_all x6, starting transfers between devices, exchange(): return lax.all_to_all(tiles, axes, split_axis=0, concat_axis=0, tiled=True)  66.4 us
    all_to_all x6, waiting for transfers between devices, exchange(): return lax.all_to_all(tiles, axes, split_axis=0, concat_axis=0, tiled=True)  39.3 us
    ppermute x8, starting transfers between devices, moved(): lax.ppermute(block, names, [(flat(*p), flat(*where(*p))) for p in places])  29.4 us
    all_to_all x1, blocking collectives, exchange(): return lax.all_to_all(tiles, axes, split_axis=0, concat_axis=0, tiled=True)  20.4 us
    ppermute x8, waiting for transfers between devices, moved(): lax.ppermute(block, names, [(flat(*p), flat(*where(*p))) for p in places])  9.33 us
    pallas_call x1, Pallas kernels, shards(): call(attend_kernel, [jax.ShapeDtypeStruct((spread, ROWS + 8, LANES), f32)...  5.29 us
  transfers between devices with their start and end apart: 14, of which 6 were waited for; matrix products, arithmetic and copies ran while one was open for 1% of the time, Pallas kernels for 0%

profile of v3, /device:TPU:1, one launch (start us, length us, event | category | flops | bytes accessed | tf_op | source)
XLA Modules:
  0.0 178.3 jit_solution(8349864573478737831)
XLA Ops:
  0.0 1.4 pad_maximum_fusion
  1.4 17.4 %all-to-all-start = ((bf16[8,24,256]{2,1,0:T(8,128)(2,1)}), bf16[8,24,256]{2,1,0:T(8,128)(2,1)S(1)}, u32[]{:S(2)}, u32[]{:S(2)}) async-start(bf16[8,24,256]{2,1,0:T(8,128)(2,1)} %pad_maximum_fusion), calls=%async_computation | async-start | bytes 196608 | tf_op jit(solution)/shard_map/all_to_all | solution.py:31
  18.8 0.0 copy-start.1
  18.9 0.0 copy-start.2
  18.9 0.7 copy-done.2
  19.5 0.1 pad_add_fusion
  19.6 0.1 convert_bitcast_fusion
  19.7 0.1 pad_maximum_fusion.1.docs_ref
  19.8 4.1 %all-to-all-done.rows_ref = bf16[8,24,256]{2,1,0:T(8,128)(2,1)S(1)} async-done(((bf16[8,24,256]{2,1,0:T(8,128)(2,1)}), bf16[8,24,256]{2,1,0:T(8,128)(2,1)S(1)}, u32[]{:S(2)}, u32[]{:S(2)}) %all-to-all-start) | async-done | bytes 98336 | tf_op jit(solution)/shard_map/all_to_all | solution.py:31
  23.9 0.0 copy-done.1
  23.9 0.7 send.1
  24.6 16.5 %all-to-all-start.1 = ((bf16[16,64,128]{2,1,0:T(8,128)(2,1)}), bf16[16,64,128]{2,1,0:T(8,128)(2,1)S(1)}, u32[]{:S(2)}, u32[]{:S(2)}) async-start(bf16[16,64,128]{2,1,0:T(8,128)(2,1)} %send.1), calls=%async_computation.1 | async-start | bytes 524288 | tf_op jit(solution)/shard_map/all_to_all | solution.py:31
  41.1 0.1 stack.23.place_ref
  41.2 24.0 %all-to-all-done.1.came_ref = bf16[16,64,128]{2,1,0:T(8,128)(2,1)S(1)} async-done(((bf16[16,64,128]{2,1,0:T(8,128)(2,1)}), bf16[16,64,128]{2,1,0:T(8,128)(2,1)S(1)}, u32[]{:S(2)}, u32[]{:S(2)}) %all-to-all-start.1) | async-done | bytes 262176 | tf_op jit(solution)/shard_map/all_to_all | solution.py:31
  65.3 1.4 spread.1
  66.6 20.4 %all_to_all.35.key_ref = bf16[8,336,128]{2,1,0:T(8,128)(2,1)S(1)} all-to-all(bf16[8,336,128]{2,1,0:T(8,128)(2,1)S(1)} %get-tuple-element.12), channel_id=1, replica_groups=mesh['zh'=8,'zp'=2,'z2'=2,'y'=4,'x'=4,'c'=2] {'x','c'}, dimensions={0} | all-to-all | bytes 1376256 | tf_op jit(solution)/shard_map/all_to_all | solution.py:31
  87.0 9.6 %all-to-all-start.2 = ((bf16[8,144,128]{2,1,0:T(8,128)(2,1)}), bf16[8,144,128]{2,1,0:T(8,128)(2,1)S(1)}, u32[]{:S(2)}, u32[]{:S(2)}) async-start(bf16[8,144,128]{2,1,0:T(8,128)(2,1)} %get-tuple-element.11), calls=%async_computation.2 | async-start | bytes 589824 | tf_op jit(solution)/shard_map/all_to_all | solution.py:31
  96.6 6.5 %collective-permute-start = (bf16[8,64,128]{2,1,0:T(8,128)(2,1)S(1)}, bf16[8,64,128]{2,1,0:T(8,128)(2,1)S(1)}, u32[]{:S(2)}, u32[]{:S(2)}) collective-permute-start(bf16[8,64,128]{2,1,0:T(8,128)(2,1)S(1)} %slice.4), channel_id=1, source_target_pairs={{0,64},{1,65},{2,66},{3,67},{4,68},{5,69},{6,70},{7,71},{8,72},{9,... | collective-permute-start | bytes 393224 | tf_op jit(solution)/shard_map/ppermute | solution.py:42
  103.1 3.0 %collective-permute-done.other_ref = bf16[8,64,128]{2,1,0:T(8,128)(2,1)S(1)} collective-permute-done((bf16[8,64,128]{2,1,0:T(8,128)(2,1)S(1)}, bf16[8,64,128]{2,1,0:T(8,128)(2,1)S(1)}, u32[]{:S(2)}, u32[]{:S(2)}) %collective-permute-start) | collective-permute-done | bytes 131104 | tf_op jit(solution)/shard_map/ppermute | solution.py:42
  106.1 0.0 all-to-all-done.2.query_ref
  106.1 5.3 %attend.1 = (f32[8,136,128]{2,1,0:T(8,128)}, bf16[2,8,64,128]{3,2,1,0:T(8,128)(2,1)S(1)}) custom-call(s32[5]{0:T(128)S(1)} %stack.23.place_ref, bf16[8,144,128]{2,1,0:T(8,128)(2,1)S(1)} %all-to-all-done.2.query_ref, bf16[8,336,128]{2,1,0:T(8,128)(2,1)S(1)} %all_to_all.35.key_ref, bf16[8,64,128]{2,1,0:T(8,128)(2,1)S(1)} %collective-permute-done.other_ref), custom_call_target="tpu_custom_call" | custom-call | flops 536870912 | bytes 2097152 | tf_op jit(solution)/shard_map/attend/pallas_call | solution.py:250
  111.4 7.6 %all-to-all-start.4 = ((f32[8,136,128]{2,1,0:T(8,128)}), f32[8,136,128]{2,1,0:T(8,128)S(1)}, u32[]{:S(2)}, u32[]{:S(2)}) async-start(f32[8,136,128]{2,1,0:T(8,128)} %get-tuple-element.13), calls=%async_computation.4 | async-start | bytes 1114112 | tf_op jit(solution)/shard_map/all_to_all | solution.py:31
  119.0 3.4 %collective-permute-start.1 = (bf16[2,8,64,128]{3,2,1,0:T(8,128)(2,1)S(1)}, bf16[2,8,64,128]{3,2,1,0:T(8,128)(2,1)S(1)}, u32[]{:S(2)}, u32[]{:S(2)}) collective-permute-start(bf16[2,8,64,128]{3,2,1,0:T(8,128)(2,1)S(1)} %get-tuple-element.14.refs_0_), channel_id=1, source_target_pairs={{0,32},{1,33},{2,34},{3,35},{4,36},{5,37},{6,38},{7,39},{8,40},{9,... | collective-permute-start | bytes 786440 | tf_op jit(solution)/shard_map/ppermute | solution.py:42
  122.4 3.1 %collective-permute-start.4 = (bf16[2,8,64,128]{3,2,1,0:T(8,128)(2,1)S(1)}, bf16[2,8,64,128]{3,2,1,0:T(8,128)(2,1)S(1)}, u32[]{:S(2)}, u32[]{:S(2)}) collective-permute-start(bf16[2,8,64,128]{3,2,1,0:T(8,128)(2,1)S(1)} %get-tuple-element.14.refs_0_), channel_id=1, source_target_pairs={{0,8},{1,9},{2,10},{3,11},{4,12},{5,13},{6,14},{7,15},{8,16},{9,17... | collective-permute-start | bytes 786440 | tf_op jit(solution)/shard_map/ppermute | solution.py:42
  125.5 6.3 %collective-permute-done.1.columns_ref = bf16[2,8,64,128]{3,2,1,0:T(8,128)(2,1)S(1)} collective-permute-done((bf16[2,8,64,128]{3,2,1,0:T(8,128)(2,1)S(1)}, bf16[2,8,64,128]{3,2,1,0:T(8,128)(2,1)S(1)}, u32[]{:S(2)}, u32[]{:S(2)}) %collective-permute-start.1) | collective-permute-done | bytes 262176 | tf_op jit(solution)/shard_map/ppermute | solution.py:42
  131.8 0.0 all-to-all-done.4.part_ref
  131.8 0.9 combine.1
  132.7 8.2 %all-to-all-start.5 = ((bf16[16,8,128]{2,1,0:T(8,128)(2,1)}), bf16[16,8,128]{2,1,0:T(8,128)(2,1)S(1)}, u32[]{:S(2)}, u32[]{:S(2)}) async-start(bf16[16,8,128]{2,1,0:T(8,128)(2,1)} %bitcast.10), calls=%async_computation.5 | async-start | bytes 65536 | tf_op jit(solution)/shard_map/all_to_all | solution.py:31
  140.9 4.5 %collective-permute-start.3 = (bf16[2,8,64,128]{3,2,1,0:T(8,128)(2,1)S(1)}, bf16[2,8,64,128]{3,2,1,0:T(8,128)(2,1)S(1)}, u32[]{:S(2)}, u32[]{:S(2)}) collective-permute-start(bf16[2,8,64,128]{3,2,1,0:T(8,128)(2,1)S(1)} %get-tuple-element.14.refs_0_), channel_id=1, source_target_pairs={{0,16},{1,17},{2,18},{3,19},{4,20},{5,21},{6,22},{7,23},{8,24},{9,... | collective-permute-start | bytes 786440 | tf_op jit(solution)/shard_map/ppermute | solution.py:42
  145.4 2.9 %collective-permute-start.2 = (bf16[2,8,64,128]{3,2,1,0:T(8,128)(2,1)S(1)}, bf16[2,8,64,128]{3,2,1,0:T(8,128)(2,1)S(1)}, u32[]{:S(2)}, u32[]{:S(2)}) collective-permute-start(bf16[2,8,64,128]{3,2,1,0:T(8,128)(2,1)S(1)} %get-tuple-element.14.refs_0_), channel_id=1, source_target_pairs={{0,24},{1,25},{2,26},{3,27},{4,28},{5,29},{6,30},{7,31},{8,0},{9,1... | collective-permute-start | bytes 786440 | tf_op jit(solution)/shard_map/ppermute | solution.py:42
  148.3 2.4 %collective-permute-start.7 = (bf16[2,8,64,128]{3,2,1,0:T(8,128)(2,1)S(1)}, bf16[2,8,64,128]{3,2,1,0:T(8,128)(2,1)S(1)}, u32[]{:S(2)}, u32[]{:S(2)}) collective-permute-start(bf16[2,8,64,128]{3,2,1,0:T(8,128)(2,1)S(1)} %get-tuple-element.16.refs_4_), channel_id=1, source_target_pairs={{0,8},{1,9},{2,10},{3,11},{4,12},{5,13},{6,14},{7,15},{8,16},{9,17... | collective-permute-start | bytes 786440 | tf_op jit(solution)/shard_map/ppermute | solution.py:42
  150.7 2.6 %collective-permute-start.6 = (bf16[2,8,64,128]{3,2,1,0:T(8,128)(2,1)S(1)}, bf16[2,8,64,128]{3,2,1,0:T(8,128)(2,1)S(1)}, u32[]{:S(2)}, u32[]{:S(2)}) collective-permute-start(bf16[2,8,64,128]{3,2,1,0:T(8,128)(2,1)S(1)} %get-tuple-element.16.refs_4_), channel_id=1, source_target_pairs={{0,16},{1,17},{2,18},{3,19},{4,20},{5,21},{6,22},{7,23},{8,24},{9,... | collective-permute-start | bytes 786440 | tf_op jit(solution)/shard_map/ppermute | solution.py:42
  153.3 0.0 collective-permute-done.4.refs_3_
  153.3 4.0 %collective-permute-start.5 = (bf16[2,8,64,128]{3,2,1,0:T(8,128)(2,1)S(1)}, bf16[2,8,64,128]{3,2,1,0:T(8,128)(2,1)S(1)}, u32[]{:S(2)}, u32[]{:S(2)}) collective-permute-start(bf16[2,8,64,128]{3,2,1,0:T(8,128)(2,1)S(1)} %get-tuple-element.16.refs_4_), channel_id=1, source_target_pairs={{0,24},{1,25},{2,26},{3,27},{4,28},{5,29},{6,30},{7,31},{8,0},{9,1... | collective-permute-start | bytes 786440 | tf_op jit(solution)/shard_map/ppermute | solution.py:42
  157.3 4.7 %all-to-all-done.5 = bf16[16,8,128]{2,1,0:T(8,128)(2,1)S(1)} async-done(((bf16[16,8,128]{2,1,0:T(8,128)(2,1)}), bf16[16,8,128]{2,1,0:T(8,128)(2,1)S(1)}, u32[]{:S(2)}, u32[]{:S(2)}) %all-to-all-start.5) | async-done | bytes 32800 | tf_op jit(solution)/shard_map/all_to_all | solution.py:31
  162.0 0.7 broadcast_in_dim.2
  162.7 0.0 copy-start
  162.7 7.0 %all-to-all-start.6 = ((bf16[8,16,8,128]{3,2,1,0:T(8,128)(2,1)}), bf16[8,16,8,128]{3,2,1,0:T(8,128)(2,1)S(1)}, u32[]{:S(2)}, u32[]{:S(2)}) async-start(bf16[8,16,8,128]{3,2,1,0:T(8,128)(2,1)} %broadcast_in_dim.2), calls=%async_computation.6 | async-start | bytes 524288 | tf_op jit(solution)/shard_map/all_to_all | solution.py:31
  169.7 0.0 collective-permute-done.3.refs_2_
  169.7 0.0 collective-permute-done.2.refs_1_
  169.8 0.0 collective-permute-done.7.refs_7_
  169.8 0.0 collective-permute-done.6.refs_6_
  169.8 0.0 collective-permute-done.5.refs_5_
  169.8 6.5 %all-to-all-done.6.attended_ref = bf16[8,16,8,128]{3,2,1,0:T(8,128)(2,1)S(1)} async-done(((bf16[8,16,8,128]{3,2,1,0:T(8,128)(2,1)}), bf16[8,16,8,128]{3,2,1,0:T(8,128)(2,1)S(1)}, u32[]{:S(2)}, u32[]{:S(2)}) %all-to-all-start.6) | async-done | bytes 262176 | tf_op jit(solution)/shard_map/all_to_all | solution.py:31
  176.3 0.0 copy-done
  176.3 2.0 %product.1 = bf16[64,512]{1,0:T(8,128)(2,1)} custom-call(s32[5]{0:T(128)S(1)} %stack.23.place_ref, bf16[8,16,8,128]{3,2,1,0:T(8,128)(2,1)S(1)} %all-to-all-done.6.attended_ref, bf16[2,8,64,128]{3,2,1,0:T(8,128)(2,1)S(1)} %get-tuple-element.14.refs_0_, bf16[2,8,64,128]{3,2,1,0:T(8,128)(2,1)S(1)} %collective-permute-done.2.refs_1_, ...), custom_call_target="tpu_custom_call" | custom-call | flops 134217728 | bytes 3145728 | tf_op jit(solution)/shard_map/product/pallas_call | solution.py:271
  (1 shorter events, 0.0 us)
Async XLA Ops:
  1.4 22.4 %all-to-all-start = ((bf16[8,24,256]{2,1,0:T(8,128)(2,1)}), bf16[8,24,256]{2,1,0:T(8,128)(2,1)S(1)}, u32[]{:S(2)}, u32[]{:S(2)}) async-start(bf16[8,24,256]{2,1,0:T(8,128)(2,1)} %pad_maximum_fusion), calls=%async_computation | async-start | bytes 196608 | tf_op jit(solution)/shard_map/all_to_all | solution.py:31
  18.8 5.0 %copy-start.1 = (bf16[256,32]{0,1:T(8,128)(2,1)S(1)}, bf16[256,32]{0,1:T(8,128)(2,1)}, u32[]{:S(2)}) copy-start(bf16[256,32]{0,1:T(8,128)(2,1)} %param.10) | copy-start | bytes 49156
  18.9 0.7 copy-start.2
  24.6 40.7 %all-to-all-start.1 = ((bf16[16,64,128]{2,1,0:T(8,128)(2,1)}), bf16[16,64,128]{2,1,0:T(8,128)(2,1)S(1)}, u32[]{:S(2)}, u32[]{:S(2)}) async-start(bf16[16,64,128]{2,1,0:T(8,128)(2,1)} %send.1), calls=%async_computation.1 | async-start | bytes 524288 | tf_op jit(solution)/shard_map/all_to_all | solution.py:31
  87.0 19.1 %all-to-all-start.2 = ((bf16[8,144,128]{2,1,0:T(8,128)(2,1)}), bf16[8,144,128]{2,1,0:T(8,128)(2,1)S(1)}, u32[]{:S(2)}, u32[]{:S(2)}) async-start(bf16[8,144,128]{2,1,0:T(8,128)(2,1)} %get-tuple-element.11), calls=%async_computation.2 | async-start | bytes 589824 | tf_op jit(solution)/shard_map/all_to_all | solution.py:31
  96.6 9.5 %collective-permute-start = (bf16[8,64,128]{2,1,0:T(8,128)(2,1)S(1)}, bf16[8,64,128]{2,1,0:T(8,128)(2,1)S(1)}, u32[]{:S(2)}, u32[]{:S(2)}) collective-permute-start(bf16[8,64,128]{2,1,0:T(8,128)(2,1)S(1)} %slice.4), channel_id=1, source_target_pairs={{0,64},{1,65},{2,66},{3,67},{4,68},{5,69},{6,70},{7,71},{8,72},{9,... | collective-permute-start | bytes 393224 | tf_op jit(solution)/shard_map/ppermute | solution.py:42
  111.4 20.4 %all-to-all-start.4 = ((f32[8,136,128]{2,1,0:T(8,128)}), f32[8,136,128]{2,1,0:T(8,128)S(1)}, u32[]{:S(2)}, u32[]{:S(2)}) async-start(f32[8,136,128]{2,1,0:T(8,128)} %get-tuple-element.13), calls=%async_computation.4 | async-start | bytes 1114112 | tf_op jit(solution)/shard_map/all_to_all | solution.py:31
  119.0 12.8 %collective-permute-start.1 = (bf16[2,8,64,128]{3,2,1,0:T(8,128)(2,1)S(1)}, bf16[2,8,64,128]{3,2,1,0:T(8,128)(2,1)S(1)}, u32[]{:S(2)}, u32[]{:S(2)}) collective-permute-start(bf16[2,8,64,128]{3,2,1,0:T(8,128)(2,1)S(1)} %get-tuple-element.14.refs_0_), channel_id=1, source_target_pairs={{0,32},{1,33},{2,34},{3,35},{4,36},{5,37},{6,38},{7,39},{8,40},{9,... | collective-permute-start | bytes 786440 | tf_op jit(solution)/shard_map/ppermute | solution.py:42
  122.4 30.9 %collective-permute-start.4 = (bf16[2,8,64,128]{3,2,1,0:T(8,128)(2,1)S(1)}, bf16[2,8,64,128]{3,2,1,0:T(8,128)(2,1)S(1)}, u32[]{:S(2)}, u32[]{:S(2)}) collective-permute-start(bf16[2,8,64,128]{3,2,1,0:T(8,128)(2,1)S(1)} %get-tuple-element.14.refs_0_), channel_id=1, source_target_pairs={{0,8},{1,9},{2,10},{3,11},{4,12},{5,13},{6,14},{7,15},{8,16},{9,17... | collective-permute-start | bytes 786440 | tf_op jit(solution)/shard_map/ppermute | solution.py:42
  132.7 29.3 %all-to-all-start.5 = ((bf16[16,8,128]{2,1,0:T(8,128)(2,1)}), bf16[16,8,128]{2,1,0:T(8,128)(2,1)S(1)}, u32[]{:S(2)}, u32[]{:S(2)}) async-start(bf16[16,8,128]{2,1,0:T(8,128)(2,1)} %bitcast.10), calls=%async_computation.5 | async-start | bytes 65536 | tf_op jit(solution)/shard_map/all_to_all | solution.py:31
  140.9 28.9 %collective-permute-start.3 = (bf16[2,8,64,128]{3,2,1,0:T(8,128)(2,1)S(1)}, bf16[2,8,64,128]{3,2,1,0:T(8,128)(2,1)S(1)}, u32[]{:S(2)}, u32[]{:S(2)}) collective-permute-start(bf16[2,8,64,128]{3,2,1,0:T(8,128)(2,1)S(1)} %get-tuple-element.14.refs_0_), channel_id=1, source_target_pairs={{0,16},{1,17},{2,18},{3,19},{4,20},{5,21},{6,22},{7,23},{8,24},{9,... | collective-permute-start | bytes 786440 | tf_op jit(solution)/shard_map/ppermute | solution.py:42
  145.4 24.4 %collective-permute-start.2 = (bf16[2,8,64,128]{3,2,1,0:T(8,128)(2,1)S(1)}, bf16[2,8,64,128]{3,2,1,0:T(8,128)(2,1)S(1)}, u32[]{:S(2)}, u32[]{:S(2)}) collective-permute-start(bf16[2,8,64,128]{3,2,1,0:T(8,128)(2,1)S(1)} %get-tuple-element.14.refs_0_), channel_id=1, source_target_pairs={{0,24},{1,25},{2,26},{3,27},{4,28},{5,29},{6,30},{7,31},{8,0},{9,1... | collective-permute-start | bytes 786440 | tf_op jit(solution)/shard_map/ppermute | solution.py:42
  148.3 21.5 %collective-permute-start.7 = (bf16[2,8,64,128]{3,2,1,0:T(8,128)(2,1)S(1)}, bf16[2,8,64,128]{3,2,1,0:T(8,128)(2,1)S(1)}, u32[]{:S(2)}, u32[]{:S(2)}) collective-permute-start(bf16[2,8,64,128]{3,2,1,0:T(8,128)(2,1)S(1)} %get-tuple-element.16.refs_4_), channel_id=1, source_target_pairs={{0,8},{1,9},{2,10},{3,11},{4,12},{5,13},{6,14},{7,15},{8,16},{9,17... | collective-permute-start | bytes 786440 | tf_op jit(solution)/shard_map/ppermute | solution.py:42
  150.7 19.1 %collective-permute-start.6 = (bf16[2,8,64,128]{3,2,1,0:T(8,128)(2,1)S(1)}, bf16[2,8,64,128]{3,2,1,0:T(8,128)(2,1)S(1)}, u32[]{:S(2)}, u32[]{:S(2)}) collective-permute-start(bf16[2,8,64,128]{3,2,1,0:T(8,128)(2,1)S(1)} %get-tuple-element.16.refs_4_), channel_id=1, source_target_pairs={{0,16},{1,17},{2,18},{3,19},{4,20},{5,21},{6,22},{7,23},{8,24},{9,... | collective-permute-start | bytes 786440 | tf_op jit(solution)/shard_map/ppermute | solution.py:42
  153.3 16.4 %collective-permute-start.5 = (bf16[2,8,64,128]{3,2,1,0:T(8,128)(2,1)S(1)}, bf16[2,8,64,128]{3,2,1,0:T(8,128)(2,1)S(1)}, u32[]{:S(2)}, u32[]{:S(2)}) collective-permute-start(bf16[2,8,64,128]{3,2,1,0:T(8,128)(2,1)S(1)} %get-tuple-element.16.refs_4_), channel_id=1, source_target_pairs={{0,24},{1,25},{2,26},{3,27},{4,28},{5,29},{6,30},{7,31},{8,0},{9,1... | collective-permute-start | bytes 786440 | tf_op jit(solution)/shard_map/ppermute | solution.py:42
  162.7 13.6 %copy-start = (bf16[64,512]{1,0:T(8,128)(2,1)S(1)}, bf16[64,512]{1,0:T(8,128)(2,1)}, u32[]{:S(2)}) copy-start(bf16[64,512]{1,0:T(8,128)(2,1)} %refs_8_.1) | copy-start | bytes 196612
  162.7 13.6 %all-to-all-start.6 = ((bf16[8,16,8,128]{3,2,1,0:T(8,128)(2,1)}), bf16[8,16,8,128]{3,2,1,0:T(8,128)(2,1)S(1)}, u32[]{:S(2)}, u32[]{:S(2)}) async-start(bf16[8,16,8,128]{3,2,1,0:T(8,128)(2,1)} %broadcast_in_dim.2), calls=%async_computation.6 | async-start | bytes 524288 | tf_op jit(solution)/shard_map/all_to_all | solution.py:31

commit v4 on v3

--- a/solution.py
+++ b/solution.py
@@ -21,7 +21,7 @@
 SEQ_AXES = ("zh", "zp", "z2", "y")
 HEAD_AXES = ("x", "c")
 PLANES = ("zh", "zp")
-QUERY_AXES = ("z2", "y")
+KEY_AXES = ("z2", "y")
 
 VMEM = pl.BlockSpec(memory_space=pltpu.VMEM)
 SMEM = pl.BlockSpec(memory_space=pltpu.SMEM)
@@ -79,12 +79,12 @@
             tile[WEIGHT_AT:SENT, :] = weight[j]
 
 
+COLUMNS_AT = ROWS + 16
+GATHERED = COLUMNS_AT + 2 * COLUMNS
 DOCS_AT = 2 * ROWS
-COLUMNS_AT = DOCS_AT + 16
-GATHERED = COLUMNS_AT + 2 * COLUMNS
-
-
-def gather_kernel(place_ref, came_ref, query_ref, key_ref):
+
+
+def gather_kernel(came_ref, query_ref, key_ref):
     planes = came_ref.shape[0]
     first = [came_ref[i, 0 : 2 * EACH, :].astype(jnp.float32) for i in range(planes)]
     second = [came_ref[i, 2 * EACH : 4 * EACH, :].astype(jnp.float32) for i in range(planes)]
@@ -96,24 +96,26 @@
     lane = lax.broadcasted_iota(jnp.int32, (EACH, LANES), 1)
     docs = jnp.zeros((EACH, LANES), jnp.float32)
     for i, tile in enumerate(second):
-        own = pltpu.roll(tile[EACH:], EACH * i, 1)
-        docs = jnp.where(lane // EACH == i, own, docs)
+        docs = jnp.where(lane // EACH == i, pltpu.roll(tile[EACH:], EACH * i, 1), docs)
     docs = jnp.concatenate([docs, docs], axis=0).astype(jnp.bfloat16)
     for s in range(query_ref.shape[0]):
         query_ref[s, 0:ROWS, :] = queries
-        query_ref[s, ROWS : ROWS + 16, :] = docs
+        query_ref[s, ROWS:COLUMNS_AT, :] = docs
+        for k in range(2):
+            at = COLUMNS_AT + k * COLUMNS
+            query_ref[s, at : at + COLUMNS, :] = came_ref[2 * s + k, WEIGHT_AT:SENT, :]
     for s in range(key_ref.shape[0]):
         key_ref[s, 0:ROWS, :] = keys
         key_ref[s, ROWS:DOCS_AT, :] = values
-        key_ref[s, DOCS_AT:COLUMNS_AT, :] = docs
-        for k in range(2):
-            at = COLUMNS_AT + k * COLUMNS
-            key_ref[s, at : at + COLUMNS, :] = came_ref[2 * s + k, WEIGHT_AT:SENT, :]
-
-
-def attend_kernel(place_ref, query_ref, key_ref, other_ref, out_ref, columns_ref, score_ref):
-    columns_ref[0] = key_ref[:, COLUMNS_AT:GATHERED, :]
-    columns_ref[1] = other_ref[...]
+        key_ref[s, DOCS_AT : DOCS_AT + 16, :] = docs
+
+
+def attend_kernel(place_ref, query_ref, key_ref, *refs):
+    by_z1, by_z2, by_z3, out_ref, own_ref, other_ref, score_ref = refs
+    own_ref[0] = query_ref[:, COLUMNS_AT:GATHERED, :]
+    own_ref[1] = by_z2[...]
+    other_ref[0] = by_z1[...]
+    other_ref[1] = by_z3[...]
     z2, y, x, c = (place_ref[k] for k in range(4))
     stripe = 2 * BLOCK * 4
 
@@ -125,8 +127,8 @@
     sources = key_ref.shape[0]
     for r in range(query_ref.shape[0]):
         queries = query_ref[r, 0:ROWS, :]
-        query_docs = transposed(query_ref[r, ROWS : ROWS + 16, :].astype(jnp.float32)[0:1])
-        query_pos = positions(r // 4, r % 4, x, c, 0)
+        query_docs = transposed(query_ref[r, ROWS:COLUMNS_AT, :].astype(jnp.float32)[0:1])
+        query_pos = positions(z2, y, r // 2, r % 2, 0)
         highest = jnp.full((ROWS, LANES), HIDDEN, jnp.float32)
         for s in range(sources):
             scores = lax.dot_general(
@@ -135,8 +137,8 @@
                 (((1,), (1,)), ((), ())),
                 preferred_element_type=jnp.float32,
             )
-            key_docs = key_ref[s, DOCS_AT:COLUMNS_AT, :].astype(jnp.float32)[0:1]
-            key_pos = positions(z2, y, s // 2, s % 2, 1)
+            key_docs = key_ref[s, DOCS_AT : DOCS_AT + 16, :].astype(jnp.float32)[0:1]
+            key_pos = positions(s // 4, s % 4, x, c, 1)
             visible = (key_pos <= query_pos) & (key_docs == query_docs)
             scores = jnp.where(visible, scores, HIDDEN)
             score_ref[s] = scores
@@ -158,8 +160,9 @@
         out_ref[r, ROWS : ROWS + 8, :] = jnp.concatenate([row_max.T[0:4], row_sum.T[0:4]], axis=0)
 
 
-def combine_kernel(part_ref, columns_ref, out_ref, same_ref):
-    same_ref[...] = columns_ref[...]
+def combine_kernel(part_ref, own_ref, other_ref, out_ref, same_own_ref, same_other_ref):
+    same_own_ref[...] = own_ref[...]
+    same_other_ref[...] = other_ref[...]
     parts = part_ref.shape[0]
     maxima = [part_ref[r, ROWS : ROWS + 1, :] for r in range(parts)]
     sums = [part_ref[r, ROWS + 4 : ROWS + 5, :] for r in range(parts)]
@@ -212,7 +215,7 @@
 def shards(query, key_states, value_states, doc_ids, out_weight, residual):
     groups = lax.axis_size(HEAD_AXES)
     planes = lax.axis_size(PLANES)
-    spread = lax.axis_size(QUERY_AXES)
+    spread = lax.axis_size(KEY_AXES)
     bf16, f32 = jnp.bfloat16, jnp.float32
     index = [lax.axis_index(a) for a in ("z2", "y", "x", "c", "zp")]
     place = jnp.stack(index)
@@ -229,42 +232,41 @@
     queries, keys = call(
         gather_kernel,
         [
-            jax.ShapeDtypeStruct((spread, ROWS + 16, LANES), bf16),
             jax.ShapeDtypeStruct((groups, GATHERED, LANES), bf16),
+            jax.ShapeDtypeStruct((spread, DOCS_AT + 16, LANES), bf16),
         ],
-        [SMEM, VMEM],
+        [VMEM],
         "spread",
-    )(place, came)
-    keys = exchange(keys, HEAD_AXES)
-    queries = exchange(queries, QUERY_AXES)
-
-    columns = keys[:, COLUMNS_AT:]
-    columns = moved(columns, lambda z, y, x, c: (z ^ 2, y, x, c))
+    )(came)
+    queries = exchange(queries, HEAD_AXES)
+    keys = exchange(keys, KEY_AXES)
+
+    columns = queries[:, COLUMNS_AT:]
+    near = [moved(columns, lambda z, y, x, c: (z ^ far, y, x, c)) for far in (1, 2, 3)]
     held = jax.ShapeDtypeStruct((2, *columns.shape), bf16)
 
-    def every_y(block):
-        return [block] + [
-            moved(block, lambda z, y, x, c: (z, (y - k) % 4, x, c)) for k in (1, 2, 3)
-        ]
-
-    parts, columns = call(
+    def from_y(block, k):
+        return moved(block, lambda z, y, x, c: (z, (y - k) % 4, x, c))
+
+    parts, own, other = call(
         attend_kernel,
-        [jax.ShapeDtypeStruct((spread, ROWS + 8, LANES), f32), held],
-        [SMEM] + [VMEM] * 3,
+        [jax.ShapeDtypeStruct((groups, ROWS + 8, LANES), f32), held, held],
+        [SMEM] + [VMEM] * 5,
         "attend",
-        [pltpu.VMEM((groups, ROWS, LANES), f32)],
+        [pltpu.VMEM((spread, ROWS, LANES), f32)],
         4 * spread * ROWS * groups * ROWS * HEAD_DIM,
         2 << 20,
-    )(place, queries, keys, columns)
-    parts = exchange(parts, QUERY_AXES)
-    weights = every_y(columns)
-    attended, columns = call(
+    )(place, queries, keys, *near)
+    parts = exchange(parts, HEAD_AXES)
+    next_own, last_own = from_y(own, 1), from_y(own, 3)
+    attended, own, other = call(
         combine_kernel,
-        [jax.ShapeDtypeStruct((ROWS, HEAD_DIM), bf16), held],
-        [VMEM] * 2,
+        [jax.ShapeDtypeStruct((ROWS, HEAD_DIM), bf16), held, held],
+        [VMEM] * 3,
         "combine",
-    )(parts, moved(columns, lambda z, y, x, c: (z ^ 1, y, x, c)))
-    weights += every_y(columns)
+    )(parts, own, other)
+    weights = [own, next_own, from_y(own, 2), last_own]
+    weights += [other] + [from_y(other, k) for k in (1, 2, 3)]
 
     back = exchange(attended.reshape(planes, EACH, HEAD_DIM), PLANES)
     everyone = exchange(jnp.broadcast_to(back[None], (groups, *back.shape)), HEAD_AXES)

time: 179 us -> 179 us (level)
  blocking collectives: 20.4 us -> 58 us
  starting transfers between devices: 95.7 us -> 77.2 us
  waiting for transfers between devices: 48.6 us -> 30.1 us
    all_to_all x1 -> x2, blocking collectives: 20.4 us -> 58 us  [exchange(): return lax.all_to_all(tiles, axes, split_axis=0, concat_axis=0, tiled=True)]
    all_to_all x6 -> x5, starting transfers between devices: 66.4 us -> 46.1 us  [exchange(): return lax.all_to_all(tiles, axes, split_axis=0, concat_axis=0, tiled=True)]
    all_to_all x6 -> x5, waiting for transfers between devices: 39.3 us -> 20.7 us  [exchange(): return lax.all_to_all(tiles, axes, split_axis=0, concat_axis=0, tiled=True)]
    ppermute x8 -> x9, starting transfers between devices: 29.4 us -> 31.1 us  [moved(): lax.ppermute(block, names, [(flat(*p), flat(*where(*p))) for p in places])]
    ppermute x8 -> x9, waiting for transfers between devices: 9.33 us -> 9.41 us  [moved(): lax.ppermute(block, names, [(flat(*p), flat(*where(*p))) for p in places])]
  transfers between devices with their start and end apart: 14 -> 14, of which waited for: 6 -> 7; matrix products, arithmetic and copies ran while one was open for 1% -> 1% of each run, Pallas kernels for 0% -> 0%
where the time goes in v4:
time: 179 us; the launch traced here: 178 us
  starting transfers between devices  77.2 us (43%)
  blocking collectives  58 us (32%)
  waiting for transfers between devices  30.1 us (17%)
  Pallas kernels  9.11 us (5%)
    all_to_all x2, blocking collectives, exchange(): return lax.all_to_all(tiles, axes, split_axis=0, concat_axis=0, tiled=True)  58 us
    all_to_all x5, starting transfers between devices, exchange(): return lax.all_to_all(tiles, axes, split_axis=0, concat_axis=0, tiled=True)  46.1 us
    ppermute x9, starting transfers between devices, moved(): lax.ppermute(block, names, [(flat(*p), flat(*where(*p))) for p in places])  31.1 us
    all_to_all x5, waiting for transfers between devices, exchange(): return lax.all_to_all(tiles, axes, split_axis=0, concat_axis=0, tiled=True)  20.7 us
    ppermute x9, waiting for transfers between devices, moved(): lax.ppermute(block, names, [(flat(*p), flat(*where(*p))) for p in places])  9.41 us
    pallas_call x1, Pallas kernels, shards(): call(attend_kernel, [jax.ShapeDtypeStruct((groups, ROWS + 8, LANES), f32)...  5.29 us
  transfers between devices with their start and end apart: 14, of which 7 were waited for; matrix products, arithmetic and copies ran while one was open for 1% of the time, Pallas kernels for 0%

profile of v4, /device:TPU:1, one launch (start us, length us, event | category | flops | bytes accessed | tf_op | source)
XLA Modules:
  0.0 177.7 jit_solution(8996607101216411350)
XLA Ops:
  0.0 1.4 pad_maximum_fusion
  1.4 17.4 %all-to-all-start = ((bf16[8,24,256]{2,1,0:T(8,128)(2,1)}), bf16[8,24,256]{2,1,0:T(8,128)(2,1)S(1)}, u32[]{:S(2)}, u32[]{:S(2)}) async-start(bf16[8,24,256]{2,1,0:T(8,128)(2,1)} %pad_maximum_fusion), calls=%async_computation | async-start | bytes 196608 | tf_op jit(solution)/shard_map/all_to_all | solution.py:31
  18.9 0.0 copy-start.2
  18.9 0.0 copy-start.1
  18.9 0.7 copy-done.2
  19.5 0.1 pad_add_fusion
  19.6 0.1 convert_bitcast_fusion
  19.7 0.1 pad_maximum_fusion.1.docs_ref
  19.7 4.1 %all-to-all-done.rows_ref = bf16[8,24,256]{2,1,0:T(8,128)(2,1)S(1)} async-done(((bf16[8,24,256]{2,1,0:T(8,128)(2,1)}), bf16[8,24,256]{2,1,0:T(8,128)(2,1)S(1)}, u32[]{:S(2)}, u32[]{:S(2)}) %all-to-all-start) | async-done | bytes 98336 | tf_op jit(solution)/shard_map/all_to_all | solution.py:31
  23.9 0.0 copy-done.1
  23.9 40.5 %all_to_all.35.came_ref = bf16[16,64,128]{2,1,0:T(8,128)(2,1)S(1)} all-to-all(bf16[16,64,128]{2,1,0:T(8,128)(2,1)S(1)} %send.1), channel_id=1, replica_groups=mesh['zh'=8,'zp'=2,'z2'=2,'y'=4,'x'=4,'c'=2] {'zh','zp'}, dimensions={0} | all-to-all | bytes 524288 | tf_op jit(solution)/shard_map/all_to_all | solution.py:31
  64.4 0.9 spread.1
  65.3 17.5 %all_to_all.36.query_ref = bf16[8,208,128]{2,1,0:T(8,128)(2,1)S(1)} all-to-all(bf16[8,208,128]{2,1,0:T(8,128)(2,1)S(1)} %get-tuple-element.13), channel_id=1, replica_groups=mesh['zh'=8,'zp'=2,'z2'=2,'y'=4,'x'=4,'c'=2] {'x','c'}, dimensions={0} | all-to-all | bytes 851968 | tf_op jit(solution)/shard_map/all_to_all | solution.py:31
  82.8 9.6 %all-to-all-start.3 = ((bf16[8,272,128]{2,1,0:T(8,128)(2,1)}), bf16[8,272,128]{2,1,0:T(8,128)(2,1)S(1)}, u32[]{:S(2)}, u32[]{:S(2)}) async-start(bf16[8,272,128]{2,1,0:T(8,128)(2,1)} %get-tuple-element.14), calls=%async_computation.3 | async-start | bytes 1114112 | tf_op jit(solution)/shard_map/all_to_all | solution.py:31
  92.4 3.4 %collective-permute-start = (bf16[8,64,128]{2,1,0:T(8,128)(2,1)S(1)}, bf16[8,64,128]{2,1,0:T(8,128)(2,1)S(1)}, u32[]{:S(2)}, u32[]{:S(2)}) collective-permute-start(bf16[8,64,128]{2,1,0:T(8,128)(2,1)S(1)} %slice.4), channel_id=1, source_target_pairs={{0,32},{1,33},{2,34},{3,35},{4,36},{5,37},{6,38},{7,39},{8,40},{9,... | collective-permute-start | bytes 393224 | tf_op jit(solution)/shard_map/ppermute | solution.py:42
  95.8 6.5 %collective-permute-start.1 = (bf16[8,64,128]{2,1,0:T(8,128)(2,1)S(1)}, bf16[8,64,128]{2,1,0:T(8,128)(2,1)S(1)}, u32[]{:S(2)}, u32[]{:S(2)}) collective-permute-start(bf16[8,64,128]{2,1,0:T(8,128)(2,1)S(1)} %slice.4), channel_id=1, source_target_pairs={{0,64},{1,65},{2,66},{3,67},{4,68},{5,69},{6,70},{7,71},{8,72},{9,... | collective-permute-start | bytes 393224 | tf_op jit(solution)/shard_map/ppermute | solution.py:42
  102.3 1.9 %collective-permute-start.2 = (bf16[8,64,128]{2,1,0:T(8,128)(2,1)S(1)}, bf16[8,64,128]{2,1,0:T(8,128)(2,1)S(1)}, u32[]{:S(2)}, u32[]{:S(2)}) collective-permute-start(bf16[8,64,128]{2,1,0:T(8,128)(2,1)S(1)} %slice.4), channel_id=1, source_target_pairs={{0,96},{1,97},{2,98},{3,99},{4,100},{5,101},{6,102},{7,103},{8,104... | collective-permute-start | bytes 393224 | tf_op jit(solution)/shard_map/ppermute | solution.py:42
  104.2 0.1 stack.23.place_ref
  104.3 0.0 collective-permute-done.refs_0_
  104.3 0.4 collective-permute-done.1.refs_1_
  104.7 7.4 %collective-permute-done.2.refs_2_ = bf16[8,64,128]{2,1,0:T(8,128)(2,1)S(1)} collective-permute-done((bf16[8,64,128]{2,1,0:T(8,128)(2,1)S(1)}, bf16[8,64,128]{2,1,0:T(8,128)(2,1)S(1)}, u32[]{:S(2)}, u32[]{:S(2)}) %collective-permute-start.2) | collective-permute-done | bytes 131104 | tf_op jit(solution)/shard_map/ppermute | solution.py:42
  112.1 0.0 all-to-all-done.3.key_ref
  112.1 5.3 %attend.1 = (f32[8,136,128]{2,1,0:T(8,128)}, bf16[2,8,64,128]{3,2,1,0:T(8,128)(2,1)S(1)}, bf16[2,8,64,128]{3,2,1,0:T(8,128)(2,1)S(1)}) custom-call(s32[5]{0:T(128)S(1)} %stack.23.place_ref, bf16[8,208,128]{2,1,0:T(8,128)(2,1)S(1)} %all_to_all.36.query_ref, bf16[8,272,128]{2,1,0:T(8,128)(2,1)S(1)} %all-to-all-done.3.key_ref, ...), custom_call_target="tpu_custom_call" | custom-call | flops 536870912 | bytes 2097152 | tf_op jit(solution)/shard_map/attend/pallas_call | solution.py:251
  117.4 5.9 %all-to-all-start.4 = ((f32[8,136,128]{2,1,0:T(8,128)}), f32[8,136,128]{2,1,0:T(8,128)S(1)}, u32[]{:S(2)}, u32[]{:S(2)}) async-start(f32[8,136,128]{2,1,0:T(8,128)} %get-tuple-element.15), calls=%async_computation.4 | async-start | bytes 1114112 | tf_op jit(solution)/shard_map/all_to_all | solution.py:31
  123.3 4.3 %collective-permute-start.3 = (bf16[2,8,64,128]{3,2,1,0:T(8,128)(2,1)S(1)}, bf16[2,8,64,128]{3,2,1,0:T(8,128)(2,1)S(1)}, u32[]{:S(2)}, u32[]{:S(2)}) collective-permute-start(bf16[2,8,64,128]{3,2,1,0:T(8,128)(2,1)S(1)} %get-tuple-element.16.own_ref), channel_id=1, source_target_pairs={{0,24},{1,25},{2,26},{3,27},{4,28},{5,29},{6,30},{7,31},{8,0},{9,1... | collective-permute-start | bytes 786440 | tf_op jit(solution)/shard_map/ppermute | solution.py:42
  127.6 5.6 %all-to-all-done.4.part_ref = f32[8,136,128]{2,1,0:T(8,128)S(1)} async-done(((f32[8,136,128]{2,1,0:T(8,128)}), f32[8,136,128]{2,1,0:T(8,128)S(1)}, u32[]{:S(2)}, u32[]{:S(2)}) %all-to-all-start.4) | async-done | bytes 557088 | tf_op jit(solution)/shard_map/all_to_all | solution.py:31
  133.1 0.9 combine.1
  134.0 7.6 %all-to-all-start.5 = ((bf16[16,8,128]{2,1,0:T(8,128)(2,1)}), bf16[16,8,128]{2,1,0:T(8,128)(2,1)S(1)}, u32[]{:S(2)}, u32[]{:S(2)}) async-start(bf16[16,8,128]{2,1,0:T(8,128)(2,1)} %bitcast.10), calls=%async_computation.5 | async-start | bytes 65536 | tf_op jit(solution)/shard_map/all_to_all | solution.py:31
  141.6 3.2 %collective-permute-start.5 = (bf16[2,8,64,128]{3,2,1,0:T(8,128)(2,1)S(1)}, bf16[2,8,64,128]{3,2,1,0:T(8,128)(2,1)S(1)}, u32[]{:S(2)}, u32[]{:S(2)}) collective-permute-start(bf16[2,8,64,128]{3,2,1,0:T(8,128)(2,1)S(1)} %get-tuple-element.16.own_ref), channel_id=1, source_target_pairs={{0,8},{1,9},{2,10},{3,11},{4,12},{5,13},{6,14},{7,15},{8,16},{9,17... | collective-permute-start | bytes 786440 | tf_op jit(solution)/shard_map/ppermute | solution.py:42
  144.8 4.3 %collective-permute-start.4 = (bf16[2,8,64,128]{3,2,1,0:T(8,128)(2,1)S(1)}, bf16[2,8,64,128]{3,2,1,0:T(8,128)(2,1)S(1)}, u32[]{:S(2)}, u32[]{:S(2)}) collective-permute-start(bf16[2,8,64,128]{3,2,1,0:T(8,128)(2,1)S(1)} %get-tuple-element.19.refs_0_), channel_id=1, source_target_pairs={{0,16},{1,17},{2,18},{3,19},{4,20},{5,21},{6,22},{7,23},{8,24},{9,... | collective-permute-start | bytes 786440 | tf_op jit(solution)/shard_map/ppermute | solution.py:42
  149.1 3.1 %collective-permute-start.6 = (bf16[2,8,64,128]{3,2,1,0:T(8,128)(2,1)S(1)}, bf16[2,8,64,128]{3,2,1,0:T(8,128)(2,1)S(1)}, u32[]{:S(2)}, u32[]{:S(2)}) collective-permute-start(bf16[2,8,64,128]{3,2,1,0:T(8,128)(2,1)S(1)} %get-tuple-element.20.refs_4_), channel_id=1, source_target_pairs={{0,24},{1,25},{2,26},{3,27},{4,28},{5,29},{6,30},{7,31},{8,0},{9,1... | collective-permute-start | bytes 786440 | tf_op jit(solution)/shard_map/ppermute | solution.py:42
  152.2 2.1 %collective-permute-start.7 = (bf16[2,8,64,128]{3,2,1,0:T(8,128)(2,1)S(1)}, bf16[2,8,64,128]{3,2,1,0:T(8,128)(2,1)S(1)}, u32[]{:S(2)}, u32[]{:S(2)}) collective-permute-start(bf16[2,8,64,128]{3,2,1,0:T(8,128)(2,1)S(1)} %get-tuple-element.20.refs_4_), channel_id=1, source_target_pairs={{0,16},{1,17},{2,18},{3,19},{4,20},{5,21},{6,22},{7,23},{8,24},{9,... | collective-permute-start | bytes 786440 | tf_op jit(solution)/shard_map/ppermute | solution.py:42
  154.3 0.0 collective-permute-done.3.refs_1_
  154.3 2.3 %collective-permute-start.8 = (bf16[2,8,64,128]{3,2,1,0:T(8,128)(2,1)S(1)}, bf16[2,8,64,128]{3,2,1,0:T(8,128)(2,1)S(1)}, u32[]{:S(2)}, u32[]{:S(2)}) collective-permute-start(bf16[2,8,64,128]{3,2,1,0:T(8,128)(2,1)S(1)} %get-tuple-element.20.refs_4_), channel_id=1, source_target_pairs={{0,8},{1,9},{2,10},{3,11},{4,12},{5,13},{6,14},{7,15},{8,16},{9,17... | collective-permute-start | bytes 786440 | tf_op jit(solution)/shard_map/ppermute | solution.py:42
  156.6 6.1 %all-to-all-done.5 = bf16[16,8,128]{2,1,0:T(8,128)(2,1)S(1)} async-done(((bf16[16,8,128]{2,1,0:T(8,128)(2,1)}), bf16[16,8,128]{2,1,0:T(8,128)(2,1)S(1)}, u32[]{:S(2)}, u32[]{:S(2)}) %all-to-all-start.5) | async-done | bytes 32800 | tf_op jit(solution)/shard_map/all_to_all | solution.py:31
  162.7 0.7 broadcast_in_dim.2
  163.4 0.0 copy-start
  163.4 5.7 %all-to-all-start.6 = ((bf16[8,16,8,128]{3,2,1,0:T(8,128)(2,1)}), bf16[8,16,8,128]{3,2,1,0:T(8,128)(2,1)S(1)}, u32[]{:S(2)}, u32[]{:S(2)}) async-start(bf16[8,16,8,128]{3,2,1,0:T(8,128)(2,1)} %broadcast_in_dim.2), calls=%async_computation.6 | async-start | bytes 524288 | tf_op jit(solution)/shard_map/all_to_all | solution.py:31
  169.1 0.0 collective-permute-done.5.refs_3_
  169.1 0.0 collective-permute-done.4.refs_2_
  169.1 0.0 collective-permute-done.6.refs_5_
  169.2 0.0 collective-permute-done.7.refs_6_
  169.2 1.6 collective-permute-done.8.refs_7_
  170.7 4.9 %all-to-all-done.6.attended_ref = bf16[8,16,8,128]{3,2,1,0:T(8,128)(2,1)S(1)} async-done(((bf16[8,16,8,128]{3,2,1,0:T(8,128)(2,1)}), bf16[8,16,8,128]{3,2,1,0:T(8,128)(2,1)S(1)}, u32[]{:S(2)}, u32[]{:S(2)}) %all-to-all-start.6) | async-done | bytes 262176 | tf_op jit(solution)/shard_map/all_to_all | solution.py:31
  175.7 0.0 copy-done
  175.7 2.0 %product.1 = bf16[64,512]{1,0:T(8,128)(2,1)} custom-call(s32[5]{0:T(128)S(1)} %stack.23.place_ref, bf16[8,16,8,128]{3,2,1,0:T(8,128)(2,1)S(1)} %all-to-all-done.6.attended_ref, bf16[2,8,64,128]{3,2,1,0:T(8,128)(2,1)S(1)} %get-tuple-element.19.refs_0_, bf16[2,8,64,128]{3,2,1,0:T(8,128)(2,1)S(1)} %collective-permute-done.3.refs_1_, ...), custom_call_target="tpu_custom_call" | custom-call | flops 134217728 | bytes 3145728 | tf_op jit(solution)/shard_map/product/pallas_call | solution.py:273
  (2 shorter events, 0.0 us)
Async XLA Ops:
  1.4 22.4 %all-to-all-start = ((bf16[8,24,256]{2,1,0:T(8,128)(2,1)}), bf16[8,24,256]{2,1,0:T(8,128)(2,1)S(1)}, u32[]{:S(2)}, u32[]{:S(2)}) async-start(bf16[8,24,256]{2,1,0:T(8,128)(2,1)} %pad_maximum_fusion), calls=%async_computation | async-start | bytes 196608 | tf_op jit(solution)/shard_map/all_to_all | solution.py:31
  18.9 0.7 copy-start.2
  18.9 5.0 %copy-start.1 = (bf16[256,32]{0,1:T(8,128)(2,1)S(1)}, bf16[256,32]{0,1:T(8,128)(2,1)}, u32[]{:S(2)}) copy-start(bf16[256,32]{0,1:T(8,128)(2,1)} %param.10) | copy-start | bytes 49156
  82.8 29.3 %all-to-all-start.3 = ((bf16[8,272,128]{2,1,0:T(8,128)(2,1)}), bf16[8,272,128]{2,1,0:T(8,128)(2,1)S(1)}, u32[]{:S(2)}, u32[]{:S(2)}) async-start(bf16[8,272,128]{2,1,0:T(8,128)(2,1)} %get-tuple-element.14), calls=%async_computation.3 | async-start | bytes 1114112 | tf_op jit(solution)/shard_map/all_to_all | solution.py:31
  92.4 11.9 %collective-permute-start = (bf16[8,64,128]{2,1,0:T(8,128)(2,1)S(1)}, bf16[8,64,128]{2,1,0:T(8,128)(2,1)S(1)}, u32[]{:S(2)}, u32[]{:S(2)}) collective-permute-start(bf16[8,64,128]{2,1,0:T(8,128)(2,1)S(1)} %slice.4), channel_id=1, source_target_pairs={{0,32},{1,33},{2,34},{3,35},{4,36},{5,37},{6,38},{7,39},{8,40},{9,... | collective-permute-start | bytes 393224 | tf_op jit(solution)/shard_map/ppermute | solution.py:42
  95.8 9.0 %collective-permute-start.1 = (bf16[8,64,128]{2,1,0:T(8,128)(2,1)S(1)}, bf16[8,64,128]{2,1,0:T(8,128)(2,1)S(1)}, u32[]{:S(2)}, u32[]{:S(2)}) collective-permute-start(bf16[8,64,128]{2,1,0:T(8,128)(2,1)S(1)} %slice.4), channel_id=1, source_target_pairs={{0,64},{1,65},{2,66},{3,67},{4,68},{5,69},{6,70},{7,71},{8,72},{9,... | collective-permute-start | bytes 393224 | tf_op jit(solution)/shard_map/ppermute | solution.py:42
  102.3 9.9 %collective-permute-start.2 = (bf16[8,64,128]{2,1,0:T(8,128)(2,1)S(1)}, bf16[8,64,128]{2,1,0:T(8,128)(2,1)S(1)}, u32[]{:S(2)}, u32[]{:S(2)}) collective-permute-start(bf16[8,64,128]{2,1,0:T(8,128)(2,1)S(1)} %slice.4), channel_id=1, source_target_pairs={{0,96},{1,97},{2,98},{3,99},{4,100},{5,101},{6,102},{7,103},{8,104... | collective-permute-start | bytes 393224 | tf_op jit(solution)/shard_map/ppermute | solution.py:42
  117.4 15.7 %all-to-all-start.4 = ((f32[8,136,128]{2,1,0:T(8,128)}), f32[8,136,128]{2,1,0:T(8,128)S(1)}, u32[]{:S(2)}, u32[]{:S(2)}) async-start(f32[8,136,128]{2,1,0:T(8,128)} %get-tuple-element.15), calls=%async_computation.4 | async-start | bytes 1114112 | tf_op jit(solution)/shard_map/all_to_all | solution.py:31
  123.3 31.0 %collective-permute-start.3 = (bf16[2,8,64,128]{3,2,1,0:T(8,128)(2,1)S(1)}, bf16[2,8,64,128]{3,2,1,0:T(8,128)(2,1)S(1)}, u32[]{:S(2)}, u32[]{:S(2)}) collective-permute-start(bf16[2,8,64,128]{3,2,1,0:T(8,128)(2,1)S(1)} %get-tuple-element.16.own_ref), channel_id=1, source_target_pairs={{0,24},{1,25},{2,26},{3,27},{4,28},{5,29},{6,30},{7,31},{8,0},{9,1... | collective-permute-start | bytes 786440 | tf_op jit(solution)/shard_map/ppermute | solution.py:42
  134.0 28.7 %all-to-all-start.5 = ((bf16[16,8,128]{2,1,0:T(8,128)(2,1)}), bf16[16,8,128]{2,1,0:T(8,128)(2,1)S(1)}, u32[]{:S(2)}, u32[]{:S(2)}) async-start(bf16[16,8,128]{2,1,0:T(8,128)(2,1)} %bitcast.10), calls=%async_computation.5 | async-start | bytes 65536 | tf_op jit(solution)/shard_map/all_to_all | solution.py:31
  141.6 27.6 %collective-permute-start.5 = (bf16[2,8,64,128]{3,2,1,0:T(8,128)(2,1)S(1)}, bf16[2,8,64,128]{3,2,1,0:T(8,128)(2,1)S(1)}, u32[]{:S(2)}, u32[]{:S(2)}) collective-permute-start(bf16[2,8,64,128]{3,2,1,0:T(8,128)(2,1)S(1)} %get-tuple-element.16.own_ref), channel_id=1, source_target_pairs={{0,8},{1,9},{2,10},{3,11},{4,12},{5,13},{6,14},{7,15},{8,16},{9,17... | collective-permute-start | bytes 786440 | tf_op jit(solution)/shard_map/ppermute | solution.py:42
  144.8 24.4 %collective-permute-start.4 = (bf16[2,8,64,128]{3,2,1,0:T(8,128)(2,1)S(1)}, bf16[2,8,64,128]{3,2,1,0:T(8,128)(2,1)S(1)}, u32[]{:S(2)}, u32[]{:S(2)}) collective-permute-start(bf16[2,8,64,128]{3,2,1,0:T(8,128)(2,1)S(1)} %get-tuple-element.19.refs_0_), channel_id=1, source_target_pairs={{0,16},{1,17},{2,18},{3,19},{4,20},{5,21},{6,22},{7,23},{8,24},{9,... | collective-permute-start | bytes 786440 | tf_op jit(solution)/shard_map/ppermute | solution.py:42
  149.1 20.1 %collective-permute-start.6 = (bf16[2,8,64,128]{3,2,1,0:T(8,128)(2,1)S(1)}, bf16[2,8,64,128]{3,2,1,0:T(8,128)(2,1)S(1)}, u32[]{:S(2)}, u32[]{:S(2)}) collective-permute-start(bf16[2,8,64,128]{3,2,1,0:T(8,128)(2,1)S(1)} %get-tuple-element.20.refs_4_), channel_id=1, source_target_pairs={{0,24},{1,25},{2,26},{3,27},{4,28},{5,29},{6,30},{7,31},{8,0},{9,1... | collective-permute-start | bytes 786440 | tf_op jit(solution)/shard_map/ppermute | solution.py:42
  152.2 17.0 %collective-permute-start.7 = (bf16[2,8,64,128]{3,2,1,0:T(8,128)(2,1)S(1)}, bf16[2,8,64,128]{3,2,1,0:T(8,128)(2,1)S(1)}, u32[]{:S(2)}, u32[]{:S(2)}) collective-permute-start(bf16[2,8,64,128]{3,2,1,0:T(8,128)(2,1)S(1)} %get-tuple-element.20.refs_4_), channel_id=1, source_target_pairs={{0,16},{1,17},{2,18},{3,19},{4,20},{5,21},{6,22},{7,23},{8,24},{9,... | collective-permute-start | bytes 786440 | tf_op jit(solution)/shard_map/ppermute | solution.py:42
  154.3 16.4 %collective-permute-start.8 = (bf16[2,8,64,128]{3,2,1,0:T(8,128)(2,1)S(1)}, bf16[2,8,64,128]{3,2,1,0:T(8,128)(2,1)S(1)}, u32[]{:S(2)}, u32[]{:S(2)}) collective-permute-start(bf16[2,8,64,128]{3,2,1,0:T(8,128)(2,1)S(1)} %get-tuple-element.20.refs_4_), channel_id=1, source_target_pairs={{0,8},{1,9},{2,10},{3,11},{4,12},{5,13},{6,14},{7,15},{8,16},{9,17... | collective-permute-start | bytes 786440 | tf_op jit(solution)/shard_map/ppermute | solution.py:42
  163.4 12.2 %copy-start = (bf16[64,512]{1,0:T(8,128)(2,1)S(1)}, bf16[64,512]{1,0:T(8,128)(2,1)}, u32[]{:S(2)}) copy-start(bf16[64,512]{1,0:T(8,128)(2,1)} %refs_8_.1) | copy-start | bytes 196612
  163.4 12.2 %all-to-all-start.6 = ((bf16[8,16,8,128]{3,2,1,0:T(8,128)(2,1)}), bf16[8,16,8,128]{3,2,1,0:T(8,128)(2,1)S(1)}, u32[]{:S(2)}, u32[]{:S(2)}) async-start(bf16[8,16,8,128]{3,2,1,0:T(8,128)(2,1)} %broadcast_in_dim.2), calls=%async_computation.6 | async-start | bytes 524288 | tf_op jit(solution)/shard_map/all_to_all | solution.py:31

commit v5 on v3

--- a/solution.py
+++ b/solution.py
@@ -84,7 +84,7 @@
 GATHERED = COLUMNS_AT + 2 * COLUMNS
 
 
-def gather_kernel(place_ref, came_ref, query_ref, key_ref):
+def gather_kernel(came_ref, query_ref, key_ref):
     planes = came_ref.shape[0]
     first = [came_ref[i, 0 : 2 * EACH, :].astype(jnp.float32) for i in range(planes)]
     second = [came_ref[i, 2 * EACH : 4 * EACH, :].astype(jnp.float32) for i in range(planes)]
@@ -96,12 +96,10 @@
     lane = lax.broadcasted_iota(jnp.int32, (EACH, LANES), 1)
     docs = jnp.zeros((EACH, LANES), jnp.float32)
     for i, tile in enumerate(second):
-        own = pltpu.roll(tile[EACH:], EACH * i, 1)
-        docs = jnp.where(lane // EACH == i, own, docs)
+        docs = jnp.where(lane // EACH == i, pltpu.roll(tile[EACH:], EACH * i, 1), docs)
     docs = jnp.concatenate([docs, docs], axis=0).astype(jnp.bfloat16)
-    for s in range(query_ref.shape[0]):
-        query_ref[s, 0:ROWS, :] = queries
-        query_ref[s, ROWS : ROWS + 16, :] = docs
+    query_ref[0:ROWS, :] = queries
+    query_ref[ROWS : ROWS + 16, :] = docs
     for s in range(key_ref.shape[0]):
         key_ref[s, 0:ROWS, :] = keys
         key_ref[s, ROWS:DOCS_AT, :] = values
@@ -111,9 +109,7 @@
             key_ref[s, at : at + COLUMNS, :] = came_ref[2 * s + k, WEIGHT_AT:SENT, :]
 
 
-def attend_kernel(place_ref, query_ref, key_ref, other_ref, out_ref, columns_ref, score_ref):
-    columns_ref[0] = key_ref[:, COLUMNS_AT:GATHERED, :]
-    columns_ref[1] = other_ref[...]
+def attend_kernel(place_ref, query_ref, key_ref, out_ref, score_ref):
     z2, y, x, c = (place_ref[k] for k in range(4))
     stripe = 2 * BLOCK * 4
 
@@ -158,8 +154,11 @@
         out_ref[r, ROWS : ROWS + 8, :] = jnp.concatenate([row_max.T[0:4], row_sum.T[0:4]], axis=0)
 
 
-def combine_kernel(part_ref, columns_ref, out_ref, same_ref):
-    same_ref[...] = columns_ref[...]
+def combine_kernel(part_ref, key_ref, by_z1, by_z2, by_z3, out_ref, own_ref, other_ref):
+    own_ref[0] = key_ref[:, COLUMNS_AT:GATHERED, :]
+    own_ref[1] = by_z2[...]
+    other_ref[0] = by_z1[...]
+    other_ref[1] = by_z3[...]
     parts = part_ref.shape[0]
     maxima = [part_ref[r, ROWS : ROWS + 1, :] for r in range(parts)]
     sums = [part_ref[r, ROWS + 4 : ROWS + 5, :] for r in range(parts)]
@@ -229,42 +228,41 @@
     queries, keys = call(
         gather_kernel,
         [
-            jax.ShapeDtypeStruct((spread, ROWS + 16, LANES), bf16),
+            jax.ShapeDtypeStruct((ROWS + 16, LANES), bf16),
             jax.ShapeDtypeStruct((groups, GATHERED, LANES), bf16),
         ],
-        [SMEM, VMEM],
+        [VMEM],
         "spread",
-    )(place, came)
+    )(came)
     keys = exchange(keys, HEAD_AXES)
-    queries = exchange(queries, QUERY_AXES)
-
-    columns = keys[:, COLUMNS_AT:]
-    columns = moved(columns, lambda z, y, x, c: (z ^ 2, y, x, c))
-    held = jax.ShapeDtypeStruct((2, *columns.shape), bf16)
-
-    def every_y(block):
-        return [block] + [
-            moved(block, lambda z, y, x, c: (z, (y - k) % 4, x, c)) for k in (1, 2, 3)
-        ]
-
-    parts, columns = call(
+    queries = lax.all_gather(queries, QUERY_AXES)
+
+    parts = call(
         attend_kernel,
-        [jax.ShapeDtypeStruct((spread, ROWS + 8, LANES), f32), held],
-        [SMEM] + [VMEM] * 3,
+        jax.ShapeDtypeStruct((spread, ROWS + 8, LANES), f32),
+        [SMEM] + [VMEM] * 2,
         "attend",
         [pltpu.VMEM((groups, ROWS, LANES), f32)],
         4 * spread * ROWS * groups * ROWS * HEAD_DIM,
         2 << 20,
-    )(place, queries, keys, columns)
+    )(place, queries, keys)
     parts = exchange(parts, QUERY_AXES)
-    weights = every_y(columns)
-    attended, columns = call(
+
+    columns = keys[:, COLUMNS_AT:]
+    near = [moved(columns, lambda z, y, x, c: (z ^ far, y, x, c)) for far in (1, 2, 3)]
+    held = jax.ShapeDtypeStruct((2, *columns.shape), bf16)
+    attended, own, other = call(
         combine_kernel,
-        [jax.ShapeDtypeStruct((ROWS, HEAD_DIM), bf16), held],
-        [VMEM] * 2,
+        [jax.ShapeDtypeStruct((ROWS, HEAD_DIM), bf16), held, held],
+        [VMEM] * 5,
         "combine",
-    )(parts, moved(columns, lambda z, y, x, c: (z ^ 1, y, x, c)))
-    weights += every_y(columns)
+    )(parts, keys, *near)
+
+    def from_y(block, k):
+        return moved(block, lambda z, y, x, c: (z, (y - k) % 4, x, c))
+
+    weights = [own] + [from_y(own, k) for k in (1, 2, 3)]
+    weights += [other] + [from_y(other, k) for k in (1, 2, 3)]
 
     back = exchange(attended.reshape(planes, EACH, HEAD_DIM), PLANES)
     everyone = exchange(jnp.broadcast_to(back[None], (groups, *back.shape)), HEAD_AXES)

time: 179 us -> 186 us (1.039)
  blocking collectives: 20.4 us -> 67.9 us
  waiting for transfers between devices: 48.6 us -> 19.9 us
  starting transfers between devices: 95.7 us -> 84.8 us
    all_gather x0 -> x1, blocking collectives: none -> 27.5 us  [shards(): queries = lax.all_gather(queries, QUERY_AXES)]
    all_to_all x6 -> x5, waiting for transfers between devices: 39.3 us -> 15.6 us  [exchange(): return lax.all_to_all(tiles, axes, split_axis=0, concat_axis=0, tiled=True)]
    all_to_all x1, blocking collectives: 20.4 us -> 40.5 us  [exchange(): return lax.all_to_all(tiles, axes, split_axis=0, concat_axis=0, tiled=True)]
    all_to_all x6 -> x5, starting transfers between devices: 66.4 us -> 53.8 us  [exchange(): return lax.all_to_all(tiles, axes, split_axis=0, concat_axis=0, tiled=True)]
    ppermute x8 -> x9, waiting for transfers between devices: 9.33 us -> 4.3 us  [moved(): lax.ppermute(block, names, [(flat(*p), flat(*where(*p))) for p in places])]
    ppermute x8 -> x9, starting transfers between devices: 29.4 us -> 31 us  [moved(): lax.ppermute(block, names, [(flat(*p), flat(*where(*p))) for p in places])]
  transfers between devices with their start and end apart: 14 -> 14, of which waited for: 6 -> 5; matrix products, arithmetic and copies ran while one was open for 1% -> 1% of each run, Pallas kernels for 0% -> 0%
where the time goes in v5:
time: 186 us; the launch traced here: 185 us
  starting transfers between devices  84.8 us (46%)
  blocking collectives  67.9 us (37%)
  waiting for transfers between devices  19.9 us (11%)
  Pallas kernels  9.11 us (5%)
    all_to_all x5, starting transfers between devices, exchange(): return lax.all_to_all(tiles, axes, split_axis=0, concat_axis=0, tiled=True)  53.8 us
    all_to_all x1, blocking collectives, exchange(): return lax.all_to_all(tiles, axes, split_axis=0, concat_axis=0, tiled=True)  40.5 us
    ppermute x9, starting transfers between devices, moved(): lax.ppermute(block, names, [(flat(*p), flat(*where(*p))) for p in places])  31 us
    all_gather x1, blocking collectives, shards(): queries = lax.all_gather(queries, QUERY_AXES)  27.5 us
    all_to_all x5, waiting for transfers between devices, exchange(): return lax.all_to_all(tiles, axes, split_axis=0, concat_axis=0, tiled=True)  15.6 us
    pallas_call x1, Pallas kernels, shards(): call(attend_kernel, jax.ShapeDtypeStruct((spread, ROWS + 8, LANES), f32),...  5.26 us
    ppermute x9, waiting for transfers between devices, moved(): lax.ppermute(block, names, [(flat(*p), flat(*where(*p))) for p in places])  4.3 us
  transfers between devices with their start and end apart: 14, of which 5 were waited for; matrix products, arithmetic and copies ran while one was open for 1% of the time, Pallas kernels for 0%

profile of v5, /device:TPU:1, one launch (start us, length us, event | category | flops | bytes accessed | tf_op | source)
XLA Modules:
  0.0 185.1 jit_solution(16544269459010901723)
XLA Ops:
  0.0 1.4 pad_maximum_fusion
  1.4 17.4 %all-to-all-start = ((bf16[8,24,256]{2,1,0:T(8,128)(2,1)}), bf16[8,24,256]{2,1,0:T(8,128)(2,1)S(1)}, u32[]{:S(2)}, u32[]{:S(2)}) async-start(bf16[8,24,256]{2,1,0:T(8,128)(2,1)} %pad_maximum_fusion), calls=%async_computation | async-start | bytes 196608 | tf_op jit(solution)/shard_map/all_to_all | solution.py:31
  18.8 0.0 copy-start.1
  18.8 0.0 copy-start.2
  18.9 0.7 copy-done.2
  19.5 0.1 pad_add_fusion
  19.6 0.1 convert_bitcast_fusion
  19.7 0.1 pad_maximum_fusion.1.docs_ref
  19.8 4.1 %all-to-all-done.rows_ref = bf16[8,24,256]{2,1,0:T(8,128)(2,1)S(1)} async-done(((bf16[8,24,256]{2,1,0:T(8,128)(2,1)}), bf16[8,24,256]{2,1,0:T(8,128)(2,1)S(1)}, u32[]{:S(2)}, u32[]{:S(2)}) %all-to-all-start) | async-done | bytes 98336 | tf_op jit(solution)/shard_map/all_to_all | solution.py:31
  23.8 0.0 copy-done.1
  23.9 40.5 %all_to_all.30.came_ref = bf16[16,64,128]{2,1,0:T(8,128)(2,1)S(1)} all-to-all(bf16[16,64,128]{2,1,0:T(8,128)(2,1)S(1)} %send.1), channel_id=1, replica_groups=mesh['zh'=8,'zp'=2,'z2'=2,'y'=4,'x'=4,'c'=2] {'zh','zp'}, dimensions={0} | all-to-all | bytes 524288 | tf_op jit(solution)/shard_map/all_to_all | solution.py:31
  64.4 1.0 spread.1
  65.3 10.2 %all-to-all-start.2 = ((bf16[8,336,128]{2,1,0:T(8,128)(2,1)}), bf16[8,336,128]{2,1,0:T(8,128)(2,1)S(1)}, u32[]{:S(2)}, u32[]{:S(2)}) async-start(bf16[8,336,128]{2,1,0:T(8,128)(2,1)} %get-tuple-element.11), calls=%async_computation.2 | async-start | bytes 1376256 | tf_op jit(solution)/shard_map/all_to_all | solution.py:31
  75.5 0.1 stack.23.place_ref
  75.6 27.5 %all-gather = bf16[1152,128]{1,0:T(8,128)(2,1)S(1)} all-gather(bf16[144,128]{1,0:T(8,128)(2,1)S(1)} %get-tuple-element.10), channel_id=2, replica_groups=mesh['zh'=8,'zp'=2,'z2'=2,'y'=4,'x'=4,'c'=2] {'z2','y'}, dimensions={0}, use_global_device_ids=true | all-gather | bytes 331776 | tf_op jit(solution)/shard_map/all_gather | solution.py:238
  103.1 0.0 all-to-all-done.2.key_ref
  103.1 5.3 %attend.1 = f32[8,136,128]{2,1,0:T(8,128)} custom-call(s32[5]{0:T(128)S(1)} %stack.23.place_ref, bf16[8,144,128]{2,1,0:T(8,128)(2,1)S(1)} %bitcast.13, bf16[8,336,128]{2,1,0:T(8,128)(2,1)S(1)} %all-to-all-done.2.key_ref), custom_call_target="tpu_custom_call" | custom-call | flops 536870912 | bytes 2097152 | tf_op jit(solution)/shard_map/attend/pallas_call | solution.py:240
  108.3 4.9 %all-to-all-start.3 = ((f32[8,136,128]{2,1,0:T(8,128)}), f32[8,136,128]{2,1,0:T(8,128)S(1)}, u32[]{:S(2)}, u32[]{:S(2)}) async-start(f32[8,136,128]{2,1,0:T(8,128)} %attend.1), calls=%async_computation.3 | async-start | bytes 1114112 | tf_op jit(solution)/shard_map/all_to_all | solution.py:31
  113.2 7.7 %collective-permute-start.2 = (bf16[8,64,128]{2,1,0:T(8,128)(2,1)S(1)}, bf16[8,64,128]{2,1,0:T(8,128)(2,1)S(1)}, u32[]{:S(2)}, u32[]{:S(2)}) collective-permute-start(bf16[8,64,128]{2,1,0:T(8,128)(2,1)S(1)} %slice.4), channel_id=1, source_target_pairs={{0,96},{1,97},{2,98},{3,99},{4,100},{5,101},{6,102},{7,103},{8,104... | collective-permute-start | bytes 393224 | tf_op jit(solution)/shard_map/ppermute | solution.py:42
  120.9 1.9 %collective-permute-start.1 = (bf16[8,64,128]{2,1,0:T(8,128)(2,1)S(1)}, bf16[8,64,128]{2,1,0:T(8,128)(2,1)S(1)}, u32[]{:S(2)}, u32[]{:S(2)}) collective-permute-start(bf16[8,64,128]{2,1,0:T(8,128)(2,1)S(1)} %slice.4), channel_id=1, source_target_pairs={{0,64},{1,65},{2,66},{3,67},{4,68},{5,69},{6,70},{7,71},{8,72},{9,... | collective-permute-start | bytes 393224 | tf_op jit(solution)/shard_map/ppermute | solution.py:42
  122.8 2.2 %collective-permute-start = (bf16[8,64,128]{2,1,0:T(8,128)(2,1)S(1)}, bf16[8,64,128]{2,1,0:T(8,128)(2,1)S(1)}, u32[]{:S(2)}, u32[]{:S(2)}) collective-permute-start(bf16[8,64,128]{2,1,0:T(8,128)(2,1)S(1)} %slice.4), channel_id=1, source_target_pairs={{0,32},{1,33},{2,34},{3,35},{4,36},{5,37},{6,38},{7,39},{8,40},{9,... | collective-permute-start | bytes 393224 | tf_op jit(solution)/shard_map/ppermute | solution.py:42
  125.0 0.0 collective-permute-done.2.by_z3
  125.0 3.7 %collective-permute-done.1.by_z2 = bf16[8,64,128]{2,1,0:T(8,128)(2,1)S(1)} collective-permute-done((bf16[8,64,128]{2,1,0:T(8,128)(2,1)S(1)}, bf16[8,64,128]{2,1,0:T(8,128)(2,1)S(1)}, u32[]{:S(2)}, u32[]{:S(2)}) %collective-permute-start.1) | collective-permute-done | bytes 131104 | tf_op jit(solution)/shard_map/ppermute | solution.py:42
  128.7 0.6 collective-permute-done.by_z1
  129.3 0.0 all-to-all-done.3.part_ref
  129.3 0.9 combine.1
  130.2 3.2 %collective-permute-start.5 = (bf16[2,8,64,128]{3,2,1,0:T(8,128)(2,1)S(1)}, bf16[2,8,64,128]{3,2,1,0:T(8,128)(2,1)S(1)}, u32[]{:S(2)}, u32[]{:S(2)}) collective-permute-start(bf16[2,8,64,128]{3,2,1,0:T(8,128)(2,1)S(1)} %get-tuple-element.13.refs_0_), channel_id=1, source_target_pairs={{0,8},{1,9},{2,10},{3,11},{4,12},{5,13},{6,14},{7,15},{8,16},{9,17... | collective-permute-start | bytes 786440 | tf_op jit(solution)/shard_map/ppermute | solution.py:42
  133.4 9.5 %all-to-all-start.4 = ((bf16[16,8,128]{2,1,0:T(8,128)(2,1)}), bf16[16,8,128]{2,1,0:T(8,128)(2,1)S(1)}, u32[]{:S(2)}, u32[]{:S(2)}) async-start(bf16[16,8,128]{2,1,0:T(8,128)(2,1)} %bitcast.11), calls=%async_computation.4 | async-start | bytes 65536 | tf_op jit(solution)/shard_map/all_to_all | solution.py:31
  142.9 4.3 %collective-permute-start.4 = (bf16[2,8,64,128]{3,2,1,0:T(8,128)(2,1)S(1)}, bf16[2,8,64,128]{3,2,1,0:T(8,128)(2,1)S(1)}, u32[]{:S(2)}, u32[]{:S(2)}) collective-permute-start(bf16[2,8,64,128]{3,2,1,0:T(8,128)(2,1)S(1)} %get-tuple-element.13.refs_0_), channel_id=1, source_target_pairs={{0,16},{1,17},{2,18},{3,19},{4,20},{5,21},{6,22},{7,23},{8,24},{9,... | collective-permute-start | bytes 786440 | tf_op jit(solution)/shard_map/ppermute | solution.py:42
  147.2 3.1 %collective-permute-start.3 = (bf16[2,8,64,128]{3,2,1,0:T(8,128)(2,1)S(1)}, bf16[2,8,64,128]{3,2,1,0:T(8,128)(2,1)S(1)}, u32[]{:S(2)}, u32[]{:S(2)}) collective-permute-start(bf16[2,8,64,128]{3,2,1,0:T(8,128)(2,1)S(1)} %get-tuple-element.13.refs_0_), channel_id=1, source_target_pairs={{0,24},{1,25},{2,26},{3,27},{4,28},{5,29},{6,30},{7,31},{8,0},{9,1... | collective-permute-start | bytes 786440 | tf_op jit(solution)/shard_map/ppermute | solution.py:42
  150.3 2.2 %collective-permute-start.8 = (bf16[2,8,64,128]{3,2,1,0:T(8,128)(2,1)S(1)}, bf16[2,8,64,128]{3,2,1,0:T(8,128)(2,1)S(1)}, u32[]{:S(2)}, u32[]{:S(2)}) collective-permute-start(bf16[2,8,64,128]{3,2,1,0:T(8,128)(2,1)S(1)} %get-tuple-element.14.refs_4_), channel_id=1, source_target_pairs={{0,8},{1,9},{2,10},{3,11},{4,12},{5,13},{6,14},{7,15},{8,16},{9,17... | collective-permute-start | bytes 786440 | tf_op jit(solution)/shard_map/ppermute | solution.py:42
  152.5 2.8 %collective-permute-start.7 = (bf16[2,8,64,128]{3,2,1,0:T(8,128)(2,1)S(1)}, bf16[2,8,64,128]{3,2,1,0:T(8,128)(2,1)S(1)}, u32[]{:S(2)}, u32[]{:S(2)}) collective-permute-start(bf16[2,8,64,128]{3,2,1,0:T(8,128)(2,1)S(1)} %get-tuple-element.14.refs_4_), channel_id=1, source_target_pairs={{0,16},{1,17},{2,18},{3,19},{4,20},{5,21},{6,22},{7,23},{8,24},{9,... | collective-permute-start | bytes 786440 | tf_op jit(solution)/shard_map/ppermute | solution.py:42
  155.3 0.0 collective-permute-done.5.refs_3_
  155.3 3.6 %collective-permute-start.6 = (bf16[2,8,64,128]{3,2,1,0:T(8,128)(2,1)S(1)}, bf16[2,8,64,128]{3,2,1,0:T(8,128)(2,1)S(1)}, u32[]{:S(2)}, u32[]{:S(2)}) collective-permute-start(bf16[2,8,64,128]{3,2,1,0:T(8,128)(2,1)S(1)} %get-tuple-element.14.refs_4_), channel_id=1, source_target_pairs={{0,24},{1,25},{2,26},{3,27},{4,28},{5,29},{6,30},{7,31},{8,0},{9,1... | collective-permute-start | bytes 786440 | tf_op jit(solution)/shard_map/ppermute | solution.py:42
  158.9 5.0 %all-to-all-done.4 = bf16[16,8,128]{2,1,0:T(8,128)(2,1)S(1)} async-done(((bf16[16,8,128]{2,1,0:T(8,128)(2,1)}), bf16[16,8,128]{2,1,0:T(8,128)(2,1)S(1)}, u32[]{:S(2)}, u32[]{:S(2)}) %all-to-all-start.4) | async-done | bytes 32800 | tf_op jit(solution)/shard_map/all_to_all | solution.py:31
  164.0 0.7 broadcast_in_dim.2
  164.7 0.0 copy-start
  164.7 11.8 %all-to-all-start.5 = ((bf16[8,16,8,128]{3,2,1,0:T(8,128)(2,1)}), bf16[8,16,8,128]{3,2,1,0:T(8,128)(2,1)S(1)}, u32[]{:S(2)}, u32[]{:S(2)}) async-start(bf16[8,16,8,128]{3,2,1,0:T(8,128)(2,1)} %broadcast_in_dim.2), calls=%async_computation.5 | async-start | bytes 524288 | tf_op jit(solution)/shard_map/all_to_all | solution.py:31
  176.5 0.0 collective-permute-done.4.refs_2_
  176.5 0.0 collective-permute-done.3.refs_1_
  176.5 0.0 collective-permute-done.8.refs_7_
  176.6 0.0 collective-permute-done.7.refs_6_
  176.6 0.0 collective-permute-done.6.refs_5_
  176.6 6.5 %all-to-all-done.5.attended_ref = bf16[8,16,8,128]{3,2,1,0:T(8,128)(2,1)S(1)} async-done(((bf16[8,16,8,128]{3,2,1,0:T(8,128)(2,1)}), bf16[8,16,8,128]{3,2,1,0:T(8,128)(2,1)S(1)}, u32[]{:S(2)}, u32[]{:S(2)}) %all-to-all-start.5) | async-done | bytes 262176 | tf_op jit(solution)/shard_map/all_to_all | solution.py:31
  183.0 0.0 copy-done
  183.0 2.0 %product.1 = bf16[64,512]{1,0:T(8,128)(2,1)} custom-call(s32[5]{0:T(128)S(1)} %stack.23.place_ref, bf16[8,16,8,128]{3,2,1,0:T(8,128)(2,1)S(1)} %all-to-all-done.5.attended_ref, bf16[2,8,64,128]{3,2,1,0:T(8,128)(2,1)S(1)} %get-tuple-element.13.refs_0_, bf16[2,8,64,128]{3,2,1,0:T(8,128)(2,1)S(1)} %collective-permute-done.3.refs_1_, ...), custom_call_target="tpu_custom_call" | custom-call | flops 134217728 | bytes 3145728 | tf_op jit(solution)/shard_map/product/pallas_call | solution.py:269
  (2 shorter events, 0.0 us)
Async XLA Ops:
  1.4 22.4 %all-to-all-start = ((bf16[8,24,256]{2,1,0:T(8,128)(2,1)}), bf16[8,24,256]{2,1,0:T(8,128)(2,1)S(1)}, u32[]{:S(2)}, u32[]{:S(2)}) async-start(bf16[8,24,256]{2,1,0:T(8,128)(2,1)} %pad_maximum_fusion), calls=%async_computation | async-start | bytes 196608 | tf_op jit(solution)/shard_map/all_to_all | solution.py:31
  18.8 5.0 %copy-start.1 = (bf16[256,32]{0,1:T(8,128)(2,1)S(1)}, bf16[256,32]{0,1:T(8,128)(2,1)}, u32[]{:S(2)}) copy-start(bf16[256,32]{0,1:T(8,128)(2,1)} %param.10) | copy-start | bytes 49156
  18.8 0.7 copy-start.2
  65.3 37.8 %all-to-all-start.2 = ((bf16[8,336,128]{2,1,0:T(8,128)(2,1)}), bf16[8,336,128]{2,1,0:T(8,128)(2,1)S(1)}, u32[]{:S(2)}, u32[]{:S(2)}) async-start(bf16[8,336,128]{2,1,0:T(8,128)(2,1)} %get-tuple-element.11), calls=%async_computation.2 | async-start | bytes 1376256 | tf_op jit(solution)/shard_map/all_to_all | solution.py:31
  108.3 21.0 %all-to-all-start.3 = ((f32[8,136,128]{2,1,0:T(8,128)}), f32[8,136,128]{2,1,0:T(8,128)S(1)}, u32[]{:S(2)}, u32[]{:S(2)}) async-start(f32[8,136,128]{2,1,0:T(8,128)} %attend.1), calls=%async_computation.3 | async-start | bytes 1114112 | tf_op jit(solution)/shard_map/all_to_all | solution.py:31
  113.2 11.8 %collective-permute-start.2 = (bf16[8,64,128]{2,1,0:T(8,128)(2,1)S(1)}, bf16[8,64,128]{2,1,0:T(8,128)(2,1)S(1)}, u32[]{:S(2)}, u32[]{:S(2)}) collective-permute-start(bf16[8,64,128]{2,1,0:T(8,128)(2,1)S(1)} %slice.4), channel_id=1, source_target_pairs={{0,96},{1,97},{2,98},{3,99},{4,100},{5,101},{6,102},{7,103},{8,104... | collective-permute-start | bytes 393224 | tf_op jit(solution)/shard_map/ppermute | solution.py:42
  120.9 7.8 %collective-permute-start.1 = (bf16[8,64,128]{2,1,0:T(8,128)(2,1)S(1)}, bf16[8,64,128]{2,1,0:T(8,128)(2,1)S(1)}, u32[]{:S(2)}, u32[]{:S(2)}) collective-permute-start(bf16[8,64,128]{2,1,0:T(8,128)(2,1)S(1)} %slice.4), channel_id=1, source_target_pairs={{0,64},{1,65},{2,66},{3,67},{4,68},{5,69},{6,70},{7,71},{8,72},{9,... | collective-permute-start | bytes 393224 | tf_op jit(solution)/shard_map/ppermute | solution.py:42
  122.8 6.5 %collective-permute-start = (bf16[8,64,128]{2,1,0:T(8,128)(2,1)S(1)}, bf16[8,64,128]{2,1,0:T(8,128)(2,1)S(1)}, u32[]{:S(2)}, u32[]{:S(2)}) collective-permute-start(bf16[8,64,128]{2,1,0:T(8,128)(2,1)S(1)} %slice.4), channel_id=1, source_target_pairs={{0,32},{1,33},{2,34},{3,35},{4,36},{5,37},{6,38},{7,39},{8,40},{9,... | collective-permute-start | bytes 393224 | tf_op jit(solution)/shard_map/ppermute | solution.py:42
  130.2 25.1 %collective-permute-start.5 = (bf16[2,8,64,128]{3,2,1,0:T(8,128)(2,1)S(1)}, bf16[2,8,64,128]{3,2,1,0:T(8,128)(2,1)S(1)}, u32[]{:S(2)}, u32[]{:S(2)}) collective-permute-start(bf16[2,8,64,128]{3,2,1,0:T(8,128)(2,1)S(1)} %get-tuple-element.13.refs_0_), channel_id=1, source_target_pairs={{0,8},{1,9},{2,10},{3,11},{4,12},{5,13},{6,14},{7,15},{8,16},{9,17... | collective-permute-start | bytes 786440 | tf_op jit(solution)/shard_map/ppermute | solution.py:42
  133.4 30.6 %all-to-all-start.4 = ((bf16[16,8,128]{2,1,0:T(8,128)(2,1)}), bf16[16,8,128]{2,1,0:T(8,128)(2,1)S(1)}, u32[]{:S(2)}, u32[]{:S(2)}) async-start(bf16[16,8,128]{2,1,0:T(8,128)(2,1)} %bitcast.11), calls=%async_computation.4 | async-start | bytes 65536 | tf_op jit(solution)/shard_map/all_to_all | solution.py:31
  142.9 33.7 %collective-permute-start.4 = (bf16[2,8,64,128]{3,2,1,0:T(8,128)(2,1)S(1)}, bf16[2,8,64,128]{3,2,1,0:T(8,128)(2,1)S(1)}, u32[]{:S(2)}, u32[]{:S(2)}) collective-permute-start(bf16[2,8,64,128]{3,2,1,0:T(8,128)(2,1)S(1)} %get-tuple-element.13.refs_0_), channel_id=1, source_target_pairs={{0,16},{1,17},{2,18},{3,19},{4,20},{5,21},{6,22},{7,23},{8,24},{9,... | collective-permute-start | bytes 786440 | tf_op jit(solution)/shard_map/ppermute | solution.py:42
  147.2 29.4 %collective-permute-start.3 = (bf16[2,8,64,128]{3,2,1,0:T(8,128)(2,1)S(1)}, bf16[2,8,64,128]{3,2,1,0:T(8,128)(2,1)S(1)}, u32[]{:S(2)}, u32[]{:S(2)}) collective-permute-start(bf16[2,8,64,128]{3,2,1,0:T(8,128)(2,1)S(1)} %get-tuple-element.13.refs_0_), channel_id=1, source_target_pairs={{0,24},{1,25},{2,26},{3,27},{4,28},{5,29},{6,30},{7,31},{8,0},{9,1... | collective-permute-start | bytes 786440 | tf_op jit(solution)/shard_map/ppermute | solution.py:42
  150.3 26.3 %collective-permute-start.8 = (bf16[2,8,64,128]{3,2,1,0:T(8,128)(2,1)S(1)}, bf16[2,8,64,128]{3,2,1,0:T(8,128)(2,1)S(1)}, u32[]{:S(2)}, u32[]{:S(2)}) collective-permute-start(bf16[2,8,64,128]{3,2,1,0:T(8,128)(2,1)S(1)} %get-tuple-element.14.refs_4_), channel_id=1, source_target_pairs={{0,8},{1,9},{2,10},{3,11},{4,12},{5,13},{6,14},{7,15},{8,16},{9,17... | collective-permute-start | bytes 786440 | tf_op jit(solution)/shard_map/ppermute | solution.py:42
  152.5 24.1 %collective-permute-start.7 = (bf16[2,8,64,128]{3,2,1,0:T(8,128)(2,1)S(1)}, bf16[2,8,64,128]{3,2,1,0:T(8,128)(2,1)S(1)}, u32[]{:S(2)}, u32[]{:S(2)}) collective-permute-start(bf16[2,8,64,128]{3,2,1,0:T(8,128)(2,1)S(1)} %get-tuple-element.14.refs_4_), channel_id=1, source_target_pairs={{0,16},{1,17},{2,18},{3,19},{4,20},{5,21},{6,22},{7,23},{8,24},{9,... | collective-permute-start | bytes 786440 | tf_op jit(solution)/shard_map/ppermute | solution.py:42
  155.3 21.3 %collective-permute-start.6 = (bf16[2,8,64,128]{3,2,1,0:T(8,128)(2,1)S(1)}, bf16[2,8,64,128]{3,2,1,0:T(8,128)(2,1)S(1)}, u32[]{:S(2)}, u32[]{:S(2)}) collective-permute-start(bf16[2,8,64,128]{3,2,1,0:T(8,128)(2,1)S(1)} %get-tuple-element.14.refs_4_), channel_id=1, source_target_pairs={{0,24},{1,25},{2,26},{3,27},{4,28},{5,29},{6,30},{7,31},{8,0},{9,1... | collective-permute-start | bytes 786440 | tf_op jit(solution)/shard_map/ppermute | solution.py:42
  164.7 18.3 %copy-start = (bf16[64,512]{1,0:T(8,128)(2,1)S(1)}, bf16[64,512]{1,0:T(8,128)(2,1)}, u32[]{:S(2)}) copy-start(bf16[64,512]{1,0:T(8,128)(2,1)} %refs_8_.1) | copy-start | bytes 196612
  164.7 18.3 %all-to-all-start.5 = ((bf16[8,16,8,128]{3,2,1,0:T(8,128)(2,1)}), bf16[8,16,8,128]{3,2,1,0:T(8,128)(2,1)S(1)}, u32[]{:S(2)}, u32[]{:S(2)}) async-start(bf16[8,16,8,128]{3,2,1,0:T(8,128)(2,1)} %broadcast_in_dim.2), calls=%async_computation.5 | async-start | bytes 524288 | tf_op jit(solution)/shard_map/all_to_all | solution.py:31

commit v6 on v5

--- a/solution.py
+++ b/solution.py
@@ -21,7 +21,8 @@
 SEQ_AXES = ("zh", "zp", "z2", "y")
 HEAD_AXES = ("x", "c")
 PLANES = ("zh", "zp")
-QUERY_AXES = ("z2", "y")
+KEY_AXES = ("z2", "x", "c")
+QUERY_AXES = ("y",)
 
 VMEM = pl.BlockSpec(memory_space=pltpu.VMEM)
 SMEM = pl.BlockSpec(memory_space=pltpu.SMEM)
@@ -106,7 +107,7 @@
         key_ref[s, DOCS_AT:COLUMNS_AT, :] = docs
         for k in range(2):
             at = COLUMNS_AT + k * COLUMNS
-            key_ref[s, at : at + COLUMNS, :] = came_ref[2 * s + k, WEIGHT_AT:SENT, :]
+            key_ref[s, at : at + COLUMNS, :] = came_ref[2 * (s % 8) + k, WEIGHT_AT:SENT, :]
 
 
 def attend_kernel(place_ref, query_ref, key_ref, out_ref, score_ref):
@@ -122,7 +123,7 @@
     for r in range(query_ref.shape[0]):
         queries = query_ref[r, 0:ROWS, :]
         query_docs = transposed(query_ref[r, ROWS : ROWS + 16, :].astype(jnp.float32)[0:1])
-        query_pos = positions(r // 4, r % 4, x, c, 0)
+        query_pos = positions(z2, r, x, c, 0)
         highest = jnp.full((ROWS, LANES), HIDDEN, jnp.float32)
         for s in range(sources):
             scores = lax.dot_general(
@@ -132,7 +133,7 @@
                 preferred_element_type=jnp.float32,
             )
             key_docs = key_ref[s, DOCS_AT:COLUMNS_AT, :].astype(jnp.float32)[0:1]
-            key_pos = positions(z2, y, s // 2, s % 2, 1)
+            key_pos = positions(s // 8, y, s % 8 // 2, s % 2, 1)
             visible = (key_pos <= query_pos) & (key_docs == query_docs)
             scores = jnp.where(visible, scores, HIDDEN)
             score_ref[s] = scores
@@ -154,11 +155,13 @@
         out_ref[r, ROWS : ROWS + 8, :] = jnp.concatenate([row_max.T[0:4], row_sum.T[0:4]], axis=0)
 
 
-def combine_kernel(part_ref, key_ref, by_z1, by_z2, by_z3, out_ref, own_ref, other_ref):
-    own_ref[0] = key_ref[:, COLUMNS_AT:GATHERED, :]
-    own_ref[1] = by_z2[...]
-    other_ref[0] = by_z1[...]
-    other_ref[1] = by_z3[...]
+def columns_kernel(key_ref, after_ref, out_ref):
+    out_ref[...] = key_ref[:, COLUMNS_AT:GATHERED, :]
+
+
+def combine_kernel(part_ref, own_ref, other_ref, out_ref, same_own_ref, same_other_ref):
+    same_own_ref[...] = own_ref[...]
+    same_other_ref[...] = other_ref[...]
     parts = part_ref.shape[0]
     maxima = [part_ref[r, ROWS : ROWS + 1, :] for r in range(parts)]
     sums = [part_ref[r, ROWS + 4 : ROWS + 5, :] for r in range(parts)]
@@ -175,43 +178,41 @@
 
 def product_kernel(place_ref, attended_ref, *refs):
     weights, (residual_ref, out_ref) = refs[:8], refs[8:]
-    z2, y, zp = place_ref[0], place_ref[1], place_ref[4]
+    y, zp = place_ref[1], place_ref[4]
+    groups = attended_ref.shape[0]
     total = jnp.zeros(out_ref.shape, jnp.float32)
-    for p in range(attended_ref.shape[0]):
+    for p in range(groups):
         heads = [
-            attended_ref[:, 2 * p + j].astype(jnp.float32).reshape(BLOCK, HEAD_DIM)
+            attended_ref[:, 2 * p + (zp ^ j)].astype(jnp.float32).reshape(BLOCK, HEAD_DIM)
             for j in range(2)
         ]
         left = jnp.concatenate(heads, axis=1).astype(jnp.bfloat16)
         blocks = []
         for k in range(2):
             rows = slice(k * COLUMNS, (k + 1) * COLUMNS)
-            for w in weights:
-                halves = [w[zp ^ j, p, rows, :] for j in range(2)]
-                blocks.append(jnp.concatenate(halves, axis=1))
+            for z2 in range(2):
+                for own, other in zip(weights[:4], weights[4:]):
+                    halves = [w[z2 * groups + p, rows, :] for w in (own, other)]
+                    blocks.append(jnp.concatenate(halves, axis=1))
         total = total + lax.dot_general(
             left,
             jnp.concatenate(blocks, axis=0),
             (((1,), (1,)), ((), ())),
             preferred_element_type=jnp.float32,
         )
-    for k in range(2):
-        own, other = (
-            pltpu.roll(total[:, at : at + LANES], y * COLUMNS, 1)
-            for at in (2 * k * LANES, (2 * k + 1) * LANES)
+    for zl in range(4):
+        columns = slice(zl * LANES, (zl + 1) * LANES)
+        summed = pltpu.roll(total[:, columns], y * COLUMNS, 1)
+        out_ref[:, columns] = (residual_ref[:, columns].astype(jnp.float32) + summed).astype(
+            out_ref.dtype
         )
-        for j in range(2):
-            columns = slice((2 * k + j) * LANES, (2 * k + j + 1) * LANES)
-            summed = jnp.where(z2 == j, own, other)
-            out_ref[:, columns] = (residual_ref[:, columns].astype(jnp.float32) + summed).astype(
-                out_ref.dtype
-            )
 
 
 def shards(query, key_states, value_states, doc_ids, out_weight, residual):
     groups = lax.axis_size(HEAD_AXES)
     planes = lax.axis_size(PLANES)
     spread = lax.axis_size(QUERY_AXES)
+    sources = lax.axis_size(KEY_AXES)
     bf16, f32 = jnp.bfloat16, jnp.float32
     index = [lax.axis_index(a) for a in ("z2", "y", "x", "c", "zp")]
     place = jnp.stack(index)
@@ -229,12 +230,12 @@
         gather_kernel,
         [
             jax.ShapeDtypeStruct((ROWS + 16, LANES), bf16),
-            jax.ShapeDtypeStruct((groups, GATHERED, LANES), bf16),
+            jax.ShapeDtypeStruct((sources, GATHERED, LANES), bf16),
         ],
         [VMEM],
         "spread",
     )(came)
-    keys = exchange(keys, HEAD_AXES)
+    keys = exchange(keys, KEY_AXES)
     queries = lax.all_gather(queries, QUERY_AXES)
 
     parts = call(
@@ -242,26 +243,28 @@
         jax.ShapeDtypeStruct((spread, ROWS + 8, LANES), f32),
         [SMEM] + [VMEM] * 2,
         "attend",
-        [pltpu.VMEM((groups, ROWS, LANES), f32)],
-        4 * spread * ROWS * groups * ROWS * HEAD_DIM,
+        [pltpu.VMEM((sources, ROWS, LANES), f32)],
+        4 * spread * ROWS * sources * ROWS * HEAD_DIM,
         2 << 20,
     )(place, queries, keys)
     parts = exchange(parts, QUERY_AXES)
 
-    columns = keys[:, COLUMNS_AT:]
-    near = [moved(columns, lambda z, y, x, c: (z ^ far, y, x, c)) for far in (1, 2, 3)]
-    held = jax.ShapeDtypeStruct((2, *columns.shape), bf16)
+    def from_y(block, k):
+        return moved(block, lambda z, y, x, c: (z, (y - k) % 4, x, c))
+
+    held = jax.ShapeDtypeStruct((sources, GATHERED - COLUMNS_AT, LANES), bf16)
+    own = call(columns_kernel, held, [VMEM, pl.BlockSpec(memory_space=pl.ANY)], "columns")(
+        keys, queries
+    )
+    other = moved(own, lambda z, y, x, c: (z ^ 2, y, x, c))
+    far = from_y(own, 2)
     attended, own, other = call(
         combine_kernel,
         [jax.ShapeDtypeStruct((ROWS, HEAD_DIM), bf16), held, held],
-        [VMEM] * 5,
+        [VMEM] * 3,
         "combine",
-    )(parts, keys, *near)
-
-    def from_y(block, k):
-        return moved(block, lambda z, y, x, c: (z, (y - k) % 4, x, c))
-
-    weights = [own] + [from_y(own, k) for k in (1, 2, 3)]
+    )(parts, own, other)
+    weights = [own, from_y(own, 1), far, from_y(own, 3)]
     weights += [other] + [from_y(other, k) for k in (1, 2, 3)]
 
     back = exchange(attended.reshape(planes, EACH, HEAD_DIM), PLANES)

time: 186 us -> 170 us (0.914)
  blocking collectives: 67.9 us -> 51 us
  waiting for transfers between devices: 19.9 us -> 26.4 us
  starting transfers between devices: 84.8 us -> 79.2 us
    all_gather x1, blocking collectives: 27.5 us -> 10.6 us  [shards(): queries = lax.all_gather(queries, QUERY_AXES)]
    all_to_all x5, waiting for transfers between devices: 15.6 us -> 26.3 us  [exchange(): return lax.all_to_all(tiles, axes, split_axis=0, concat_axis=0, tiled=True)]
    ppermute x9 -> x7, waiting for transfers between devices: 4.3 us -> 0.02 us  [moved(): lax.ppermute(block, names, [(flat(*p), flat(*where(*p))) for p in places])]
    ppermute x9 -> x7, starting transfers between devices: 31 us -> 27.4 us  [moved(): lax.ppermute(block, names, [(flat(*p), flat(*where(*p))) for p in places])]
    all_to_all x5, starting transfers between devices: 53.8 us -> 51.8 us  [exchange(): return lax.all_to_all(tiles, axes, split_axis=0, concat_axis=0, tiled=True)]
  transfers between devices with their start and end apart: 14 -> 12, of which waited for: 5 -> 5; matrix products, arithmetic and copies ran while one was open for 1% -> 1% of each run, Pallas kernels for 0% -> 3%
where the time goes in v6:
time: 170 us; the launch traced here: 169 us
  starting transfers between devices  79.2 us (47%)
  blocking collectives  51 us (30%)
  waiting for transfers between devices  26.4 us (16%)
  Pallas kernels  8.52 us (5%)
  other arithmetic  2.4 us (1%)
    all_to_all x5, starting transfers between devices, exchange(): return lax.all_to_all(tiles, axes, split_axis=0, concat_axis=0, tiled=True)  51.8 us
    all_to_all x1, blocking collectives, exchange(): return lax.all_to_all(tiles, axes, split_axis=0, concat_axis=0, tiled=True)  40.5 us
    ppermute x7, starting transfers between devices, moved(): lax.ppermute(block, names, [(flat(*p), flat(*where(*p))) for p in places])  27.4 us
    all_to_all x5, waiting for transfers between devices, exchange(): return lax.all_to_all(tiles, axes, split_axis=0, concat_axis=0, tiled=True)  26.3 us
    all_gather x1, blocking collectives, shards(): queries = lax.all_gather(queries, QUERY_AXES)  10.6 us
    pallas_call x1, Pallas kernels, shards(): call(attend_kernel, jax.ShapeDtypeStruct((spread, ROWS + 8, LANES), f32),...  4.42 us
  transfers between devices with their start and end apart: 12, of which 5 were waited for; matrix products, arithmetic and copies ran while one was open for 1% of the time, Pallas kernels for 3%

profile of v6, /device:TPU:1, one launch (start us, length us, event | category | flops | bytes accessed | tf_op | source)
XLA Modules:
  0.0 169.1 jit_solution(7036282719775676550)
XLA Ops:
  0.0 1.4 pad_maximum_fusion
  1.4 17.4 %all-to-all-start = ((bf16[8,24,256]{2,1,0:T(8,128)(2,1)}), bf16[8,24,256]{2,1,0:T(8,128)(2,1)S(1)}, u32[]{:S(2)}, u32[]{:S(2)}) async-start(bf16[8,24,256]{2,1,0:T(8,128)(2,1)} %pad_maximum_fusion), calls=%async_computation | async-start | bytes 196608 | tf_op jit(solution)/shard_map/all_to_all | solution.py:32
  18.9 0.8 pad_add_fusion
  19.7 0.1 convert_bitcast_fusion
  19.7 0.1 pad_maximum_fusion.1.docs_ref
  19.8 4.0 %all-to-all-done.rows_ref = bf16[8,24,256]{2,1,0:T(8,128)(2,1)S(1)} async-done(((bf16[8,24,256]{2,1,0:T(8,128)(2,1)}), bf16[8,24,256]{2,1,0:T(8,128)(2,1)S(1)}, u32[]{:S(2)}, u32[]{:S(2)}) %all-to-all-start) | async-done | bytes 98336 | tf_op jit(solution)/shard_map/all_to_all | solution.py:32
  23.9 0.0 copy-start.1
  23.9 0.7 copy-done.1
  24.6 40.5 %all_to_all.30.came_ref = bf16[16,64,128]{2,1,0:T(8,128)(2,1)S(1)} all-to-all(bf16[16,64,128]{2,1,0:T(8,128)(2,1)S(1)} %send.1), channel_id=1, replica_groups=mesh['zh'=8,'zp'=2,'z2'=2,'y'=4,'x'=4,'c'=2] {'zh','zp'}, dimensions={0} | all-to-all | bytes 524288 | tf_op jit(solution)/shard_map/all_to_all | solution.py:32
  65.1 1.3 spread.1
  66.3 14.6 %all-to-all-start.2 = ((bf16[16,336,128]{2,1,0:T(8,128)(2,1)}), bf16[16,336,128]{2,1,0:T(8,128)(2,1)S(1)}, u32[]{:S(2)}, u32[]{:S(2)}) async-start(bf16[16,336,128]{2,1,0:T(8,128)(2,1)} %get-tuple-element.11), calls=%async_computation.2 | async-start | bytes 2752512 | tf_op jit(solution)/shard_map/all_to_all | solution.py:32
  80.9 10.6 %all-gather = bf16[576,128]{1,0:T(8,128)(2,1)S(1)} all-gather(bf16[144,128]{1,0:T(8,128)(2,1)S(1)} %get-tuple-element.10), channel_id=2, replica_groups=mesh['zh'=8,'zp'=2,'z2'=2,'y'=4,'x'=4,'c'=2] {'y'}, dimensions={0}, use_global_device_ids=true | all-gather | bytes 184320 | tf_op jit(solution)/shard_map/all_gather | solution.py:239
  91.5 8.9 %all-to-all-done.2.key_ref = bf16[16,336,128]{2,1,0:T(8,128)(2,1)S(1)} async-done(((bf16[16,336,128]{2,1,0:T(8,128)(2,1)}), bf16[16,336,128]{2,1,0:T(8,128)(2,1)S(1)}, u32[]{:S(2)}, u32[]{:S(2)}) %all-to-all-start.2) | async-done | bytes 1376288 | tf_op jit(solution)/shard_map/all_to_all | solution.py:32
  100.4 7.6 %collective-permute-start = (bf16[16,64,128]{2,1,0:T(8,128)(2,1)S(1)}, bf16[16,64,128]{2,1,0:T(8,128)(2,1)S(1)}, u32[]{:S(2)}, u32[]{:S(2)}) collective-permute-start(bf16[16,64,128]{2,1,0:T(8,128)(2,1)S(1)} %columns.1.own_ref), channel_id=1, source_target_pairs={{0,64},{1,65},{2,66},{3,67},{4,68},{5,69},{6,70},{7,71},{8,72},{9,... | collective-permute-start | bytes 786440 | tf_op jit(solution)/shard_map/ppermute | solution.py:43
  108.0 0.1 stack.23.place_ref
  108.1 4.4 %attend.1 = f32[4,136,128]{2,1,0:T(8,128)} custom-call(s32[5]{0:T(128)S(1)} %stack.23.place_ref, bf16[4,144,128]{2,1,0:T(8,128)(2,1)S(1)} %bitcast.14, bf16[16,336,128]{2,1,0:T(8,128)(2,1)S(1)} %all-to-all-done.2.key_ref), custom_call_target="tpu_custom_call" | custom-call | flops 536870912 | bytes 2097152 | tf_op jit(solution)/shard_map/attend/pallas_call | solution.py:241
  112.5 0.0 copy-start
  112.5 4.3 %all-to-all-start.3 = ((f32[4,136,128]{2,1,0:T(8,128)}), f32[4,136,128]{2,1,0:T(8,128)S(1)}, u32[]{:S(2)}, u32[]{:S(2)}) async-start(f32[4,136,128]{2,1,0:T(8,128)} %attend.1), calls=%async_computation.3 | async-start | bytes 557056 | tf_op jit(solution)/shard_map/all_to_all | solution.py:32
  116.8 4.9 %collective-permute-start.2 = (bf16[16,64,128]{2,1,0:T(8,128)(2,1)S(1)}, bf16[16,64,128]{2,1,0:T(8,128)(2,1)S(1)}, u32[]{:S(2)}, u32[]{:S(2)}) collective-permute-start(bf16[16,64,128]{2,1,0:T(8,128)(2,1)S(1)} %columns.1.own_ref), channel_id=1, source_target_pairs={{0,16},{1,17},{2,18},{3,19},{4,20},{5,21},{6,22},{7,23},{8,24},{9,... | collective-permute-start | bytes 786440 | tf_op jit(solution)/shard_map/ppermute | solution.py:43
  121.7 0.7 all-to-all-done.3.part_ref
  122.4 0.0 collective-permute-done.other_ref
  122.4 0.8 combine.1
  123.2 6.6 %all-to-all-start.4 = ((bf16[16,8,128]{2,1,0:T(8,128)(2,1)}), bf16[16,8,128]{2,1,0:T(8,128)(2,1)S(1)}, u32[]{:S(2)}, u32[]{:S(2)}) async-start(bf16[16,8,128]{2,1,0:T(8,128)(2,1)} %bitcast.11), calls=%async_computation.4 | async-start | bytes 65536 | tf_op jit(solution)/shard_map/all_to_all | solution.py:32
  129.8 2.2 %collective-permute-start.3 = (bf16[16,64,128]{2,1,0:T(8,128)(2,1)S(1)}, bf16[16,64,128]{2,1,0:T(8,128)(2,1)S(1)}, u32[]{:S(2)}, u32[]{:S(2)}) collective-permute-start(bf16[16,64,128]{2,1,0:T(8,128)(2,1)S(1)} %get-tuple-element.13.refs_0_), channel_id=1, source_target_pairs={{0,8},{1,9},{2,10},{3,11},{4,12},{5,13},{6,14},{7,15},{8,16},{9,17... | collective-permute-start | bytes 786440 | tf_op jit(solution)/shard_map/ppermute | solution.py:43
  132.0 4.3 %collective-permute-start.1 = (bf16[16,64,128]{2,1,0:T(8,128)(2,1)S(1)}, bf16[16,64,128]{2,1,0:T(8,128)(2,1)S(1)}, u32[]{:S(2)}, u32[]{:S(2)}) collective-permute-start(bf16[16,64,128]{2,1,0:T(8,128)(2,1)S(1)} %get-tuple-element.13.refs_0_), channel_id=1, source_target_pairs={{0,24},{1,25},{2,26},{3,27},{4,28},{5,29},{6,30},{7,31},{8,0},{9,1... | collective-permute-start | bytes 786440 | tf_op jit(solution)/shard_map/ppermute | solution.py:43
  136.3 1.9 %collective-permute-start.6 = (bf16[16,64,128]{2,1,0:T(8,128)(2,1)S(1)}, bf16[16,64,128]{2,1,0:T(8,128)(2,1)S(1)}, u32[]{:S(2)}, u32[]{:S(2)}) collective-permute-start(bf16[16,64,128]{2,1,0:T(8,128)(2,1)S(1)} %get-tuple-element.14.refs_4_), channel_id=1, source_target_pairs={{0,8},{1,9},{2,10},{3,11},{4,12},{5,13},{6,14},{7,15},{8,16},{9,17... | collective-permute-start | bytes 786440 | tf_op jit(solution)/shard_map/ppermute | solution.py:43
  138.3 3.1 %collective-permute-start.5 = (bf16[16,64,128]{2,1,0:T(8,128)(2,1)S(1)}, bf16[16,64,128]{2,1,0:T(8,128)(2,1)S(1)}, u32[]{:S(2)}, u32[]{:S(2)}) collective-permute-start(bf16[16,64,128]{2,1,0:T(8,128)(2,1)S(1)} %get-tuple-element.14.refs_4_), channel_id=1, source_target_pairs={{0,16},{1,17},{2,18},{3,19},{4,20},{5,21},{6,22},{7,23},{8,24},{9,... | collective-permute-start | bytes 786440 | tf_op jit(solution)/shard_map/ppermute | solution.py:43
  141.4 0.0 collective-permute-done.2.refs_2_
  141.4 3.4 %collective-permute-start.4 = (bf16[16,64,128]{2,1,0:T(8,128)(2,1)S(1)}, bf16[16,64,128]{2,1,0:T(8,128)(2,1)S(1)}, u32[]{:S(2)}, u32[]{:S(2)}) collective-permute-start(bf16[16,64,128]{2,1,0:T(8,128)(2,1)S(1)} %get-tuple-element.14.refs_4_), channel_id=1, source_target_pairs={{0,24},{1,25},{2,26},{3,27},{4,28},{5,29},{6,30},{7,31},{8,0},{9,1... | collective-permute-start | bytes 786440 | tf_op jit(solution)/shard_map/ppermute | solution.py:43
  144.8 6.2 %all-to-all-done.4 = bf16[16,8,128]{2,1,0:T(8,128)(2,1)S(1)} async-done(((bf16[16,8,128]{2,1,0:T(8,128)(2,1)}), bf16[16,8,128]{2,1,0:T(8,128)(2,1)S(1)}, u32[]{:S(2)}, u32[]{:S(2)}) %all-to-all-start.4) | async-done | bytes 32800 | tf_op jit(solution)/shard_map/all_to_all | solution.py:32
  151.0 0.7 broadcast_in_dim.2
  151.7 8.9 %all-to-all-start.5 = ((bf16[8,16,8,128]{3,2,1,0:T(8,128)(2,1)}), bf16[8,16,8,128]{3,2,1,0:T(8,128)(2,1)S(1)}, u32[]{:S(2)}, u32[]{:S(2)}) async-start(bf16[8,16,8,128]{3,2,1,0:T(8,128)(2,1)} %broadcast_in_dim.2), calls=%async_computation.5 | async-start | bytes 524288 | tf_op jit(solution)/shard_map/all_to_all | solution.py:32
  160.6 0.0 collective-permute-done.3.refs_3_
  160.6 0.0 collective-permute-done.1.refs_1_
  160.6 0.0 collective-permute-done.6.refs_7_
  160.6 0.0 collective-permute-done.5.refs_6_
  160.6 0.0 collective-permute-done.4.refs_5_
  160.6 6.5 %all-to-all-done.5.attended_ref = bf16[8,16,8,128]{3,2,1,0:T(8,128)(2,1)S(1)} async-done(((bf16[8,16,8,128]{3,2,1,0:T(8,128)(2,1)}), bf16[8,16,8,128]{3,2,1,0:T(8,128)(2,1)S(1)}, u32[]{:S(2)}, u32[]{:S(2)}) %all-to-all-start.5) | async-done | bytes 262176 | tf_op jit(solution)/shard_map/all_to_all | solution.py:32
  167.1 0.0 copy-done
  167.1 2.0 %product.1 = bf16[64,512]{1,0:T(8,128)(2,1)} custom-call(s32[5]{0:T(128)S(1)} %stack.23.place_ref, bf16[8,16,8,128]{3,2,1,0:T(8,128)(2,1)S(1)} %all-to-all-done.5.attended_ref, bf16[16,64,128]{2,1,0:T(8,128)(2,1)S(1)} %get-tuple-element.13.refs_0_, bf16[16,64,128]{2,1,0:T(8,128)(2,1)S(1)} %collective-permute-done.1.refs_1_, ...), custom_call_target="tpu_custom_call" | custom-call | flops 134217728 | bytes 3145728 | tf_op jit(solution)/shard_map/product/pallas_call | solution.py:272
  (2 shorter events, 0.0 us)
Async XLA Ops:
  1.4 22.4 %all-to-all-start = ((bf16[8,24,256]{2,1,0:T(8,128)(2,1)}), bf16[8,24,256]{2,1,0:T(8,128)(2,1)S(1)}, u32[]{:S(2)}, u32[]{:S(2)}) async-start(bf16[8,24,256]{2,1,0:T(8,128)(2,1)} %pad_maximum_fusion), calls=%async_computation | async-start | bytes 196608 | tf_op jit(solution)/shard_map/all_to_all | solution.py:32
  23.9 0.7 copy-start.1
  66.3 34.0 %all-to-all-start.2 = ((bf16[16,336,128]{2,1,0:T(8,128)(2,1)}), bf16[16,336,128]{2,1,0:T(8,128)(2,1)S(1)}, u32[]{:S(2)}, u32[]{:S(2)}) async-start(bf16[16,336,128]{2,1,0:T(8,128)(2,1)} %get-tuple-element.11), calls=%async_computation.2 | async-start | bytes 2752512 | tf_op jit(solution)/shard_map/all_to_all | solution.py:32
  100.4 22.0 %collective-permute-start = (bf16[16,64,128]{2,1,0:T(8,128)(2,1)S(1)}, bf16[16,64,128]{2,1,0:T(8,128)(2,1)S(1)}, u32[]{:S(2)}, u32[]{:S(2)}) collective-permute-start(bf16[16,64,128]{2,1,0:T(8,128)(2,1)S(1)} %columns.1.own_ref), channel_id=1, source_target_pairs={{0,64},{1,65},{2,66},{3,67},{4,68},{5,69},{6,70},{7,71},{8,72},{9,... | collective-permute-start | bytes 786440 | tf_op jit(solution)/shard_map/ppermute | solution.py:43
  112.5 54.6 %copy-start = (bf16[64,512]{1,0:T(8,128)(2,1)S(1)}, bf16[64,512]{1,0:T(8,128)(2,1)}, u32[]{:S(2)}) copy-start(bf16[64,512]{1,0:T(8,128)(2,1)} %refs_8_.1) | copy-start | bytes 196612
  112.5 9.9 %all-to-all-start.3 = ((f32[4,136,128]{2,1,0:T(8,128)}), f32[4,136,128]{2,1,0:T(8,128)S(1)}, u32[]{:S(2)}, u32[]{:S(2)}) async-start(f32[4,136,128]{2,1,0:T(8,128)} %attend.1), calls=%async_computation.3 | async-start | bytes 557056 | tf_op jit(solution)/shard_map/all_to_all | solution.py:32
  116.8 24.6 %collective-permute-start.2 = (bf16[16,64,128]{2,1,0:T(8,128)(2,1)S(1)}, bf16[16,64,128]{2,1,0:T(8,128)(2,1)S(1)}, u32[]{:S(2)}, u32[]{:S(2)}) collective-permute-start(bf16[16,64,128]{2,1,0:T(8,128)(2,1)S(1)} %columns.1.own_ref), channel_id=1, source_target_pairs={{0,16},{1,17},{2,18},{3,19},{4,20},{5,21},{6,22},{7,23},{8,24},{9,... | collective-permute-start | bytes 786440 | tf_op jit(solution)/shard_map/ppermute | solution.py:43
  123.2 27.8 %all-to-all-start.4 = ((bf16[16,8,128]{2,1,0:T(8,128)(2,1)}), bf16[16,8,128]{2,1,0:T(8,128)(2,1)S(1)}, u32[]{:S(2)}, u32[]{:S(2)}) async-start(bf16[16,8,128]{2,1,0:T(8,128)(2,1)} %bitcast.11), calls=%async_computation.4 | async-start | bytes 65536 | tf_op jit(solution)/shard_map/all_to_all | solution.py:32
  129.8 30.8 %collective-permute-start.3 = (bf16[16,64,128]{2,1,0:T(8,128)(2,1)S(1)}, bf16[16,64,128]{2,1,0:T(8,128)(2,1)S(1)}, u32[]{:S(2)}, u32[]{:S(2)}) collective-permute-start(bf16[16,64,128]{2,1,0:T(8,128)(2,1)S(1)} %get-tuple-element.13.refs_0_), channel_id=1, source_target_pairs={{0,8},{1,9},{2,10},{3,11},{4,12},{5,13},{6,14},{7,15},{8,16},{9,17... | collective-permute-start | bytes 786440 | tf_op jit(solution)/shard_map/ppermute | solution.py:43
  132.0 28.6 %collective-permute-start.1 = (bf16[16,64,128]{2,1,0:T(8,128)(2,1)S(1)}, bf16[16,64,128]{2,1,0:T(8,128)(2,1)S(1)}, u32[]{:S(2)}, u32[]{:S(2)}) collective-permute-start(bf16[16,64,128]{2,1,0:T(8,128)(2,1)S(1)} %get-tuple-element.13.refs_0_), channel_id=1, source_target_pairs={{0,24},{1,25},{2,26},{3,27},{4,28},{5,29},{6,30},{7,31},{8,0},{9,1... | collective-permute-start | bytes 786440 | tf_op jit(solution)/shard_map/ppermute | solution.py:43
  136.3 24.3 %collective-permute-start.6 = (bf16[16,64,128]{2,1,0:T(8,128)(2,1)S(1)}, bf16[16,64,128]{2,1,0:T(8,128)(2,1)S(1)}, u32[]{:S(2)}, u32[]{:S(2)}) collective-permute-start(bf16[16,64,128]{2,1,0:T(8,128)(2,1)S(1)} %get-tuple-element.14.refs_4_), channel_id=1, source_target_pairs={{0,8},{1,9},{2,10},{3,11},{4,12},{5,13},{6,14},{7,15},{8,16},{9,17... | collective-permute-start | bytes 786440 | tf_op jit(solution)/shard_map/ppermute | solution.py:43
  138.3 22.4 %collective-permute-start.5 = (bf16[16,64,128]{2,1,0:T(8,128)(2,1)S(1)}, bf16[16,64,128]{2,1,0:T(8,128)(2,1)S(1)}, u32[]{:S(2)}, u32[]{:S(2)}) collective-permute-start(bf16[16,64,128]{2,1,0:T(8,128)(2,1)S(1)} %get-tuple-element.14.refs_4_), channel_id=1, source_target_pairs={{0,16},{1,17},{2,18},{3,19},{4,20},{5,21},{6,22},{7,23},{8,24},{9,... | collective-permute-start | bytes 786440 | tf_op jit(solution)/shard_map/ppermute | solution.py:43
  141.4 19.3 %collective-permute-start.4 = (bf16[16,64,128]{2,1,0:T(8,128)(2,1)S(1)}, bf16[16,64,128]{2,1,0:T(8,128)(2,1)S(1)}, u32[]{:S(2)}, u32[]{:S(2)}) collective-permute-start(bf16[16,64,128]{2,1,0:T(8,128)(2,1)S(1)} %get-tuple-element.14.refs_4_), channel_id=1, source_target_pairs={{0,24},{1,25},{2,26},{3,27},{4,28},{5,29},{6,30},{7,31},{8,0},{9,1... | collective-permute-start | bytes 786440 | tf_op jit(solution)/shard_map/ppermute | solution.py:43
  151.7 15.4 %all-to-all-start.5 = ((bf16[8,16,8,128]{3,2,1,0:T(8,128)(2,1)}), bf16[8,16,8,128]{3,2,1,0:T(8,128)(2,1)S(1)}, u32[]{:S(2)}, u32[]{:S(2)}) async-start(bf16[8,16,8,128]{3,2,1,0:T(8,128)(2,1)} %broadcast_in_dim.2), calls=%async_computation.5 | async-start | bytes 524288 | tf_op jit(solution)/shard_map/all_to_all | solution.py:32

commit v7 on v6

--- a/solution.py
+++ b/solution.py
@@ -120,11 +120,23 @@
         return first + (index >> 3) * stripe + (index & 7)
 
     sources = key_ref.shape[0]
-    for r in range(query_ref.shape[0]):
-        queries = query_ref[r, 0:ROWS, :]
-        query_docs = transposed(query_ref[r, ROWS : ROWS + 16, :].astype(jnp.float32)[0:1])
-        query_pos = positions(z2, r, x, c, 0)
-        highest = jnp.full((ROWS, LANES), HIDDEN, jnp.float32)
+    key_docs = [
+        key_ref[s, DOCS_AT:COLUMNS_AT, :].astype(jnp.float32)[0:1] for s in range(sources)
+    ]
+    key_pos = [positions(s // 8, y, s % 8 // 2, s % 2, 1)[0:1] for s in range(sources)]
+    for first in range(0, query_ref.shape[0], 2):
+        pair = (first, first + 1)
+        queries = jnp.concatenate([query_ref[r, 0:ROWS, :] for r in pair], axis=0)
+        query_docs = jnp.concatenate(
+            [
+                transposed(query_ref[r, ROWS : ROWS + 16, :].astype(jnp.float32)[0:1])
+                for r in pair
+            ],
+            axis=0,
+        )
+        query_pos = jnp.concatenate([positions(z2, r, x, c, 0) for r in pair], axis=0)
+        shape = query_pos.shape
+        highest = jnp.full(shape, HIDDEN, jnp.float32)
         for s in range(sources):
             scores = lax.dot_general(
                 queries,
@@ -132,27 +144,33 @@
                 (((1,), (1,)), ((), ())),
                 preferred_element_type=jnp.float32,
             )
-            key_docs = key_ref[s, DOCS_AT:COLUMNS_AT, :].astype(jnp.float32)[0:1]
-            key_pos = positions(s // 8, y, s % 8 // 2, s % 2, 1)
-            visible = (key_pos <= query_pos) & (key_docs == query_docs)
+            visible = (key_pos[s] <= query_pos) & (key_docs[s] == query_docs)
             scores = jnp.where(visible, scores, HIDDEN)
             score_ref[s] = scores
             highest = jnp.maximum(highest, scores)
         row_max = jnp.maximum(jnp.max(highest, axis=1, keepdims=True), LOWEST)
-        row_max = jnp.broadcast_to(row_max, (ROWS, LANES))
-        total = jnp.zeros((ROWS, LANES), jnp.float32)
-        mixed = jnp.zeros((ROWS, HEAD_DIM), jnp.float32)
-        for s in range(sources):
-            weights = jnp.exp2((score_ref[s] - row_max) * FACTOR)
-            total = total + weights
+        row_max = jnp.broadcast_to(row_max, shape)
+        total = jnp.zeros(shape, jnp.float32)
+        mixed = jnp.zeros(shape, jnp.float32)
+        for s in range(0, sources, 2):
+            weights, values = [], []
+            for k in (s, s + 1):
+                weight = jnp.exp2((score_ref[k] - row_max) * FACTOR)
+                total = total + weight
+                weights.append(weight.astype(jnp.bfloat16))
+                values.append(key_ref[k, ROWS:DOCS_AT, :])
             mixed = mixed + jnp.dot(
-                weights.astype(jnp.bfloat16),
-                key_ref[s, ROWS:DOCS_AT, :],
+                jnp.concatenate(weights, axis=1),
+                jnp.concatenate(values, axis=0),
                 preferred_element_type=jnp.float32,
             )
-        row_sum = jnp.broadcast_to(jnp.sum(total, axis=1, keepdims=True), (ROWS, LANES))
-        out_ref[r, 0:ROWS, :] = mixed
-        out_ref[r, ROWS : ROWS + 8, :] = jnp.concatenate([row_max.T[0:4], row_sum.T[0:4]], axis=0)
+        row_sum = jnp.broadcast_to(jnp.sum(total, axis=1, keepdims=True), shape)
+        for k, r in enumerate(pair):
+            rows = slice(k * ROWS, (k + 1) * ROWS)
+            out_ref[r, 0:ROWS, :] = mixed[rows]
+            out_ref[r, ROWS : ROWS + 8, :] = jnp.concatenate(
+                [row_max[rows].T[0:4], row_sum[rows].T[0:4]], axis=0
+            )
 
 
 def columns_kernel(key_ref, after_ref, out_ref):
@@ -243,7 +261,7 @@
         jax.ShapeDtypeStruct((spread, ROWS + 8, LANES), f32),
         [SMEM] + [VMEM] * 2,
         "attend",
-        [pltpu.VMEM((sources, ROWS, LANES), f32)],
+        [pltpu.VMEM((sources, 2 * ROWS, LANES), f32)],
         4 * spread * ROWS * sources * ROWS * HEAD_DIM,
         2 << 20,
     )(place, queries, keys)
@@ -257,14 +275,14 @@
         keys, queries
     )
     other = moved(own, lambda z, y, x, c: (z ^ 2, y, x, c))
-    far = from_y(own, 2)
+    next_own = from_y(own, 1)
     attended, own, other = call(
         combine_kernel,
         [jax.ShapeDtypeStruct((ROWS, HEAD_DIM), bf16), held, held],
         [VMEM] * 3,
         "combine",
     )(parts, own, other)
-    weights = [own, from_y(own, 1), far, from_y(own, 3)]
+    weights = [own, next_own, from_y(next_own, 1), from_y(own, 3)]
     weights += [other] + [from_y(other, k) for k in (1, 2, 3)]
 
     back = exchange(attended.reshape(planes, EACH, HEAD_DIM), PLANES)

time: 170 us -> 168 us (0.988)
  transfers between devices with their start and end apart: 12 -> 12, of which waited for: 5 -> 5; matrix products, arithmetic and copies ran while one was open for 1% -> 1% of each run, Pallas kernels for 3% -> 2%
where the time goes in v7:
time: 168 us; the launch traced here: 167 us
  starting transfers between devices  78.2 us (47%)
  blocking collectives  51 us (30%)
  waiting for transfers between devices  26 us (15%)
  Pallas kernels  7.4 us (4%)
  other arithmetic  2.4 us (1%)
    all_to_all x5, starting transfers between devices, exchange(): return lax.all_to_all(tiles, axes, split_axis=0, concat_axis=0, tiled=True)  50.5 us
    all_to_all x1, blocking collectives, exchange(): return lax.all_to_all(tiles, axes, split_axis=0, concat_axis=0, tiled=True)  40.5 us
    ppermute x7, starting transfers between devices, moved(): lax.ppermute(block, names, [(flat(*p), flat(*where(*p))) for p in places])  27.7 us
    all_to_all x5, waiting for transfers between devices, exchange(): return lax.all_to_all(tiles, axes, split_axis=0, concat_axis=0, tiled=True)  26 us
    all_gather x1, blocking collectives, shards(): queries = lax.all_gather(queries, QUERY_AXES)  10.6 us
  transfers between devices with their start and end apart: 12, of which 5 were waited for; matrix products, arithmetic and copies ran while one was open for 1% of the time, Pallas kernels for 2%

profile of v7, /device:TPU:1, one launch (start us, length us, event | category | flops | bytes accessed | tf_op | source)
XLA Modules:
  0.0 166.7 jit_solution(16654672737317662230)
XLA Ops:
  0.0 1.4 pad_maximum_fusion
  1.4 17.4 %all-to-all-start = ((bf16[8,24,256]{2,1,0:T(8,128)(2,1)}), bf16[8,24,256]{2,1,0:T(8,128)(2,1)S(1)}, u32[]{:S(2)}, u32[]{:S(2)}) async-start(bf16[8,24,256]{2,1,0:T(8,128)(2,1)} %pad_maximum_fusion), calls=%async_computation | async-start | bytes 196608 | tf_op jit(solution)/shard_map/all_to_all | solution.py:32
  18.9 0.8 pad_add_fusion
  19.7 0.1 convert_bitcast_fusion
  19.7 0.1 pad_maximum_fusion.1.docs_ref
  19.8 4.0 %all-to-all-done.rows_ref = bf16[8,24,256]{2,1,0:T(8,128)(2,1)S(1)} async-done(((bf16[8,24,256]{2,1,0:T(8,128)(2,1)}), bf16[8,24,256]{2,1,0:T(8,128)(2,1)S(1)}, u32[]{:S(2)}, u32[]{:S(2)}) %all-to-all-start) | async-done | bytes 98336 | tf_op jit(solution)/shard_map/all_to_all | solution.py:32
  23.9 0.0 copy-start.1
  23.9 0.7 copy-done.1
  24.6 40.5 %all_to_all.30.came_ref = bf16[16,64,128]{2,1,0:T(8,128)(2,1)S(1)} all-to-all(bf16[16,64,128]{2,1,0:T(8,128)(2,1)S(1)} %send.1), channel_id=1, replica_groups=mesh['zh'=8,'zp'=2,'z2'=2,'y'=4,'x'=4,'c'=2] {'zh','zp'}, dimensions={0} | all-to-all | bytes 524288 | tf_op jit(solution)/shard_map/all_to_all | solution.py:32
  65.1 1.3 spread.1
  66.3 14.6 %all-to-all-start.2 = ((bf16[16,336,128]{2,1,0:T(8,128)(2,1)}), bf16[16,336,128]{2,1,0:T(8,128)(2,1)S(1)}, u32[]{:S(2)}, u32[]{:S(2)}) async-start(bf16[16,336,128]{2,1,0:T(8,128)(2,1)} %get-tuple-element.11), calls=%async_computation.2 | async-start | bytes 2752512 | tf_op jit(solution)/shard_map/all_to_all | solution.py:32
  80.9 10.6 %all-gather = bf16[576,128]{1,0:T(8,128)(2,1)S(1)} all-gather(bf16[144,128]{1,0:T(8,128)(2,1)S(1)} %get-tuple-element.10), channel_id=2, replica_groups=mesh['zh'=8,'zp'=2,'z2'=2,'y'=4,'x'=4,'c'=2] {'y'}, dimensions={0}, use_global_device_ids=true | all-gather | bytes 184320 | tf_op jit(solution)/shard_map/all_gather | solution.py:257
  91.5 8.9 %all-to-all-done.2.key_ref = bf16[16,336,128]{2,1,0:T(8,128)(2,1)S(1)} async-done(((bf16[16,336,128]{2,1,0:T(8,128)(2,1)}), bf16[16,336,128]{2,1,0:T(8,128)(2,1)S(1)}, u32[]{:S(2)}, u32[]{:S(2)}) %all-to-all-start.2) | async-done | bytes 1376288 | tf_op jit(solution)/shard_map/all_to_all | solution.py:32
  100.4 7.6 %collective-permute-start = (bf16[16,64,128]{2,1,0:T(8,128)(2,1)S(1)}, bf16[16,64,128]{2,1,0:T(8,128)(2,1)S(1)}, u32[]{:S(2)}, u32[]{:S(2)}) collective-permute-start(bf16[16,64,128]{2,1,0:T(8,128)(2,1)S(1)} %columns.1.own_ref), channel_id=1, source_target_pairs={{0,64},{1,65},{2,66},{3,67},{4,68},{5,69},{6,70},{7,71},{8,72},{9,... | collective-permute-start | bytes 786440 | tf_op jit(solution)/shard_map/ppermute | solution.py:43
  108.0 0.1 stack.23.place_ref
  108.1 3.3 %attend.1 = f32[4,136,128]{2,1,0:T(8,128)} custom-call(s32[5]{0:T(128)S(1)} %stack.23.place_ref, bf16[4,144,128]{2,1,0:T(8,128)(2,1)S(1)} %bitcast.14, bf16[16,336,128]{2,1,0:T(8,128)(2,1)S(1)} %all-to-all-done.2.key_ref), custom_call_target="tpu_custom_call" | custom-call | flops 536870912 | bytes 2097152 | tf_op jit(solution)/shard_map/attend/pallas_call | solution.py:259
  111.4 0.0 copy-start
  111.4 4.3 %all-to-all-start.3 = ((f32[4,136,128]{2,1,0:T(8,128)}), f32[4,136,128]{2,1,0:T(8,128)S(1)}, u32[]{:S(2)}, u32[]{:S(2)}) async-start(f32[4,136,128]{2,1,0:T(8,128)} %attend.1), calls=%async_computation.3 | async-start | bytes 557056 | tf_op jit(solution)/shard_map/all_to_all | solution.py:32
  115.7 4.6 %collective-permute-start.1 = (bf16[16,64,128]{2,1,0:T(8,128)(2,1)S(1)}, bf16[16,64,128]{2,1,0:T(8,128)(2,1)S(1)}, u32[]{:S(2)}, u32[]{:S(2)}) collective-permute-start(bf16[16,64,128]{2,1,0:T(8,128)(2,1)S(1)} %columns.1.own_ref), channel_id=1, source_target_pairs={{0,24},{1,25},{2,26},{3,27},{4,28},{5,29},{6,30},{7,31},{8,0},{9,1... | collective-permute-start | bytes 786440 | tf_op jit(solution)/shard_map/ppermute | solution.py:43
  120.3 1.0 all-to-all-done.3.part_ref
  121.3 0.0 collective-permute-done.other_ref
  121.3 0.8 combine.1
  122.1 6.6 %all-to-all-start.4 = ((bf16[16,8,128]{2,1,0:T(8,128)(2,1)}), bf16[16,8,128]{2,1,0:T(8,128)(2,1)S(1)}, u32[]{:S(2)}, u32[]{:S(2)}) async-start(bf16[16,8,128]{2,1,0:T(8,128)(2,1)} %bitcast.11), calls=%async_computation.4 | async-start | bytes 65536 | tf_op jit(solution)/shard_map/all_to_all | solution.py:32
  128.7 2.7 %collective-permute-start.3 = (bf16[16,64,128]{2,1,0:T(8,128)(2,1)S(1)}, bf16[16,64,128]{2,1,0:T(8,128)(2,1)S(1)}, u32[]{:S(2)}, u32[]{:S(2)}) collective-permute-start(bf16[16,64,128]{2,1,0:T(8,128)(2,1)S(1)} %get-tuple-element.13.refs_0_), channel_id=1, source_target_pairs={{0,8},{1,9},{2,10},{3,11},{4,12},{5,13},{6,14},{7,15},{8,16},{9,17... | collective-permute-start | bytes 786440 | tf_op jit(solution)/shard_map/ppermute | solution.py:43
  131.4 0.0 collective-permute-done.1.refs_1_
  131.4 3.8 %collective-permute-start.2 = (bf16[16,64,128]{2,1,0:T(8,128)(2,1)S(1)}, bf16[16,64,128]{2,1,0:T(8,128)(2,1)S(1)}, u32[]{:S(2)}, u32[]{:S(2)}) collective-permute-start(bf16[16,64,128]{2,1,0:T(8,128)(2,1)S(1)} %collective-permute-done.1.refs_1_), channel_id=1, source_target_pairs={{0,24},{1,25},{2,26},{3,27},{4,28},{5,29},{6,30},{7,31},{8,0},{9,1... | collective-permute-start | bytes 786440 | tf_op jit(solution)/shard_map/ppermute | solution.py:43
  135.2 1.9 %collective-permute-start.6 = (bf16[16,64,128]{2,1,0:T(8,128)(2,1)S(1)}, bf16[16,64,128]{2,1,0:T(8,128)(2,1)S(1)}, u32[]{:S(2)}, u32[]{:S(2)}) collective-permute-start(bf16[16,64,128]{2,1,0:T(8,128)(2,1)S(1)} %get-tuple-element.14.refs_4_), channel_id=1, source_target_pairs={{0,8},{1,9},{2,10},{3,11},{4,12},{5,13},{6,14},{7,15},{8,16},{9,17... | collective-permute-start | bytes 786440 | tf_op jit(solution)/shard_map/ppermute | solution.py:43
  137.1 4.1 %collective-permute-start.5 = (bf16[16,64,128]{2,1,0:T(8,128)(2,1)S(1)}, bf16[16,64,128]{2,1,0:T(8,128)(2,1)S(1)}, u32[]{:S(2)}, u32[]{:S(2)}) collective-permute-start(bf16[16,64,128]{2,1,0:T(8,128)(2,1)S(1)} %get-tuple-element.14.refs_4_), channel_id=1, source_target_pairs={{0,16},{1,17},{2,18},{3,19},{4,20},{5,21},{6,22},{7,23},{8,24},{9,... | collective-permute-start | bytes 786440 | tf_op jit(solution)/shard_map/ppermute | solution.py:43
  141.3 3.0 %collective-permute-start.4 = (bf16[16,64,128]{2,1,0:T(8,128)(2,1)S(1)}, bf16[16,64,128]{2,1,0:T(8,128)(2,1)S(1)}, u32[]{:S(2)}, u32[]{:S(2)}) collective-permute-start(bf16[16,64,128]{2,1,0:T(8,128)(2,1)S(1)} %get-tuple-element.14.refs_4_), channel_id=1, source_target_pairs={{0,24},{1,25},{2,26},{3,27},{4,28},{5,29},{6,30},{7,31},{8,0},{9,1... | collective-permute-start | bytes 786440 | tf_op jit(solution)/shard_map/ppermute | solution.py:43
  144.2 5.6 %all-to-all-done.4 = bf16[16,8,128]{2,1,0:T(8,128)(2,1)S(1)} async-done(((bf16[16,8,128]{2,1,0:T(8,128)(2,1)}), bf16[16,8,128]{2,1,0:T(8,128)(2,1)S(1)}, u32[]{:S(2)}, u32[]{:S(2)}) %all-to-all-start.4) | async-done | bytes 32800 | tf_op jit(solution)/shard_map/all_to_all | solution.py:32
  149.8 0.7 broadcast_in_dim.2
  150.5 7.6 %all-to-all-start.5 = ((bf16[8,16,8,128]{3,2,1,0:T(8,128)(2,1)}), bf16[8,16,8,128]{3,2,1,0:T(8,128)(2,1)S(1)}, u32[]{:S(2)}, u32[]{:S(2)}) async-start(bf16[8,16,8,128]{3,2,1,0:T(8,128)(2,1)} %broadcast_in_dim.2), calls=%async_computation.5 | async-start | bytes 524288 | tf_op jit(solution)/shard_map/all_to_all | solution.py:32
  158.1 0.0 collective-permute-done.2.refs_2_
  158.1 0.0 collective-permute-done.3.refs_3_
  158.1 0.0 collective-permute-done.6.refs_7_
  158.2 0.0 collective-permute-done.5.refs_6_
  158.2 0.0 collective-permute-done.4.refs_5_
  158.2 6.5 %all-to-all-done.5.attended_ref = bf16[8,16,8,128]{3,2,1,0:T(8,128)(2,1)S(1)} async-done(((bf16[8,16,8,128]{3,2,1,0:T(8,128)(2,1)}), bf16[8,16,8,128]{3,2,1,0:T(8,128)(2,1)S(1)}, u32[]{:S(2)}, u32[]{:S(2)}) %all-to-all-start.5) | async-done | bytes 262176 | tf_op jit(solution)/shard_map/all_to_all | solution.py:32
  164.6 0.0 copy-done
  164.6 2.0 %product.1 = bf16[64,512]{1,0:T(8,128)(2,1)} custom-call(s32[5]{0:T(128)S(1)} %stack.23.place_ref, bf16[8,16,8,128]{3,2,1,0:T(8,128)(2,1)S(1)} %all-to-all-done.5.attended_ref, bf16[16,64,128]{2,1,0:T(8,128)(2,1)S(1)} %get-tuple-element.13.refs_0_, bf16[16,64,128]{2,1,0:T(8,128)(2,1)S(1)} %collective-permute-done.1.refs_1_, ...), custom_call_target="tpu_custom_call" | custom-call | flops 134217728 | bytes 3145728 | tf_op jit(solution)/shard_map/product/pallas_call | solution.py:290
  (2 shorter events, 0.0 us)
Async XLA Ops:
  1.4 22.4 %all-to-all-start = ((bf16[8,24,256]{2,1,0:T(8,128)(2,1)}), bf16[8,24,256]{2,1,0:T(8,128)(2,1)S(1)}, u32[]{:S(2)}, u32[]{:S(2)}) async-start(bf16[8,24,256]{2,1,0:T(8,128)(2,1)} %pad_maximum_fusion), calls=%async_computation | async-start | bytes 196608 | tf_op jit(solution)/shard_map/all_to_all | solution.py:32
  23.9 0.7 copy-start.1
  66.3 34.0 %all-to-all-start.2 = ((bf16[16,336,128]{2,1,0:T(8,128)(2,1)}), bf16[16,336,128]{2,1,0:T(8,128)(2,1)S(1)}, u32[]{:S(2)}, u32[]{:S(2)}) async-start(bf16[16,336,128]{2,1,0:T(8,128)(2,1)} %get-tuple-element.11), calls=%async_computation.2 | async-start | bytes 2752512 | tf_op jit(solution)/shard_map/all_to_all | solution.py:32
  100.4 20.9 %collective-permute-start = (bf16[16,64,128]{2,1,0:T(8,128)(2,1)S(1)}, bf16[16,64,128]{2,1,0:T(8,128)(2,1)S(1)}, u32[]{:S(2)}, u32[]{:S(2)}) collective-permute-start(bf16[16,64,128]{2,1,0:T(8,128)(2,1)S(1)} %columns.1.own_ref), channel_id=1, source_target_pairs={{0,64},{1,65},{2,66},{3,67},{4,68},{5,69},{6,70},{7,71},{8,72},{9,... | collective-permute-start | bytes 786440 | tf_op jit(solution)/shard_map/ppermute | solution.py:43
  111.4 53.3 %copy-start = (bf16[64,512]{1,0:T(8,128)(2,1)S(1)}, bf16[64,512]{1,0:T(8,128)(2,1)}, u32[]{:S(2)}) copy-start(bf16[64,512]{1,0:T(8,128)(2,1)} %refs_8_.1) | copy-start | bytes 196612
  111.4 9.9 %all-to-all-start.3 = ((f32[4,136,128]{2,1,0:T(8,128)}), f32[4,136,128]{2,1,0:T(8,128)S(1)}, u32[]{:S(2)}, u32[]{:S(2)}) async-start(f32[4,136,128]{2,1,0:T(8,128)} %attend.1), calls=%async_computation.3 | async-start | bytes 557056 | tf_op jit(solution)/shard_map/all_to_all | solution.py:32
  115.7 15.7 %collective-permute-start.1 = (bf16[16,64,128]{2,1,0:T(8,128)(2,1)S(1)}, bf16[16,64,128]{2,1,0:T(8,128)(2,1)S(1)}, u32[]{:S(2)}, u32[]{:S(2)}) collective-permute-start(bf16[16,64,128]{2,1,0:T(8,128)(2,1)S(1)} %columns.1.own_ref), channel_id=1, source_target_pairs={{0,24},{1,25},{2,26},{3,27},{4,28},{5,29},{6,30},{7,31},{8,0},{9,1... | collective-permute-start | bytes 786440 | tf_op jit(solution)/shard_map/ppermute | solution.py:43
  122.1 27.7 %all-to-all-start.4 = ((bf16[16,8,128]{2,1,0:T(8,128)(2,1)}), bf16[16,8,128]{2,1,0:T(8,128)(2,1)S(1)}, u32[]{:S(2)}, u32[]{:S(2)}) async-start(bf16[16,8,128]{2,1,0:T(8,128)(2,1)} %bitcast.11), calls=%async_computation.4 | async-start | bytes 65536 | tf_op jit(solution)/shard_map/all_to_all | solution.py:32
  128.7 29.5 %collective-permute-start.3 = (bf16[16,64,128]{2,1,0:T(8,128)(2,1)S(1)}, bf16[16,64,128]{2,1,0:T(8,128)(2,1)S(1)}, u32[]{:S(2)}, u32[]{:S(2)}) collective-permute-start(bf16[16,64,128]{2,1,0:T(8,128)(2,1)S(1)} %get-tuple-element.13.refs_0_), channel_id=1, source_target_pairs={{0,8},{1,9},{2,10},{3,11},{4,12},{5,13},{6,14},{7,15},{8,16},{9,17... | collective-permute-start | bytes 786440 | tf_op jit(solution)/shard_map/ppermute | solution.py:43
  131.4 26.7 %collective-permute-start.2 = (bf16[16,64,128]{2,1,0:T(8,128)(2,1)S(1)}, bf16[16,64,128]{2,1,0:T(8,128)(2,1)S(1)}, u32[]{:S(2)}, u32[]{:S(2)}) collective-permute-start(bf16[16,64,128]{2,1,0:T(8,128)(2,1)S(1)} %collective-permute-done.1.refs_1_), channel_id=1, source_target_pairs={{0,24},{1,25},{2,26},{3,27},{4,28},{5,29},{6,30},{7,31},{8,0},{9,1... | collective-permute-start | bytes 786440 | tf_op jit(solution)/shard_map/ppermute | solution.py:43
  135.2 22.9 %collective-permute-start.6 = (bf16[16,64,128]{2,1,0:T(8,128)(2,1)S(1)}, bf16[16,64,128]{2,1,0:T(8,128)(2,1)S(1)}, u32[]{:S(2)}, u32[]{:S(2)}) collective-permute-start(bf16[16,64,128]{2,1,0:T(8,128)(2,1)S(1)} %get-tuple-element.14.refs_4_), channel_id=1, source_target_pairs={{0,8},{1,9},{2,10},{3,11},{4,12},{5,13},{6,14},{7,15},{8,16},{9,17... | collective-permute-start | bytes 786440 | tf_op jit(solution)/shard_map/ppermute | solution.py:43
  137.1 21.0 %collective-permute-start.5 = (bf16[16,64,128]{2,1,0:T(8,128)(2,1)S(1)}, bf16[16,64,128]{2,1,0:T(8,128)(2,1)S(1)}, u32[]{:S(2)}, u32[]{:S(2)}) collective-permute-start(bf16[16,64,128]{2,1,0:T(8,128)(2,1)S(1)} %get-tuple-element.14.refs_4_), channel_id=1, source_target_pairs={{0,16},{1,17},{2,18},{3,19},{4,20},{5,21},{6,22},{7,23},{8,24},{9,... | collective-permute-start | bytes 786440 | tf_op jit(solution)/shard_map/ppermute | solution.py:43
  141.3 16.9 %collective-permute-start.4 = (bf16[16,64,128]{2,1,0:T(8,128)(2,1)S(1)}, bf16[16,64,128]{2,1,0:T(8,128)(2,1)S(1)}, u32[]{:S(2)}, u32[]{:S(2)}) collective-permute-start(bf16[16,64,128]{2,1,0:T(8,128)(2,1)S(1)} %get-tuple-element.14.refs_4_), channel_id=1, source_target_pairs={{0,24},{1,25},{2,26},{3,27},{4,28},{5,29},{6,30},{7,31},{8,0},{9,1... | collective-permute-start | bytes 786440 | tf_op jit(solution)/shard_map/ppermute | solution.py:43
  150.5 14.1 %all-to-all-start.5 = ((bf16[8,16,8,128]{3,2,1,0:T(8,128)(2,1)}), bf16[8,16,8,128]{3,2,1,0:T(8,128)(2,1)S(1)}, u32[]{:S(2)}, u32[]{:S(2)}) async-start(bf16[8,16,8,128]{3,2,1,0:T(8,128)(2,1)} %broadcast_in_dim.2), calls=%async_computation.5 | async-start | bytes 524288 | tf_op jit(solution)/shard_map/all_to_all | solution.py:32

commit v8 on v7

--- a/solution.py
+++ b/solution.py
@@ -45,6 +45,15 @@
 
 def transposed(row):
     return jnp.broadcast_to(row, (LANES, LANES)).T
+
+
+def in_parts(value):
+    parts = []
+    for _ in range(3):
+        part = value.astype(jnp.bfloat16).astype(jnp.float32)
+        parts.append(part)
+        value = value - part
+    return parts
 
 
 def call(kernel, out_shape, in_specs, name, scratch=(), flops=0, moved_bytes=1 << 20):
@@ -65,9 +74,8 @@
 SENT = WEIGHT_AT + COLUMNS
 
 
-def send_kernel(rows_ref, docs_ref, weight_ref, out_ref):
-    docs = jnp.broadcast_to(docs_ref[...].astype(jnp.float32), (EACH, LANES))
-    weight = [weight_ref[:, k * LANES : (k + 1) * LANES] for k in range(2)]
+def send_kernel(rows_ref, extra_ref, out_ref):
+    docs = extra_ref[COLUMNS : COLUMNS + 16, 0:LANES].astype(jnp.float32)[0:EACH]
     for group in range(rows_ref.shape[0]):
         for j in range(2):
             lanes = slice(j * LANES, (j + 1) * LANES)
@@ -77,7 +85,7 @@
             tile[2 * EACH : 4 * EACH, :] = jnp.concatenate([values, docs], axis=0).astype(
                 jnp.bfloat16
             )
-            tile[WEIGHT_AT:SENT, :] = weight[j]
+            tile[WEIGHT_AT:SENT, :] = extra_ref[0:COLUMNS, lanes]
 
 
 DOCS_AT = 2 * ROWS
@@ -165,12 +173,13 @@
                 preferred_element_type=jnp.float32,
             )
         row_sum = jnp.broadcast_to(jnp.sum(total, axis=1, keepdims=True), shape)
+        means = jnp.where(row_sum > 0.0, mixed / row_sum, 0.0).astype(jnp.bfloat16)
         for k, r in enumerate(pair):
             rows = slice(k * ROWS, (k + 1) * ROWS)
-            out_ref[r, 0:ROWS, :] = mixed[rows]
-            out_ref[r, ROWS : ROWS + 8, :] = jnp.concatenate(
-                [row_max[rows].T[0:4], row_sum[rows].T[0:4]], axis=0
-            )
+            out_ref[r, 0:ROWS, :] = means[rows]
+            stats = in_parts(row_max[rows].T[0:1]) + in_parts(row_sum[rows].T[0:1])
+            stats = jnp.concatenate(stats + [jnp.zeros((10, LANES), jnp.float32)], axis=0)
+            out_ref[r, ROWS : ROWS + 16, :] = stats.astype(jnp.bfloat16)
 
 
 def columns_kernel(key_ref, after_ref, out_ref):
@@ -181,16 +190,19 @@
     same_own_ref[...] = own_ref[...]
     same_other_ref[...] = other_ref[...]
     parts = part_ref.shape[0]
-    maxima = [part_ref[r, ROWS : ROWS + 1, :] for r in range(parts)]
-    sums = [part_ref[r, ROWS + 4 : ROWS + 5, :] for r in range(parts)]
+    stats = [part_ref[r, ROWS : ROWS + 16, :].astype(jnp.float32) for r in range(parts)]
+    maxima = [t[0:1] + t[1:2] + t[2:3] for t in stats]
+    sums = [t[3:4] + t[4:5] + t[5:6] for t in stats]
     row_max = maxima[0]
     for m in maxima[1:]:
         row_max = jnp.maximum(row_max, m)
     scales = [jnp.exp2((m - row_max) * FACTOR) for m in maxima]
-    row_sum = sum(scale * s for scale, s in zip(scales, sums))
+    scales = [scale * s for scale, s in zip(scales, sums)]
+    row_sum = sum(scales)
     mixed = jnp.zeros((ROWS, HEAD_DIM), jnp.float32)
     for r in range(parts):
-        mixed = mixed + part_ref[r, 0:ROWS, :] * transposed(scales[r] / row_sum)
+        mean = part_ref[r, 0:ROWS, :].astype(jnp.float32)
+        mixed = mixed + mean * transposed(scales[r] / row_sum)
     out_ref[...] = mixed.astype(out_ref.dtype)
 
 
@@ -239,10 +251,11 @@
     by_rows = exchange(jnp.concatenate(cut, axis=1), HEAD_AXES)
     first = (2 * lax.axis_index("x") + lax.axis_index("c")) * EACH
     docs = jnp.roll(doc_ids, -first)
-    docs = jnp.concatenate([docs, docs]).astype(bf16).reshape(1, LANES)
+    docs = jnp.tile(docs.astype(bf16), 2 * LANES // BLOCK)
+    extra = jnp.concatenate([out_weight.T, jnp.broadcast_to(docs, (16, 2 * LANES))])
     sent = call(
-        send_kernel, jax.ShapeDtypeStruct((planes, SENT, LANES), bf16), [VMEM] * 3, "send"
-    )(by_rows, docs, out_weight.T)
+        send_kernel, jax.ShapeDtypeStruct((planes, SENT, LANES), bf16), [VMEM] * 2, "send"
+    )(by_rows, extra)
     came = exchange(sent, PLANES)
     queries, keys = call(
         gather_kernel,
@@ -258,7 +271,7 @@
 
     parts = call(
         attend_kernel,
-        jax.ShapeDtypeStruct((spread, ROWS + 8, LANES), f32),
+        jax.ShapeDtypeStruct((spread, ROWS + 16, LANES), bf16),
         [SMEM] + [VMEM] * 2,
         "attend",
         [pltpu.VMEM((sources, 2 * ROWS, LANES), f32)],

time: 168 us -> 166 us (0.988)
  waiting for transfers between devices: 26 us -> 24.1 us
    all_to_all x5, waiting for transfers between devices: 26 us -> 24 us  [exchange(): return lax.all_to_all(tiles, axes, split_axis=0, concat_axis=0, tiled=True)]
  transfers between devices with their start and end apart: 12 -> 12, of which waited for: 5 -> 5; matrix products, arithmetic and copies ran while one was open for 1% -> 2% of each run, Pallas kernels for 2% -> 2%
where the time goes in v8:
time: 166 us; the launch traced here: 165 us
  starting transfers between devices  78.4 us (47%)
  blocking collectives  51 us (31%)
  waiting for transfers between devices  24.1 us (15%)
  Pallas kernels  7.4 us (4%)
  other arithmetic  3.03 us (2%)
    all_to_all x5, starting transfers between devices, exchange(): return lax.all_to_all(tiles, axes, split_axis=0, concat_axis=0, tiled=True)  50.2 us
    all_to_all x1, blocking collectives, exchange(): return lax.all_to_all(tiles, axes, split_axis=0, concat_axis=0, tiled=True)  40.5 us
    ppermute x7, starting transfers between devices, moved(): lax.ppermute(block, names, [(flat(*p), flat(*where(*p))) for p in places])  28.2 us
    all_to_all x5, waiting for transfers between devices, exchange(): return lax.all_to_all(tiles, axes, split_axis=0, concat_axis=0, tiled=True)  24 us
    all_gather x1, blocking collectives, shards(): queries = lax.all_gather(queries, QUERY_AXES)  10.6 us
  transfers between devices with their start and end apart: 12, of which 5 were waited for; matrix products, arithmetic and copies ran while one was open for 2% of the time, Pallas kernels for 2%

profile of v8, /device:TPU:1, one launch (start us, length us, event | category | flops | bytes accessed | tf_op | source)
XLA Modules:
  0.0 165.0 jit_solution(13307895601382341172)
XLA Ops:
  0.0 1.4 pad_maximum_fusion
  1.4 17.4 %all-to-all-start = ((bf16[8,24,256]{2,1,0:T(8,128)(2,1)}), bf16[8,24,256]{2,1,0:T(8,128)(2,1)S(1)}, u32[]{:S(2)}, u32[]{:S(2)}) async-start(bf16[8,24,256]{2,1,0:T(8,128)(2,1)} %pad_maximum_fusion), calls=%async_computation | async-start | bytes 196608 | tf_op jit(solution)/shard_map/all_to_all | solution.py:32
  18.8 0.8 pad_add_fusion
  19.7 0.1 dynamic-slice_convert_fusion
  19.7 0.1 tile.10
  19.8 0.7 pad_maximum_fusion.1.extra_ref
  20.6 3.3 %all-to-all-done.rows_ref = bf16[8,24,256]{2,1,0:T(8,128)(2,1)S(1)} async-done(((bf16[8,24,256]{2,1,0:T(8,128)(2,1)}), bf16[8,24,256]{2,1,0:T(8,128)(2,1)S(1)}, u32[]{:S(2)}, u32[]{:S(2)}) %all-to-all-start) | async-done | bytes 98336 | tf_op jit(solution)/shard_map/all_to_all | solution.py:32
  23.9 40.5 %all_to_all.30.came_ref = bf16[16,64,128]{2,1,0:T(8,128)(2,1)S(1)} all-to-all(bf16[16,64,128]{2,1,0:T(8,128)(2,1)S(1)} %send.1), channel_id=1, replica_groups=mesh['zh'=8,'zp'=2,'z2'=2,'y'=4,'x'=4,'c'=2] {'zh','zp'}, dimensions={0} | all-to-all | bytes 524288 | tf_op jit(solution)/shard_map/all_to_all | solution.py:32
  64.4 1.3 spread.1
  65.6 14.6 %all-to-all-start.2 = ((bf16[16,336,128]{2,1,0:T(8,128)(2,1)}), bf16[16,336,128]{2,1,0:T(8,128)(2,1)S(1)}, u32[]{:S(2)}, u32[]{:S(2)}) async-start(bf16[16,336,128]{2,1,0:T(8,128)(2,1)} %get-tuple-element.11), calls=%async_computation.2 | async-start | bytes 2752512 | tf_op jit(solution)/shard_map/all_to_all | solution.py:32
  80.2 10.6 %all-gather = bf16[576,128]{1,0:T(8,128)(2,1)S(1)} all-gather(bf16[144,128]{1,0:T(8,128)(2,1)S(1)} %get-tuple-element.10), channel_id=2, replica_groups=mesh['zh'=8,'zp'=2,'z2'=2,'y'=4,'x'=4,'c'=2] {'y'}, dimensions={0}, use_global_device_ids=true | all-gather | bytes 184320 | tf_op jit(solution)/shard_map/all_gather | solution.py:270
  90.8 8.9 %all-to-all-done.2.key_ref = bf16[16,336,128]{2,1,0:T(8,128)(2,1)S(1)} async-done(((bf16[16,336,128]{2,1,0:T(8,128)(2,1)}), bf16[16,336,128]{2,1,0:T(8,128)(2,1)S(1)}, u32[]{:S(2)}, u32[]{:S(2)}) %all-to-all-start.2) | async-done | bytes 1376288 | tf_op jit(solution)/shard_map/all_to_all | solution.py:32
  99.7 7.6 %collective-permute-start = (bf16[16,64,128]{2,1,0:T(8,128)(2,1)S(1)}, bf16[16,64,128]{2,1,0:T(8,128)(2,1)S(1)}, u32[]{:S(2)}, u32[]{:S(2)}) collective-permute-start(bf16[16,64,128]{2,1,0:T(8,128)(2,1)S(1)} %columns.1.own_ref), channel_id=1, source_target_pairs={{0,64},{1,65},{2,66},{3,67},{4,68},{5,69},{6,70},{7,71},{8,72},{9,... | collective-permute-start | bytes 786440 | tf_op jit(solution)/shard_map/ppermute | solution.py:43
  107.3 0.1 stack.23.place_ref
  107.4 3.3 %attend.1 = bf16[4,144,128]{2,1,0:T(8,128)(2,1)} custom-call(s32[5]{0:T(128)S(1)} %stack.23.place_ref, bf16[4,144,128]{2,1,0:T(8,128)(2,1)S(1)} %bitcast.12, bf16[16,336,128]{2,1,0:T(8,128)(2,1)S(1)} %all-to-all-done.2.key_ref), custom_call_target="tpu_custom_call" | custom-call | flops 536870912 | bytes 2097152 | tf_op jit(solution)/shard_map/attend/pallas_call | solution.py:272
  110.6 0.0 copy-start
  110.6 4.3 %all-to-all-start.3 = ((bf16[4,144,128]{2,1,0:T(8,128)(2,1)}), bf16[4,144,128]{2,1,0:T(8,128)(2,1)S(1)}, u32[]{:S(2)}, u32[]{:S(2)}) async-start(bf16[4,144,128]{2,1,0:T(8,128)(2,1)} %attend.1), calls=%async_computation.3 | async-start | bytes 294912 | tf_op jit(solution)/shard_map/all_to_all | solution.py:32
  115.0 4.6 %collective-permute-start.1 = (bf16[16,64,128]{2,1,0:T(8,128)(2,1)S(1)}, bf16[16,64,128]{2,1,0:T(8,128)(2,1)S(1)}, u32[]{:S(2)}, u32[]{:S(2)}) collective-permute-start(bf16[16,64,128]{2,1,0:T(8,128)(2,1)S(1)} %columns.1.own_ref), channel_id=1, source_target_pairs={{0,24},{1,25},{2,26},{3,27},{4,28},{5,29},{6,30},{7,31},{8,0},{9,1... | collective-permute-start | bytes 786440 | tf_op jit(solution)/shard_map/ppermute | solution.py:43
  119.6 0.3 all-to-all-done.3.part_ref
  119.9 0.0 collective-permute-done.other_ref
  119.9 0.8 combine.1
  120.7 6.8 %all-to-all-start.4 = ((bf16[16,8,128]{2,1,0:T(8,128)(2,1)}), bf16[16,8,128]{2,1,0:T(8,128)(2,1)S(1)}, u32[]{:S(2)}, u32[]{:S(2)}) async-start(bf16[16,8,128]{2,1,0:T(8,128)(2,1)} %bitcast.10), calls=%async_computation.4 | async-start | bytes 65536 | tf_op jit(solution)/shard_map/all_to_all | solution.py:32
  127.5 3.2 %collective-permute-start.3 = (bf16[16,64,128]{2,1,0:T(8,128)(2,1)S(1)}, bf16[16,64,128]{2,1,0:T(8,128)(2,1)S(1)}, u32[]{:S(2)}, u32[]{:S(2)}) collective-permute-start(bf16[16,64,128]{2,1,0:T(8,128)(2,1)S(1)} %get-tuple-element.13.refs_0_), channel_id=1, source_target_pairs={{0,8},{1,9},{2,10},{3,11},{4,12},{5,13},{6,14},{7,15},{8,16},{9,17... | collective-permute-start | bytes 786440 | tf_op jit(solution)/shard_map/ppermute | solution.py:43
  130.7 0.0 collective-permute-done.1.refs_1_
  130.7 3.4 %collective-permute-start.2 = (bf16[16,64,128]{2,1,0:T(8,128)(2,1)S(1)}, bf16[16,64,128]{2,1,0:T(8,128)(2,1)S(1)}, u32[]{:S(2)}, u32[]{:S(2)}) collective-permute-start(bf16[16,64,128]{2,1,0:T(8,128)(2,1)S(1)} %collective-permute-done.1.refs_1_), channel_id=1, source_target_pairs={{0,24},{1,25},{2,26},{3,27},{4,28},{5,29},{6,30},{7,31},{8,0},{9,1... | collective-permute-start | bytes 786440 | tf_op jit(solution)/shard_map/ppermute | solution.py:43
  134.1 1.9 %collective-permute-start.6 = (bf16[16,64,128]{2,1,0:T(8,128)(2,1)S(1)}, bf16[16,64,128]{2,1,0:T(8,128)(2,1)S(1)}, u32[]{:S(2)}, u32[]{:S(2)}) collective-permute-start(bf16[16,64,128]{2,1,0:T(8,128)(2,1)S(1)} %get-tuple-element.14.refs_4_), channel_id=1, source_target_pairs={{0,8},{1,9},{2,10},{3,11},{4,12},{5,13},{6,14},{7,15},{8,16},{9,17... | collective-permute-start | bytes 786440 | tf_op jit(solution)/shard_map/ppermute | solution.py:43
  136.0 4.5 %collective-permute-start.5 = (bf16[16,64,128]{2,1,0:T(8,128)(2,1)S(1)}, bf16[16,64,128]{2,1,0:T(8,128)(2,1)S(1)}, u32[]{:S(2)}, u32[]{:S(2)}) collective-permute-start(bf16[16,64,128]{2,1,0:T(8,128)(2,1)S(1)} %get-tuple-element.14.refs_4_), channel_id=1, source_target_pairs={{0,16},{1,17},{2,18},{3,19},{4,20},{5,21},{6,22},{7,23},{8,24},{9,... | collective-permute-start | bytes 786440 | tf_op jit(solution)/shard_map/ppermute | solution.py:43
  140.5 3.0 %collective-permute-start.4 = (bf16[16,64,128]{2,1,0:T(8,128)(2,1)S(1)}, bf16[16,64,128]{2,1,0:T(8,128)(2,1)S(1)}, u32[]{:S(2)}, u32[]{:S(2)}) collective-permute-start(bf16[16,64,128]{2,1,0:T(8,128)(2,1)S(1)} %get-tuple-element.14.refs_4_), channel_id=1, source_target_pairs={{0,24},{1,25},{2,26},{3,27},{4,28},{5,29},{6,30},{7,31},{8,0},{9,1... | collective-permute-start | bytes 786440 | tf_op jit(solution)/shard_map/ppermute | solution.py:43
  143.5 5.1 %all-to-all-done.4 = bf16[16,8,128]{2,1,0:T(8,128)(2,1)S(1)} async-done(((bf16[16,8,128]{2,1,0:T(8,128)(2,1)}), bf16[16,8,128]{2,1,0:T(8,128)(2,1)S(1)}, u32[]{:S(2)}, u32[]{:S(2)}) %all-to-all-start.4) | async-done | bytes 32800 | tf_op jit(solution)/shard_map/all_to_all | solution.py:32
  148.6 0.7 broadcast_in_dim.10
  149.3 7.1 %all-to-all-start.5 = ((bf16[8,16,8,128]{3,2,1,0:T(8,128)(2,1)}), bf16[8,16,8,128]{3,2,1,0:T(8,128)(2,1)S(1)}, u32[]{:S(2)}, u32[]{:S(2)}) async-start(bf16[8,16,8,128]{3,2,1,0:T(8,128)(2,1)} %broadcast_in_dim.10), calls=%async_computation.5 | async-start | bytes 524288 | tf_op jit(solution)/shard_map/all_to_all | solution.py:32
  156.4 0.0 collective-permute-done.2.refs_2_
  156.4 0.0 collective-permute-done.3.refs_3_
  156.4 0.0 collective-permute-done.6.refs_7_
  156.5 0.0 collective-permute-done.5.refs_6_
  156.5 0.0 collective-permute-done.4.refs_5_
  156.5 6.5 %all-to-all-done.5.attended_ref = bf16[8,16,8,128]{3,2,1,0:T(8,128)(2,1)S(1)} async-done(((bf16[8,16,8,128]{3,2,1,0:T(8,128)(2,1)}), bf16[8,16,8,128]{3,2,1,0:T(8,128)(2,1)S(1)}, u32[]{:S(2)}, u32[]{:S(2)}) %all-to-all-start.5) | async-done | bytes 262176 | tf_op jit(solution)/shard_map/all_to_all | solution.py:32
  162.9 0.0 copy-done
  162.9 2.0 %product.1 = bf16[64,512]{1,0:T(8,128)(2,1)} custom-call(s32[5]{0:T(128)S(1)} %stack.23.place_ref, bf16[8,16,8,128]{3,2,1,0:T(8,128)(2,1)S(1)} %all-to-all-done.5.attended_ref, bf16[16,64,128]{2,1,0:T(8,128)(2,1)S(1)} %get-tuple-element.13.refs_0_, bf16[16,64,128]{2,1,0:T(8,128)(2,1)S(1)} %collective-permute-done.1.refs_1_, ...), custom_call_target="tpu_custom_call" | custom-call | flops 134217728 | bytes 3145728 | tf_op jit(solution)/shard_map/product/pallas_call | solution.py:303
  (4 shorter events, 0.1 us)
Async XLA Ops:
  1.4 22.4 %all-to-all-start = ((bf16[8,24,256]{2,1,0:T(8,128)(2,1)}), bf16[8,24,256]{2,1,0:T(8,128)(2,1)S(1)}, u32[]{:S(2)}, u32[]{:S(2)}) async-start(bf16[8,24,256]{2,1,0:T(8,128)(2,1)} %pad_maximum_fusion), calls=%async_computation | async-start | bytes 196608 | tf_op jit(solution)/shard_map/all_to_all | solution.py:32
  65.6 34.0 %all-to-all-start.2 = ((bf16[16,336,128]{2,1,0:T(8,128)(2,1)}), bf16[16,336,128]{2,1,0:T(8,128)(2,1)S(1)}, u32[]{:S(2)}, u32[]{:S(2)}) async-start(bf16[16,336,128]{2,1,0:T(8,128)(2,1)} %get-tuple-element.11), calls=%async_computation.2 | async-start | bytes 2752512 | tf_op jit(solution)/shard_map/all_to_all | solution.py:32
  99.7 20.2 %collective-permute-start = (bf16[16,64,128]{2,1,0:T(8,128)(2,1)S(1)}, bf16[16,64,128]{2,1,0:T(8,128)(2,1)S(1)}, u32[]{:S(2)}, u32[]{:S(2)}) collective-permute-start(bf16[16,64,128]{2,1,0:T(8,128)(2,1)S(1)} %columns.1.own_ref), channel_id=1, source_target_pairs={{0,64},{1,65},{2,66},{3,67},{4,68},{5,69},{6,70},{7,71},{8,72},{9,... | collective-permute-start | bytes 786440 | tf_op jit(solution)/shard_map/ppermute | solution.py:43
  110.6 52.3 %copy-start = (bf16[64,512]{1,0:T(8,128)(2,1)S(1)}, bf16[64,512]{1,0:T(8,128)(2,1)}, u32[]{:S(2)}) copy-start(bf16[64,512]{1,0:T(8,128)(2,1)} %refs_8_.1) | copy-start | bytes 196612
  110.6 9.2 %all-to-all-start.3 = ((bf16[4,144,128]{2,1,0:T(8,128)(2,1)}), bf16[4,144,128]{2,1,0:T(8,128)(2,1)S(1)}, u32[]{:S(2)}, u32[]{:S(2)}) async-start(bf16[4,144,128]{2,1,0:T(8,128)(2,1)} %attend.1), calls=%async_computation.3 | async-start | bytes 294912 | tf_op jit(solution)/shard_map/all_to_all | solution.py:32
  115.0 15.7 %collective-permute-start.1 = (bf16[16,64,128]{2,1,0:T(8,128)(2,1)S(1)}, bf16[16,64,128]{2,1,0:T(8,128)(2,1)S(1)}, u32[]{:S(2)}, u32[]{:S(2)}) collective-permute-start(bf16[16,64,128]{2,1,0:T(8,128)(2,1)S(1)} %columns.1.own_ref), channel_id=1, source_target_pairs={{0,24},{1,25},{2,26},{3,27},{4,28},{5,29},{6,30},{7,31},{8,0},{9,1... | collective-permute-start | bytes 786440 | tf_op jit(solution)/shard_map/ppermute | solution.py:43
  120.7 27.9 %all-to-all-start.4 = ((bf16[16,8,128]{2,1,0:T(8,128)(2,1)}), bf16[16,8,128]{2,1,0:T(8,128)(2,1)S(1)}, u32[]{:S(2)}, u32[]{:S(2)}) async-start(bf16[16,8,128]{2,1,0:T(8,128)(2,1)} %bitcast.10), calls=%async_computation.4 | async-start | bytes 65536 | tf_op jit(solution)/shard_map/all_to_all | solution.py:32
  127.5 29.0 %collective-permute-start.3 = (bf16[16,64,128]{2,1,0:T(8,128)(2,1)S(1)}, bf16[16,64,128]{2,1,0:T(8,128)(2,1)S(1)}, u32[]{:S(2)}, u32[]{:S(2)}) collective-permute-start(bf16[16,64,128]{2,1,0:T(8,128)(2,1)S(1)} %get-tuple-element.13.refs_0_), channel_id=1, source_target_pairs={{0,8},{1,9},{2,10},{3,11},{4,12},{5,13},{6,14},{7,15},{8,16},{9,17... | collective-permute-start | bytes 786440 | tf_op jit(solution)/shard_map/ppermute | solution.py:43
  130.7 25.7 %collective-permute-start.2 = (bf16[16,64,128]{2,1,0:T(8,128)(2,1)S(1)}, bf16[16,64,128]{2,1,0:T(8,128)(2,1)S(1)}, u32[]{:S(2)}, u32[]{:S(2)}) collective-permute-start(bf16[16,64,128]{2,1,0:T(8,128)(2,1)S(1)} %collective-permute-done.1.refs_1_), channel_id=1, source_target_pairs={{0,24},{1,25},{2,26},{3,27},{4,28},{5,29},{6,30},{7,31},{8,0},{9,1... | collective-permute-start | bytes 786440 | tf_op jit(solution)/shard_map/ppermute | solution.py:43
  134.1 22.4 %collective-permute-start.6 = (bf16[16,64,128]{2,1,0:T(8,128)(2,1)S(1)}, bf16[16,64,128]{2,1,0:T(8,128)(2,1)S(1)}, u32[]{:S(2)}, u32[]{:S(2)}) collective-permute-start(bf16[16,64,128]{2,1,0:T(8,128)(2,1)S(1)} %get-tuple-element.14.refs_4_), channel_id=1, source_target_pairs={{0,8},{1,9},{2,10},{3,11},{4,12},{5,13},{6,14},{7,15},{8,16},{9,17... | collective-permute-start | bytes 786440 | tf_op jit(solution)/shard_map/ppermute | solution.py:43
  136.0 20.5 %collective-permute-start.5 = (bf16[16,64,128]{2,1,0:T(8,128)(2,1)S(1)}, bf16[16,64,128]{2,1,0:T(8,128)(2,1)S(1)}, u32[]{:S(2)}, u32[]{:S(2)}) collective-permute-start(bf16[16,64,128]{2,1,0:T(8,128)(2,1)S(1)} %get-tuple-element.14.refs_4_), channel_id=1, source_target_pairs={{0,16},{1,17},{2,18},{3,19},{4,20},{5,21},{6,22},{7,23},{8,24},{9,... | collective-permute-start | bytes 786440 | tf_op jit(solution)/shard_map/ppermute | solution.py:43
  140.5 15.9 %collective-permute-start.4 = (bf16[16,64,128]{2,1,0:T(8,128)(2,1)S(1)}, bf16[16,64,128]{2,1,0:T(8,128)(2,1)S(1)}, u32[]{:S(2)}, u32[]{:S(2)}) collective-permute-start(bf16[16,64,128]{2,1,0:T(8,128)(2,1)S(1)} %get-tuple-element.14.refs_4_), channel_id=1, source_target_pairs={{0,24},{1,25},{2,26},{3,27},{4,28},{5,29},{6,30},{7,31},{8,0},{9,1... | collective-permute-start | bytes 786440 | tf_op jit(solution)/shard_map/ppermute | solution.py:43
  149.3 13.6 %all-to-all-start.5 = ((bf16[8,16,8,128]{3,2,1,0:T(8,128)(2,1)}), bf16[8,16,8,128]{3,2,1,0:T(8,128)(2,1)S(1)}, u32[]{:S(2)}, u32[]{:S(2)}) async-start(bf16[8,16,8,128]{3,2,1,0:T(8,128)(2,1)} %broadcast_in_dim.10), calls=%async_computation.5 | async-start | bytes 524288 | tf_op jit(solution)/shard_map/all_to_all | solution.py:32

commit v9 on v8

--- a/solution.py
+++ b/solution.py
@@ -88,7 +88,7 @@
             tile[WEIGHT_AT:SENT, :] = extra_ref[0:COLUMNS, lanes]
 
 
-DOCS_AT = 2 * ROWS
+DOCS_AT = ROWS
 COLUMNS_AT = DOCS_AT + 16
 GATHERED = COLUMNS_AT + 2 * COLUMNS
 
@@ -110,16 +110,28 @@
     query_ref[0:ROWS, :] = queries
     query_ref[ROWS : ROWS + 16, :] = docs
     for s in range(key_ref.shape[0]):
-        key_ref[s, 0:ROWS, :] = keys
-        key_ref[s, ROWS:DOCS_AT, :] = values
+        key_ref[s, 0:ROWS, :] = (keys, values)[s % 2]
         key_ref[s, DOCS_AT:COLUMNS_AT, :] = docs
         for k in range(2):
             at = COLUMNS_AT + k * COLUMNS
             key_ref[s, at : at + COLUMNS, :] = came_ref[2 * (s % 8) + k, WEIGHT_AT:SENT, :]
 
 
-def attend_kernel(place_ref, query_ref, key_ref, out_ref, score_ref):
+def attend_kernel(
+    place_ref, query_ref, key_ref, swapped_ref, out_ref, score_ref, keys_ref, values_ref
+):
     z2, y, x, c = (place_ref[k] for k in range(4))
+
+    @pl.when(c == 0)
+    def _():
+        keys_ref[...] = key_ref[:, 0:ROWS, :]
+        values_ref[...] = swapped_ref[...]
+
+    @pl.when(c != 0)
+    def _():
+        keys_ref[...] = swapped_ref[...]
+        values_ref[...] = key_ref[:, 0:ROWS, :]
+
     stripe = 2 * BLOCK * 4
 
     def positions(z2, y, x, c, dim):
@@ -148,7 +160,7 @@
         for s in range(sources):
             scores = lax.dot_general(
                 queries,
-                key_ref[s, 0:ROWS, :],
+                keys_ref[s],
                 (((1,), (1,)), ((), ())),
                 preferred_element_type=jnp.float32,
             )
@@ -166,7 +178,7 @@
                 weight = jnp.exp2((score_ref[k] - row_max) * FACTOR)
                 total = total + weight
                 weights.append(weight.astype(jnp.bfloat16))
-                values.append(key_ref[k, ROWS:DOCS_AT, :])
+                values.append(values_ref[k])
             mixed = mixed + jnp.dot(
                 jnp.concatenate(weights, axis=1),
                 jnp.concatenate(values, axis=0),
@@ -182,8 +194,9 @@
             out_ref[r, ROWS : ROWS + 16, :] = stats.astype(jnp.bfloat16)
 
 
-def columns_kernel(key_ref, after_ref, out_ref):
+def columns_kernel(key_ref, after_ref, out_ref, half_ref):
     out_ref[...] = key_ref[:, COLUMNS_AT:GATHERED, :]
+    half_ref[...] = key_ref[:, 0:ROWS, :]
 
 
 def combine_kernel(part_ref, own_ref, other_ref, out_ref, same_own_ref, same_other_ref):
@@ -269,24 +282,31 @@
     keys = exchange(keys, KEY_AXES)
     queries = lax.all_gather(queries, QUERY_AXES)
 
+    held = jax.ShapeDtypeStruct((sources, GATHERED - COLUMNS_AT, LANES), bf16)
+    half = jax.ShapeDtypeStruct((sources, ROWS, LANES), bf16)
+    own, half = call(
+        columns_kernel, [held, half], [VMEM, pl.BlockSpec(memory_space=pl.ANY)], "columns"
+    )(keys, queries)
+    swapped = moved(half, lambda z, y, x, c: (z, y, x, 1 - c))
+
     parts = call(
         attend_kernel,
         jax.ShapeDtypeStruct((spread, ROWS + 16, LANES), bf16),
-        [SMEM] + [VMEM] * 2,
+        [SMEM] + [VMEM] * 3,
         "attend",
-        [pltpu.VMEM((sources, 2 * ROWS, LANES), f32)],
+        [
+            pltpu.VMEM((sources, 2 * ROWS, LANES), f32),
+            pltpu.VMEM((sources, ROWS, LANES), bf16),
+            pltpu.VMEM((sources, ROWS, LANES), bf16),
+        ],
         4 * spread * ROWS * sources * ROWS * HEAD_DIM,
         2 << 20,
-    )(place, queries, keys)
+    )(place, queries, keys, swapped)
     parts = exchange(parts, QUERY_AXES)
 
     def from_y(block, k):
         return moved(block, lambda z, y, x, c: (z, (y - k) % 4, x, c))
 
-    held = jax.ShapeDtypeStruct((sources, GATHERED - COLUMNS_AT, LANES), bf16)
-    own = call(columns_kernel, held, [VMEM, pl.BlockSpec(memory_space=pl.ANY)], "columns")(
-        keys, queries
-    )
     other = moved(own, lambda z, y, x, c: (z ^ 2, y, x, c))
     next_own = from_y(own, 1)
     attended, own, other = call(

time: 166 us -> 162 us (0.976)
  waiting for transfers between devices: 24.1 us -> 19.6 us
    all_to_all x5, waiting for transfers between devices: 24 us -> 19 us  [exchange(): return lax.all_to_all(tiles, axes, split_axis=0, concat_axis=0, tiled=True)]
    ppermute x7 -> x8, starting transfers between devices: 28.2 us -> 30.4 us  [moved(): lax.ppermute(block, names, [(flat(*p), flat(*where(*p))) for p in places])]
  transfers between devices with their start and end apart: 12 -> 13, of which waited for: 5 -> 7; matrix products, arithmetic and copies ran while one was open for 2% -> 1% of each run, Pallas kernels for 2% -> 3%
where the time goes in v9:
time: 162 us; the launch traced here: 161 us
  starting transfers between devices  79.7 us (49%)
  blocking collectives  51 us (31%)
  waiting for transfers between devices  19.6 us (12%)
  Pallas kernels  7.28 us (4%)
    all_to_all x5, starting transfers between devices, exchange(): return lax.all_to_all(tiles, axes, split_axis=0, concat_axis=0, tiled=True)  49.3 us
    all_to_all x1, blocking collectives, exchange(): return lax.all_to_all(tiles, axes, split_axis=0, concat_axis=0, tiled=True)  40.5 us
    ppermute x8, starting transfers between devices, moved(): lax.ppermute(block, names, [(flat(*p), flat(*where(*p))) for p in places])  30.4 us
    all_to_all x5, waiting for transfers between devices, exchange(): return lax.all_to_all(tiles, axes, split_axis=0, concat_axis=0, tiled=True)  19 us
    all_gather x1, blocking collectives, shards(): queries = lax.all_gather(queries, QUERY_AXES)  10.6 us
    pallas_call x1, Pallas kernels, shards(): call(attend_kernel, jax.ShapeDtypeStruct((spread, ROWS + 16, LANES), bf16...  3.38 us
  transfers between devices with their start and end apart: 13, of which 7 were waited for; matrix products, arithmetic and copies ran while one was open for 1% of the time, Pallas kernels for 3%

profile of v9, /device:TPU:1, one launch (start us, length us, event | category | flops | bytes accessed | tf_op | source)
XLA Modules:
  0.0 160.9 jit_solution(12488755509288277828)
XLA Ops:
  0.0 1.4 pad_maximum_fusion
  1.4 17.4 %all-to-all-start = ((bf16[8,24,256]{2,1,0:T(8,128)(2,1)}), bf16[8,24,256]{2,1,0:T(8,128)(2,1)S(1)}, u32[]{:S(2)}, u32[]{:S(2)}) async-start(bf16[8,24,256]{2,1,0:T(8,128)(2,1)} %pad_maximum_fusion), calls=%async_computation | async-start | bytes 196608 | tf_op jit(solution)/shard_map/all_to_all | solution.py:32
  18.8 0.0 copy-start.2
  18.8 0.0 copy-start.1
  18.9 0.7 copy-done.2
  19.5 0.1 pad_add_fusion
  19.6 0.1 dynamic-slice_convert_fusion
  19.7 0.1 tile.10
  19.8 0.0 copy-done.1
  19.8 4.1 %all-to-all-done.rows_ref = bf16[8,24,256]{2,1,0:T(8,128)(2,1)S(1)} async-done(((bf16[8,24,256]{2,1,0:T(8,128)(2,1)}), bf16[8,24,256]{2,1,0:T(8,128)(2,1)S(1)}, u32[]{:S(2)}, u32[]{:S(2)}) %all-to-all-start) | async-done | bytes 98336 | tf_op jit(solution)/shard_map/all_to_all | solution.py:32
  23.9 40.5 %all_to_all.30.came_ref = bf16[16,64,128]{2,1,0:T(8,128)(2,1)S(1)} all-to-all(bf16[16,64,128]{2,1,0:T(8,128)(2,1)S(1)} %send.1), channel_id=1, replica_groups=mesh['zh'=8,'zp'=2,'z2'=2,'y'=4,'x'=4,'c'=2] {'zh','zp'}, dimensions={0} | all-to-all | bytes 524288 | tf_op jit(solution)/shard_map/all_to_all | solution.py:32
  64.4 1.0 spread.1
  65.4 14.6 %all-to-all-start.2 = ((bf16[16,208,128]{2,1,0:T(8,128)(2,1)}), bf16[16,208,128]{2,1,0:T(8,128)(2,1)S(1)}, u32[]{:S(2)}, u32[]{:S(2)}) async-start(bf16[16,208,128]{2,1,0:T(8,128)(2,1)} %get-tuple-element.13), calls=%async_computation.2 | async-start | bytes 1703936 | tf_op jit(solution)/shard_map/all_to_all | solution.py:32
  79.9 10.6 %all-gather = bf16[576,128]{1,0:T(8,128)(2,1)S(1)} all-gather(bf16[144,128]{1,0:T(8,128)(2,1)S(1)} %get-tuple-element.12), channel_id=2, replica_groups=mesh['zh'=8,'zp'=2,'z2'=2,'y'=4,'x'=4,'c'=2] {'y'}, dimensions={0}, use_global_device_ids=true | all-gather | bytes 184320 | tf_op jit(solution)/shard_map/all_gather | solution.py:283
  90.5 3.1 %all-to-all-done.2.key_ref = bf16[16,208,128]{2,1,0:T(8,128)(2,1)S(1)} async-done(((bf16[16,208,128]{2,1,0:T(8,128)(2,1)}), bf16[16,208,128]{2,1,0:T(8,128)(2,1)S(1)}, u32[]{:S(2)}, u32[]{:S(2)}) %all-to-all-start.2) | async-done | bytes 852000 | tf_op jit(solution)/shard_map/all_to_all | solution.py:32
  93.6 0.1 columns.1
  93.7 2.8 %collective-permute-start = (bf16[16,128,128]{2,1,0:T(8,128)(2,1)S(1)}, bf16[16,128,128]{2,1,0:T(8,128)(2,1)S(1)}, u32[]{:S(2)}, u32[]{:S(2)}) collective-permute-start(bf16[16,128,128]{2,1,0:T(8,128)(2,1)S(1)} %get-tuple-element.14), channel_id=1, source_target_pairs={{0,1},{1,0},{2,3},{3,2},{4,5},{5,4},{6,7},{7,6},{8,9},{9,8},{10,11... | collective-permute-start | bytes 1572872 | tf_op jit(solution)/shard_map/ppermute | solution.py:43
  96.5 7.5 %collective-permute-start.1 = (bf16[16,64,128]{2,1,0:T(8,128)(2,1)S(1)}, bf16[16,64,128]{2,1,0:T(8,128)(2,1)S(1)}, u32[]{:S(2)}, u32[]{:S(2)}) collective-permute-start(bf16[16,64,128]{2,1,0:T(8,128)(2,1)S(1)} %get-tuple-element.15.own_ref), channel_id=1, source_target_pairs={{0,64},{1,65},{2,66},{3,67},{4,68},{5,69},{6,70},{7,71},{8,72},{9,... | collective-permute-start | bytes 786440 | tf_op jit(solution)/shard_map/ppermute | solution.py:43
  104.0 0.1 stack.23.place_ref
  104.1 0.0 collective-permute-done.swapped_ref
  104.1 3.4 %attend.1 = bf16[4,144,128]{2,1,0:T(8,128)(2,1)} custom-call(s32[5]{0:T(128)S(1)} %stack.23.place_ref, bf16[4,144,128]{2,1,0:T(8,128)(2,1)S(1)} %bitcast.12, bf16[16,208,128]{2,1,0:T(8,128)(2,1)S(1)} %all-to-all-done.2.key_ref, bf16[16,128,128]{2,1,0:T(8,128)(2,1)S(1)} %collective-permute-done.swapped_ref), custom_call_target="tpu_custom_call" | custom-call | flops 536870912 | bytes 2097152 | tf_op jit(solution)/shard_map/attend/pallas_call | solution.py:292
  107.5 4.2 %all-to-all-start.3 = ((bf16[4,144,128]{2,1,0:T(8,128)(2,1)}), bf16[4,144,128]{2,1,0:T(8,128)(2,1)S(1)}, u32[]{:S(2)}, u32[]{:S(2)}) async-start(bf16[4,144,128]{2,1,0:T(8,128)(2,1)} %attend.1), calls=%async_computation.3 | async-start | bytes 294912 | tf_op jit(solution)/shard_map/all_to_all | solution.py:32
  111.7 4.6 %collective-permute-start.2 = (bf16[16,64,128]{2,1,0:T(8,128)(2,1)S(1)}, bf16[16,64,128]{2,1,0:T(8,128)(2,1)S(1)}, u32[]{:S(2)}, u32[]{:S(2)}) collective-permute-start(bf16[16,64,128]{2,1,0:T(8,128)(2,1)S(1)} %get-tuple-element.15.own_ref), channel_id=1, source_target_pairs={{0,24},{1,25},{2,26},{3,27},{4,28},{5,29},{6,30},{7,31},{8,0},{9,1... | collective-permute-start | bytes 786440 | tf_op jit(solution)/shard_map/ppermute | solution.py:43
  116.3 0.1 collective-permute-done.1.other_ref
  116.4 0.2 all-to-all-done.3.part_ref
  116.6 0.8 combine.1
  117.4 7.0 %all-to-all-start.4 = ((bf16[16,8,128]{2,1,0:T(8,128)(2,1)}), bf16[16,8,128]{2,1,0:T(8,128)(2,1)S(1)}, u32[]{:S(2)}, u32[]{:S(2)}) async-start(bf16[16,8,128]{2,1,0:T(8,128)(2,1)} %bitcast.10), calls=%async_computation.4 | async-start | bytes 65536 | tf_op jit(solution)/shard_map/all_to_all | solution.py:32
  124.4 0.0 collective-permute-done.2.refs_1_
  124.4 4.6 %collective-permute-start.3 = (bf16[16,64,128]{2,1,0:T(8,128)(2,1)S(1)}, bf16[16,64,128]{2,1,0:T(8,128)(2,1)S(1)}, u32[]{:S(2)}, u32[]{:S(2)}) collective-permute-start(bf16[16,64,128]{2,1,0:T(8,128)(2,1)S(1)} %collective-permute-done.2.refs_1_), channel_id=1, source_target_pairs={{0,24},{1,25},{2,26},{3,27},{4,28},{5,29},{6,30},{7,31},{8,0},{9,1... | collective-permute-start | bytes 786440 | tf_op jit(solution)/shard_map/ppermute | solution.py:43
  129.0 1.9 %collective-permute-start.4 = (bf16[16,64,128]{2,1,0:T(8,128)(2,1)S(1)}, bf16[16,64,128]{2,1,0:T(8,128)(2,1)S(1)}, u32[]{:S(2)}, u32[]{:S(2)}) collective-permute-start(bf16[16,64,128]{2,1,0:T(8,128)(2,1)S(1)} %get-tuple-element.17.refs_0_), channel_id=1, source_target_pairs={{0,8},{1,9},{2,10},{3,11},{4,12},{5,13},{6,14},{7,15},{8,16},{9,17... | collective-permute-start | bytes 786440 | tf_op jit(solution)/shard_map/ppermute | solution.py:43
  130.9 4.6 %collective-permute-start.5 = (bf16[16,64,128]{2,1,0:T(8,128)(2,1)S(1)}, bf16[16,64,128]{2,1,0:T(8,128)(2,1)S(1)}, u32[]{:S(2)}, u32[]{:S(2)}) collective-permute-start(bf16[16,64,128]{2,1,0:T(8,128)(2,1)S(1)} %get-tuple-element.18.refs_4_), channel_id=1, source_target_pairs={{0,24},{1,25},{2,26},{3,27},{4,28},{5,29},{6,30},{7,31},{8,0},{9,1... | collective-permute-start | bytes 786440 | tf_op jit(solution)/shard_map/ppermute | solution.py:43
  135.5 1.9 %collective-permute-start.6 = (bf16[16,64,128]{2,1,0:T(8,128)(2,1)S(1)}, bf16[16,64,128]{2,1,0:T(8,128)(2,1)S(1)}, u32[]{:S(2)}, u32[]{:S(2)}) collective-permute-start(bf16[16,64,128]{2,1,0:T(8,128)(2,1)S(1)} %get-tuple-element.18.refs_4_), channel_id=1, source_target_pairs={{0,16},{1,17},{2,18},{3,19},{4,20},{5,21},{6,22},{7,23},{8,24},{9,... | collective-permute-start | bytes 786440 | tf_op jit(solution)/shard_map/ppermute | solution.py:43
  137.5 2.5 %collective-permute-start.7 = (bf16[16,64,128]{2,1,0:T(8,128)(2,1)S(1)}, bf16[16,64,128]{2,1,0:T(8,128)(2,1)S(1)}, u32[]{:S(2)}, u32[]{:S(2)}) collective-permute-start(bf16[16,64,128]{2,1,0:T(8,128)(2,1)S(1)} %get-tuple-element.18.refs_4_), channel_id=1, source_target_pairs={{0,8},{1,9},{2,10},{3,11},{4,12},{5,13},{6,14},{7,15},{8,16},{9,17... | collective-permute-start | bytes 786440 | tf_op jit(solution)/shard_map/ppermute | solution.py:43
  139.9 5.5 %all-to-all-done.4 = bf16[16,8,128]{2,1,0:T(8,128)(2,1)S(1)} async-done(((bf16[16,8,128]{2,1,0:T(8,128)(2,1)}), bf16[16,8,128]{2,1,0:T(8,128)(2,1)S(1)}, u32[]{:S(2)}, u32[]{:S(2)}) %all-to-all-start.4) | async-done | bytes 32800 | tf_op jit(solution)/shard_map/all_to_all | solution.py:32
  145.5 0.7 broadcast_in_dim.10
  146.2 0.0 copy-start
  146.2 6.2 %all-to-all-start.5 = ((bf16[8,16,8,128]{3,2,1,0:T(8,128)(2,1)}), bf16[8,16,8,128]{3,2,1,0:T(8,128)(2,1)S(1)}, u32[]{:S(2)}, u32[]{:S(2)}) async-start(bf16[8,16,8,128]{3,2,1,0:T(8,128)(2,1)} %broadcast_in_dim.10), calls=%async_computation.5 | async-start | bytes 524288 | tf_op jit(solution)/shard_map/all_to_all | solution.py:32
  152.4 0.0 collective-permute-done.3.refs_2_
  152.4 0.0 collective-permute-done.4.refs_3_
  152.4 0.0 collective-permute-done.5.refs_5_
  152.4 0.0 collective-permute-done.6.refs_6_
  152.4 0.4 collective-permute-done.7.refs_7_
  152.8 6.1 %all-to-all-done.5.attended_ref = bf16[8,16,8,128]{3,2,1,0:T(8,128)(2,1)S(1)} async-done(((bf16[8,16,8,128]{3,2,1,0:T(8,128)(2,1)}), bf16[8,16,8,128]{3,2,1,0:T(8,128)(2,1)S(1)}, u32[]{:S(2)}, u32[]{:S(2)}) %all-to-all-start.5) | async-done | bytes 262176 | tf_op jit(solution)/shard_map/all_to_all | solution.py:32
  158.9 0.0 copy-done
  158.9 2.0 %product.1 = bf16[64,512]{1,0:T(8,128)(2,1)} custom-call(s32[5]{0:T(128)S(1)} %stack.23.place_ref, bf16[8,16,8,128]{3,2,1,0:T(8,128)(2,1)S(1)} %all-to-all-done.5.attended_ref, bf16[16,64,128]{2,1,0:T(8,128)(2,1)S(1)} %get-tuple-element.17.refs_0_, bf16[16,64,128]{2,1,0:T(8,128)(2,1)S(1)} %collective-permute-done.2.refs_1_, ...), custom_call_target="tpu_custom_call" | custom-call | flops 134217728 | bytes 3145728 | tf_op jit(solution)/shard_map/product/pallas_call | solution.py:323
  (4 shorter events, 0.1 us)
Async XLA Ops:
  1.4 22.4 %all-to-all-start = ((bf16[8,24,256]{2,1,0:T(8,128)(2,1)}), bf16[8,24,256]{2,1,0:T(8,128)(2,1)S(1)}, u32[]{:S(2)}, u32[]{:S(2)}) async-start(bf16[8,24,256]{2,1,0:T(8,128)(2,1)} %pad_maximum_fusion), calls=%async_computation | async-start | bytes 196608 | tf_op jit(solution)/shard_map/all_to_all | solution.py:32
  18.8 0.7 copy-start.2
  18.8 0.9 copy-start.1
  65.4 28.3 %all-to-all-start.2 = ((bf16[16,208,128]{2,1,0:T(8,128)(2,1)}), bf16[16,208,128]{2,1,0:T(8,128)(2,1)S(1)}, u32[]{:S(2)}, u32[]{:S(2)}) async-start(bf16[16,208,128]{2,1,0:T(8,128)(2,1)} %get-tuple-element.13), calls=%async_computation.2 | async-start | bytes 1703936 | tf_op jit(solution)/shard_map/all_to_all | solution.py:32
  93.7 10.4 %collective-permute-start = (bf16[16,128,128]{2,1,0:T(8,128)(2,1)S(1)}, bf16[16,128,128]{2,1,0:T(8,128)(2,1)S(1)}, u32[]{:S(2)}, u32[]{:S(2)}) collective-permute-start(bf16[16,128,128]{2,1,0:T(8,128)(2,1)S(1)} %get-tuple-element.14), channel_id=1, source_target_pairs={{0,1},{1,0},{2,3},{3,2},{4,5},{5,4},{6,7},{7,6},{8,9},{9,8},{10,11... | collective-permute-start | bytes 1572872 | tf_op jit(solution)/shard_map/ppermute | solution.py:43
  96.5 19.9 %collective-permute-start.1 = (bf16[16,64,128]{2,1,0:T(8,128)(2,1)S(1)}, bf16[16,64,128]{2,1,0:T(8,128)(2,1)S(1)}, u32[]{:S(2)}, u32[]{:S(2)}) collective-permute-start(bf16[16,64,128]{2,1,0:T(8,128)(2,1)S(1)} %get-tuple-element.15.own_ref), channel_id=1, source_target_pairs={{0,64},{1,65},{2,66},{3,67},{4,68},{5,69},{6,70},{7,71},{8,72},{9,... | collective-permute-start | bytes 786440 | tf_op jit(solution)/shard_map/ppermute | solution.py:43
  107.5 9.1 %all-to-all-start.3 = ((bf16[4,144,128]{2,1,0:T(8,128)(2,1)}), bf16[4,144,128]{2,1,0:T(8,128)(2,1)S(1)}, u32[]{:S(2)}, u32[]{:S(2)}) async-start(bf16[4,144,128]{2,1,0:T(8,128)(2,1)} %attend.1), calls=%async_computation.3 | async-start | bytes 294912 | tf_op jit(solution)/shard_map/all_to_all | solution.py:32
  111.7 12.7 %collective-permute-start.2 = (bf16[16,64,128]{2,1,0:T(8,128)(2,1)S(1)}, bf16[16,64,128]{2,1,0:T(8,128)(2,1)S(1)}, u32[]{:S(2)}, u32[]{:S(2)}) collective-permute-start(bf16[16,64,128]{2,1,0:T(8,128)(2,1)S(1)} %get-tuple-element.15.own_ref), channel_id=1, source_target_pairs={{0,24},{1,25},{2,26},{3,27},{4,28},{5,29},{6,30},{7,31},{8,0},{9,1... | collective-permute-start | bytes 786440 | tf_op jit(solution)/shard_map/ppermute | solution.py:43
  117.4 28.1 %all-to-all-start.4 = ((bf16[16,8,128]{2,1,0:T(8,128)(2,1)}), bf16[16,8,128]{2,1,0:T(8,128)(2,1)S(1)}, u32[]{:S(2)}, u32[]{:S(2)}) async-start(bf16[16,8,128]{2,1,0:T(8,128)(2,1)} %bitcast.10), calls=%async_computation.4 | async-start | bytes 65536 | tf_op jit(solution)/shard_map/all_to_all | solution.py:32
  124.4 28.0 %collective-permute-start.3 = (bf16[16,64,128]{2,1,0:T(8,128)(2,1)S(1)}, bf16[16,64,128]{2,1,0:T(8,128)(2,1)S(1)}, u32[]{:S(2)}, u32[]{:S(2)}) collective-permute-start(bf16[16,64,128]{2,1,0:T(8,128)(2,1)S(1)} %collective-permute-done.2.refs_1_), channel_id=1, source_target_pairs={{0,24},{1,25},{2,26},{3,27},{4,28},{5,29},{6,30},{7,31},{8,0},{9,1... | collective-permute-start | bytes 786440 | tf_op jit(solution)/shard_map/ppermute | solution.py:43
  129.0 23.4 %collective-permute-start.4 = (bf16[16,64,128]{2,1,0:T(8,128)(2,1)S(1)}, bf16[16,64,128]{2,1,0:T(8,128)(2,1)S(1)}, u32[]{:S(2)}, u32[]{:S(2)}) collective-permute-start(bf16[16,64,128]{2,1,0:T(8,128)(2,1)S(1)} %get-tuple-element.17.refs_0_), channel_id=1, source_target_pairs={{0,8},{1,9},{2,10},{3,11},{4,12},{5,13},{6,14},{7,15},{8,16},{9,17... | collective-permute-start | bytes 786440 | tf_op jit(solution)/shard_map/ppermute | solution.py:43
  130.9 21.4 %collective-permute-start.5 = (bf16[16,64,128]{2,1,0:T(8,128)(2,1)S(1)}, bf16[16,64,128]{2,1,0:T(8,128)(2,1)S(1)}, u32[]{:S(2)}, u32[]{:S(2)}) collective-permute-start(bf16[16,64,128]{2,1,0:T(8,128)(2,1)S(1)} %get-tuple-element.18.refs_4_), channel_id=1, source_target_pairs={{0,24},{1,25},{2,26},{3,27},{4,28},{5,29},{6,30},{7,31},{8,0},{9,1... | collective-permute-start | bytes 786440 | tf_op jit(solution)/shard_map/ppermute | solution.py:43
  135.5 16.9 %collective-permute-start.6 = (bf16[16,64,128]{2,1,0:T(8,128)(2,1)S(1)}, bf16[16,64,128]{2,1,0:T(8,128)(2,1)S(1)}, u32[]{:S(2)}, u32[]{:S(2)}) collective-permute-start(bf16[16,64,128]{2,1,0:T(8,128)(2,1)S(1)} %get-tuple-element.18.refs_4_), channel_id=1, source_target_pairs={{0,16},{1,17},{2,18},{3,19},{4,20},{5,21},{6,22},{7,23},{8,24},{9,... | collective-permute-start | bytes 786440 | tf_op jit(solution)/shard_map/ppermute | solution.py:43
  137.5 15.3 %collective-permute-start.7 = (bf16[16,64,128]{2,1,0:T(8,128)(2,1)S(1)}, bf16[16,64,128]{2,1,0:T(8,128)(2,1)S(1)}, u32[]{:S(2)}, u32[]{:S(2)}) collective-permute-start(bf16[16,64,128]{2,1,0:T(8,128)(2,1)S(1)} %get-tuple-element.18.refs_4_), channel_id=1, source_target_pairs={{0,8},{1,9},{2,10},{3,11},{4,12},{5,13},{6,14},{7,15},{8,16},{9,17... | collective-permute-start | bytes 786440 | tf_op jit(solution)/shard_map/ppermute | solution.py:43
  146.2 12.7 %copy-start = (bf16[64,512]{1,0:T(8,128)(2,1)S(1)}, bf16[64,512]{1,0:T(8,128)(2,1)}, u32[]{:S(2)}) copy-start(bf16[64,512]{1,0:T(8,128)(2,1)} %refs_8_.1) | copy-start | bytes 196612
  146.2 12.7 %all-to-all-start.5 = ((bf16[8,16,8,128]{3,2,1,0:T(8,128)(2,1)}), bf16[8,16,8,128]{3,2,1,0:T(8,128)(2,1)S(1)}, u32[]{:S(2)}, u32[]{:S(2)}) async-start(bf16[8,16,8,128]{3,2,1,0:T(8,128)(2,1)} %broadcast_in_dim.10), calls=%async_computation.5 | async-start | bytes 524288 | tf_op jit(solution)/shard_map/all_to_all | solution.py:32

commit v10 on v9

--- a/solution.py
+++ b/solution.py
@@ -199,9 +199,12 @@
     half_ref[...] = key_ref[:, 0:ROWS, :]
 
 
-def combine_kernel(part_ref, own_ref, other_ref, out_ref, same_own_ref, same_other_ref):
+def after_kernel(block_ref, after_ref, out_ref):
+    out_ref[...] = block_ref[...]
+
+
+def combine_kernel(part_ref, own_ref, out_ref, same_own_ref):
     same_own_ref[...] = own_ref[...]
-    same_other_ref[...] = other_ref[...]
     parts = part_ref.shape[0]
     stats = [part_ref[r, ROWS : ROWS + 16, :].astype(jnp.float32) for r in range(parts)]
     maxima = [t[0:1] + t[1:2] + t[2:3] for t in stats]
@@ -309,12 +312,15 @@
 
     other = moved(own, lambda z, y, x, c: (z ^ 2, y, x, c))
     next_own = from_y(own, 1)
-    attended, own, other = call(
+    attended, own = call(
         combine_kernel,
-        [jax.ShapeDtypeStruct((ROWS, HEAD_DIM), bf16), held, held],
-        [VMEM] * 3,
+        [jax.ShapeDtypeStruct((ROWS, HEAD_DIM), bf16), held],
+        [VMEM] * 2,
         "combine",
-    )(parts, own, other)
+    )(parts, own)
+    other = call(after_kernel, held, [VMEM, pl.BlockSpec(memory_space=pl.ANY)], "after")(
+        other, attended
+    )
     weights = [own, next_own, from_y(next_own, 1), from_y(own, 3)]
     weights += [other] + [from_y(other, k) for k in (1, 2, 3)]
 

time: 162 us -> 163 us (level)
  waiting for transfers between devices: 19.6 us -> 22.6 us
  starting transfers between devices: 79.7 us -> 77.7 us
    ppermute x8, waiting for transfers between devices: 0.53 us -> 6.17 us  [moved(): lax.ppermute(block, names, [(flat(*p), flat(*where(*p))) for p in places])]
    all_to_all x5, waiting for transfers between devices: 19 us -> 16.5 us  [exchange(): return lax.all_to_all(tiles, axes, split_axis=0, concat_axis=0, tiled=True)]
    ppermute x8, starting transfers between devices: 30.4 us -> 28.2 us  [moved(): lax.ppermute(block, names, [(flat(*p), flat(*where(*p))) for p in places])]
  transfers between devices with their start and end apart: 13 -> 13, of which waited for: 7 -> 7; matrix products, arithmetic and copies ran while one was open for 1% -> 1% of each run, Pallas kernels for 3% -> 0%
where the time goes in v10:
time: 163 us; the launch traced here: 162 us
  starting transfers between devices  77.7 us (48%)
  blocking collectives  51 us (31%)
  waiting for transfers between devices  22.6 us (14%)
  Pallas kernels  7.3 us (4%)
    all_to_all x5, starting transfers between devices, exchange(): return lax.all_to_all(tiles, axes, split_axis=0, concat_axis=0, tiled=True)  49.4 us
    all_to_all x1, blocking collectives, exchange(): return lax.all_to_all(tiles, axes, split_axis=0, concat_axis=0, tiled=True)  40.5 us
    ppermute x8, starting transfers between devices, moved(): lax.ppermute(block, names, [(flat(*p), flat(*where(*p))) for p in places])  28.2 us
    all_to_all x5, waiting for transfers between devices, exchange(): return lax.all_to_all(tiles, axes, split_axis=0, concat_axis=0, tiled=True)  16.5 us
    all_gather x1, blocking collectives, shards(): queries = lax.all_gather(queries, QUERY_AXES)  10.6 us
    ppermute x8, waiting for transfers between devices, moved(): lax.ppermute(block, names, [(flat(*p), flat(*where(*p))) for p in places])  6.17 us
    pallas_call x1, Pallas kernels, shards(): call(attend_kernel, jax.ShapeDtypeStruct((spread, ROWS + 16, LANES), bf16...  3.38 us
  transfers between devices with their start and end apart: 13, of which 7 were waited for; matrix products, arithmetic and copies ran while one was open for 1% of the time, Pallas kernels for 0%

profile of v10, /device:TPU:1, one launch (start us, length us, event | category | flops | bytes accessed | tf_op | source)
XLA Modules:
  0.0 161.9 jit_solution(5298366953373357401)
XLA Ops:
  0.0 1.4 pad_maximum_fusion
  1.4 17.4 %all-to-all-start = ((bf16[8,24,256]{2,1,0:T(8,128)(2,1)}), bf16[8,24,256]{2,1,0:T(8,128)(2,1)S(1)}, u32[]{:S(2)}, u32[]{:S(2)}) async-start(bf16[8,24,256]{2,1,0:T(8,128)(2,1)} %pad_maximum_fusion), calls=%async_computation | async-start | bytes 196608 | tf_op jit(solution)/shard_map/all_to_all | solution.py:32
  18.8 0.0 copy-start.2
  18.8 0.0 copy-start.1
  18.9 0.7 copy-done.2
  19.5 0.1 pad_add_fusion
  19.6 0.1 dynamic-slice_convert_fusion
  19.7 0.1 tile.10
  19.8 0.0 copy-done.1
  19.8 4.1 %all-to-all-done.rows_ref = bf16[8,24,256]{2,1,0:T(8,128)(2,1)S(1)} async-done(((bf16[8,24,256]{2,1,0:T(8,128)(2,1)}), bf16[8,24,256]{2,1,0:T(8,128)(2,1)S(1)}, u32[]{:S(2)}, u32[]{:S(2)}) %all-to-all-start) | async-done | bytes 98336 | tf_op jit(solution)/shard_map/all_to_all | solution.py:32
  23.9 40.5 %all_to_all.30.came_ref = bf16[16,64,128]{2,1,0:T(8,128)(2,1)S(1)} all-to-all(bf16[16,64,128]{2,1,0:T(8,128)(2,1)S(1)} %send.1), channel_id=1, replica_groups=mesh['zh'=8,'zp'=2,'z2'=2,'y'=4,'x'=4,'c'=2] {'zh','zp'}, dimensions={0} | all-to-all | bytes 524288 | tf_op jit(solution)/shard_map/all_to_all | solution.py:32
  64.4 1.0 spread.1
  65.4 14.6 %all-to-all-start.2 = ((bf16[16,208,128]{2,1,0:T(8,128)(2,1)}), bf16[16,208,128]{2,1,0:T(8,128)(2,1)S(1)}, u32[]{:S(2)}, u32[]{:S(2)}) async-start(bf16[16,208,128]{2,1,0:T(8,128)(2,1)} %get-tuple-element.12), calls=%async_computation.2 | async-start | bytes 1703936 | tf_op jit(solution)/shard_map/all_to_all | solution.py:32
  79.9 10.6 %all-gather = bf16[576,128]{1,0:T(8,128)(2,1)S(1)} all-gather(bf16[144,128]{1,0:T(8,128)(2,1)S(1)} %get-tuple-element.11), channel_id=2, replica_groups=mesh['zh'=8,'zp'=2,'z2'=2,'y'=4,'x'=4,'c'=2] {'y'}, dimensions={0}, use_global_device_ids=true | all-gather | bytes 184320 | tf_op jit(solution)/shard_map/all_gather | solution.py:286
  90.5 3.1 %all-to-all-done.2.key_ref = bf16[16,208,128]{2,1,0:T(8,128)(2,1)S(1)} async-done(((bf16[16,208,128]{2,1,0:T(8,128)(2,1)}), bf16[16,208,128]{2,1,0:T(8,128)(2,1)S(1)}, u32[]{:S(2)}, u32[]{:S(2)}) %all-to-all-start.2) | async-done | bytes 852000 | tf_op jit(solution)/shard_map/all_to_all | solution.py:32
  93.6 0.1 columns.1
  93.7 2.8 %collective-permute-start = (bf16[16,128,128]{2,1,0:T(8,128)(2,1)S(1)}, bf16[16,128,128]{2,1,0:T(8,128)(2,1)S(1)}, u32[]{:S(2)}, u32[]{:S(2)}) collective-permute-start(bf16[16,128,128]{2,1,0:T(8,128)(2,1)S(1)} %get-tuple-element.13), channel_id=1, source_target_pairs={{0,1},{1,0},{2,3},{3,2},{4,5},{5,4},{6,7},{7,6},{8,9},{9,8},{10,11... | collective-permute-start | bytes 1572872 | tf_op jit(solution)/shard_map/ppermute | solution.py:43
  96.5 0.1 stack.23.place_ref
  96.6 1.4 collective-permute-done.swapped_ref
  98.0 3.4 %attend.1 = bf16[4,144,128]{2,1,0:T(8,128)(2,1)} custom-call(s32[5]{0:T(128)S(1)} %stack.23.place_ref, bf16[4,144,128]{2,1,0:T(8,128)(2,1)S(1)} %bitcast.12, bf16[16,208,128]{2,1,0:T(8,128)(2,1)S(1)} %all-to-all-done.2.key_ref, bf16[16,128,128]{2,1,0:T(8,128)(2,1)S(1)} %collective-permute-done.swapped_ref), custom_call_target="tpu_custom_call" | custom-call | flops 536870912 | bytes 2097152 | tf_op jit(solution)/shard_map/attend/pallas_call | solution.py:295
  101.4 4.2 %all-to-all-start.3 = ((bf16[4,144,128]{2,1,0:T(8,128)(2,1)}), bf16[4,144,128]{2,1,0:T(8,128)(2,1)S(1)}, u32[]{:S(2)}, u32[]{:S(2)}) async-start(bf16[4,144,128]{2,1,0:T(8,128)(2,1)} %attend.1), calls=%async_computation.3 | async-start | bytes 294912 | tf_op jit(solution)/shard_map/all_to_all | solution.py:32
  105.6 4.6 %collective-permute-start.1 = (bf16[16,64,128]{2,1,0:T(8,128)(2,1)S(1)}, bf16[16,64,128]{2,1,0:T(8,128)(2,1)S(1)}, u32[]{:S(2)}, u32[]{:S(2)}) collective-permute-start(bf16[16,64,128]{2,1,0:T(8,128)(2,1)S(1)} %get-tuple-element.14.own_ref), channel_id=1, source_target_pairs={{0,24},{1,25},{2,26},{3,27},{4,28},{5,29},{6,30},{7,31},{8,0},{9,1... | collective-permute-start | bytes 786440 | tf_op jit(solution)/shard_map/ppermute | solution.py:43
  110.1 7.5 %collective-permute-start.4 = (bf16[16,64,128]{2,1,0:T(8,128)(2,1)S(1)}, bf16[16,64,128]{2,1,0:T(8,128)(2,1)S(1)}, u32[]{:S(2)}, u32[]{:S(2)}) collective-permute-start(bf16[16,64,128]{2,1,0:T(8,128)(2,1)S(1)} %get-tuple-element.14.own_ref), channel_id=1, source_target_pairs={{0,64},{1,65},{2,66},{3,67},{4,68},{5,69},{6,70},{7,71},{8,72},{9,... | collective-permute-start | bytes 786440 | tf_op jit(solution)/shard_map/ppermute | solution.py:43
  117.7 0.0 all-to-all-done.3.part_ref
  117.7 0.8 combine.1
  118.5 6.6 %all-to-all-start.4 = ((bf16[16,8,128]{2,1,0:T(8,128)(2,1)}), bf16[16,8,128]{2,1,0:T(8,128)(2,1)S(1)}, u32[]{:S(2)}, u32[]{:S(2)}) async-start(bf16[16,8,128]{2,1,0:T(8,128)(2,1)} %bitcast.10), calls=%async_computation.4 | async-start | bytes 65536 | tf_op jit(solution)/shard_map/all_to_all | solution.py:32
  125.1 0.0 collective-permute-done.1.refs_1_
  125.1 2.5 %collective-permute-start.2 = (bf16[16,64,128]{2,1,0:T(8,128)(2,1)S(1)}, bf16[16,64,128]{2,1,0:T(8,128)(2,1)S(1)}, u32[]{:S(2)}, u32[]{:S(2)}) collective-permute-start(bf16[16,64,128]{2,1,0:T(8,128)(2,1)S(1)} %collective-permute-done.1.refs_1_), channel_id=1, source_target_pairs={{0,24},{1,25},{2,26},{3,27},{4,28},{5,29},{6,30},{7,31},{8,0},{9,1... | collective-permute-start | bytes 786440 | tf_op jit(solution)/shard_map/ppermute | solution.py:43
  127.6 2.6 %collective-permute-done.4.block_ref = bf16[16,64,128]{2,1,0:T(8,128)(2,1)S(1)} collective-permute-done((bf16[16,64,128]{2,1,0:T(8,128)(2,1)S(1)}, bf16[16,64,128]{2,1,0:T(8,128)(2,1)S(1)}, u32[]{:S(2)}, u32[]{:S(2)}) %collective-permute-start.4) | collective-permute-done | bytes 262176 | tf_op jit(solution)/shard_map/ppermute | solution.py:43
  130.2 2.5 %collective-permute-start.5 = (bf16[16,64,128]{2,1,0:T(8,128)(2,1)S(1)}, bf16[16,64,128]{2,1,0:T(8,128)(2,1)S(1)}, u32[]{:S(2)}, u32[]{:S(2)}) collective-permute-start(bf16[16,64,128]{2,1,0:T(8,128)(2,1)S(1)} %after.1.refs_4_), channel_id=1, source_target_pairs={{0,24},{1,25},{2,26},{3,27},{4,28},{5,29},{6,30},{7,31},{8,0},{9,1... | collective-permute-start | bytes 786440 | tf_op jit(solution)/shard_map/ppermute | solution.py:43
  132.7 1.9 %collective-permute-start.6 = (bf16[16,64,128]{2,1,0:T(8,128)(2,1)S(1)}, bf16[16,64,128]{2,1,0:T(8,128)(2,1)S(1)}, u32[]{:S(2)}, u32[]{:S(2)}) collective-permute-start(bf16[16,64,128]{2,1,0:T(8,128)(2,1)S(1)} %after.1.refs_4_), channel_id=1, source_target_pairs={{0,16},{1,17},{2,18},{3,19},{4,20},{5,21},{6,22},{7,23},{8,24},{9,... | collective-permute-start | bytes 786440 | tf_op jit(solution)/shard_map/ppermute | solution.py:43
  134.6 2.8 %collective-permute-start.7 = (bf16[16,64,128]{2,1,0:T(8,128)(2,1)S(1)}, bf16[16,64,128]{2,1,0:T(8,128)(2,1)S(1)}, u32[]{:S(2)}, u32[]{:S(2)}) collective-permute-start(bf16[16,64,128]{2,1,0:T(8,128)(2,1)S(1)} %after.1.refs_4_), channel_id=1, source_target_pairs={{0,8},{1,9},{2,10},{3,11},{4,12},{5,13},{6,14},{7,15},{8,16},{9,17... | collective-permute-start | bytes 786440 | tf_op jit(solution)/shard_map/ppermute | solution.py:43
  137.4 3.7 %collective-permute-start.3 = (bf16[16,64,128]{2,1,0:T(8,128)(2,1)S(1)}, bf16[16,64,128]{2,1,0:T(8,128)(2,1)S(1)}, u32[]{:S(2)}, u32[]{:S(2)}) collective-permute-start(bf16[16,64,128]{2,1,0:T(8,128)(2,1)S(1)} %get-tuple-element.16.refs_0_), channel_id=1, source_target_pairs={{0,8},{1,9},{2,10},{3,11},{4,12},{5,13},{6,14},{7,15},{8,16},{9,17... | collective-permute-start | bytes 786440 | tf_op jit(solution)/shard_map/ppermute | solution.py:43
  141.1 4.9 %all-to-all-done.4 = bf16[16,8,128]{2,1,0:T(8,128)(2,1)S(1)} async-done(((bf16[16,8,128]{2,1,0:T(8,128)(2,1)}), bf16[16,8,128]{2,1,0:T(8,128)(2,1)S(1)}, u32[]{:S(2)}, u32[]{:S(2)}) %all-to-all-start.4) | async-done | bytes 32800 | tf_op jit(solution)/shard_map/all_to_all | solution.py:32
  146.0 0.7 broadcast_in_dim.10
  146.7 0.0 copy-start
  146.7 6.7 %all-to-all-start.5 = ((bf16[8,16,8,128]{3,2,1,0:T(8,128)(2,1)}), bf16[8,16,8,128]{3,2,1,0:T(8,128)(2,1)S(1)}, u32[]{:S(2)}, u32[]{:S(2)}) async-start(bf16[8,16,8,128]{3,2,1,0:T(8,128)(2,1)} %broadcast_in_dim.10), calls=%async_computation.5 | async-start | bytes 524288 | tf_op jit(solution)/shard_map/all_to_all | solution.py:32
  153.4 0.0 collective-permute-done.2.refs_2_
  153.4 0.0 collective-permute-done.5.refs_5_
  153.4 0.0 collective-permute-done.6.refs_6_
  153.4 0.0 collective-permute-done.7.refs_7_
  153.4 2.1 %collective-permute-done.3.refs_3_ = bf16[16,64,128]{2,1,0:T(8,128)(2,1)S(1)} collective-permute-done((bf16[16,64,128]{2,1,0:T(8,128)(2,1)S(1)}, bf16[16,64,128]{2,1,0:T(8,128)(2,1)S(1)}, u32[]{:S(2)}, u32[]{:S(2)}) %collective-permute-start.3) | collective-permute-done | bytes 262176 | tf_op jit(solution)/shard_map/ppermute | solution.py:43
  155.6 4.4 %all-to-all-done.5.attended_ref = bf16[8,16,8,128]{3,2,1,0:T(8,128)(2,1)S(1)} async-done(((bf16[8,16,8,128]{3,2,1,0:T(8,128)(2,1)}), bf16[8,16,8,128]{3,2,1,0:T(8,128)(2,1)S(1)}, u32[]{:S(2)}, u32[]{:S(2)}) %all-to-all-start.5) | async-done | bytes 262176 | tf_op jit(solution)/shard_map/all_to_all | solution.py:32
  159.9 0.0 copy-done
  159.9 2.0 %product.1 = bf16[64,512]{1,0:T(8,128)(2,1)} custom-call(s32[5]{0:T(128)S(1)} %stack.23.place_ref, bf16[8,16,8,128]{3,2,1,0:T(8,128)(2,1)S(1)} %all-to-all-done.5.attended_ref, bf16[16,64,128]{2,1,0:T(8,128)(2,1)S(1)} %get-tuple-element.16.refs_0_, bf16[16,64,128]{2,1,0:T(8,128)(2,1)S(1)} %collective-permute-done.1.refs_1_, ...), custom_call_target="tpu_custom_call" | custom-call | flops 134217728 | bytes 3145728 | tf_op jit(solution)/shard_map/product/pallas_call | solution.py:329
  (5 shorter events, 0.1 us)
Async XLA Ops:
  1.4 22.4 %all-to-all-start = ((bf16[8,24,256]{2,1,0:T(8,128)(2,1)}), bf16[8,24,256]{2,1,0:T(8,128)(2,1)S(1)}, u32[]{:S(2)}, u32[]{:S(2)}) async-start(bf16[8,24,256]{2,1,0:T(8,128)(2,1)} %pad_maximum_fusion), calls=%async_computation | async-start | bytes 196608 | tf_op jit(solution)/shard_map/all_to_all | solution.py:32
  18.8 0.7 copy-start.2
  18.8 0.9 copy-start.1
  65.4 28.3 %all-to-all-start.2 = ((bf16[16,208,128]{2,1,0:T(8,128)(2,1)}), bf16[16,208,128]{2,1,0:T(8,128)(2,1)S(1)}, u32[]{:S(2)}, u32[]{:S(2)}) async-start(bf16[16,208,128]{2,1,0:T(8,128)(2,1)} %get-tuple-element.12), calls=%async_computation.2 | async-start | bytes 1703936 | tf_op jit(solution)/shard_map/all_to_all | solution.py:32
  93.7 4.3 %collective-permute-start = (bf16[16,128,128]{2,1,0:T(8,128)(2,1)S(1)}, bf16[16,128,128]{2,1,0:T(8,128)(2,1)S(1)}, u32[]{:S(2)}, u32[]{:S(2)}) collective-permute-start(bf16[16,128,128]{2,1,0:T(8,128)(2,1)S(1)} %get-tuple-element.13), channel_id=1, source_target_pairs={{0,1},{1,0},{2,3},{3,2},{4,5},{5,4},{6,7},{7,6},{8,9},{9,8},{10,11... | collective-permute-start | bytes 1572872 | tf_op jit(solution)/shard_map/ppermute | solution.py:43
  101.4 16.3 %all-to-all-start.3 = ((bf16[4,144,128]{2,1,0:T(8,128)(2,1)}), bf16[4,144,128]{2,1,0:T(8,128)(2,1)S(1)}, u32[]{:S(2)}, u32[]{:S(2)}) async-start(bf16[4,144,128]{2,1,0:T(8,128)(2,1)} %attend.1), calls=%async_computation.3 | async-start | bytes 294912 | tf_op jit(solution)/shard_map/all_to_all | solution.py:32
  105.6 19.5 %collective-permute-start.1 = (bf16[16,64,128]{2,1,0:T(8,128)(2,1)S(1)}, bf16[16,64,128]{2,1,0:T(8,128)(2,1)S(1)}, u32[]{:S(2)}, u32[]{:S(2)}) collective-permute-start(bf16[16,64,128]{2,1,0:T(8,128)(2,1)S(1)} %get-tuple-element.14.own_ref), channel_id=1, source_target_pairs={{0,24},{1,25},{2,26},{3,27},{4,28},{5,29},{6,30},{7,31},{8,0},{9,1... | collective-permute-start | bytes 786440 | tf_op jit(solution)/shard_map/ppermute | solution.py:43
  110.1 20.1 %collective-permute-start.4 = (bf16[16,64,128]{2,1,0:T(8,128)(2,1)S(1)}, bf16[16,64,128]{2,1,0:T(8,128)(2,1)S(1)}, u32[]{:S(2)}, u32[]{:S(2)}) collective-permute-start(bf16[16,64,128]{2,1,0:T(8,128)(2,1)S(1)} %get-tuple-element.14.own_ref), channel_id=1, source_target_pairs={{0,64},{1,65},{2,66},{3,67},{4,68},{5,69},{6,70},{7,71},{8,72},{9,... | collective-permute-start | bytes 786440 | tf_op jit(solution)/shard_map/ppermute | solution.py:43
  118.5 27.5 %all-to-all-start.4 = ((bf16[16,8,128]{2,1,0:T(8,128)(2,1)}), bf16[16,8,128]{2,1,0:T(8,128)(2,1)S(1)}, u32[]{:S(2)}, u32[]{:S(2)}) async-start(bf16[16,8,128]{2,1,0:T(8,128)(2,1)} %bitcast.10), calls=%async_computation.4 | async-start | bytes 65536 | tf_op jit(solution)/shard_map/all_to_all | solution.py:32
  125.1 28.3 %collective-permute-start.2 = (bf16[16,64,128]{2,1,0:T(8,128)(2,1)S(1)}, bf16[16,64,128]{2,1,0:T(8,128)(2,1)S(1)}, u32[]{:S(2)}, u32[]{:S(2)}) collective-permute-start(bf16[16,64,128]{2,1,0:T(8,128)(2,1)S(1)} %collective-permute-done.1.refs_1_), channel_id=1, source_target_pairs={{0,24},{1,25},{2,26},{3,27},{4,28},{5,29},{6,30},{7,31},{8,0},{9,1... | collective-permute-start | bytes 786440 | tf_op jit(solution)/shard_map/ppermute | solution.py:43
  130.2 23.2 %collective-permute-start.5 = (bf16[16,64,128]{2,1,0:T(8,128)(2,1)S(1)}, bf16[16,64,128]{2,1,0:T(8,128)(2,1)S(1)}, u32[]{:S(2)}, u32[]{:S(2)}) collective-permute-start(bf16[16,64,128]{2,1,0:T(8,128)(2,1)S(1)} %after.1.refs_4_), channel_id=1, source_target_pairs={{0,24},{1,25},{2,26},{3,27},{4,28},{5,29},{6,30},{7,31},{8,0},{9,1... | collective-permute-start | bytes 786440 | tf_op jit(solution)/shard_map/ppermute | solution.py:43
  132.7 20.7 %collective-permute-start.6 = (bf16[16,64,128]{2,1,0:T(8,128)(2,1)S(1)}, bf16[16,64,128]{2,1,0:T(8,128)(2,1)S(1)}, u32[]{:S(2)}, u32[]{:S(2)}) collective-permute-start(bf16[16,64,128]{2,1,0:T(8,128)(2,1)S(1)} %after.1.refs_4_), channel_id=1, source_target_pairs={{0,16},{1,17},{2,18},{3,19},{4,20},{5,21},{6,22},{7,23},{8,24},{9,... | collective-permute-start | bytes 786440 | tf_op jit(solution)/shard_map/ppermute | solution.py:43
  134.6 18.8 %collective-permute-start.7 = (bf16[16,64,128]{2,1,0:T(8,128)(2,1)S(1)}, bf16[16,64,128]{2,1,0:T(8,128)(2,1)S(1)}, u32[]{:S(2)}, u32[]{:S(2)}) collective-permute-start(bf16[16,64,128]{2,1,0:T(8,128)(2,1)S(1)} %after.1.refs_4_), channel_id=1, source_target_pairs={{0,8},{1,9},{2,10},{3,11},{4,12},{5,13},{6,14},{7,15},{8,16},{9,17... | collective-permute-start | bytes 786440 | tf_op jit(solution)/shard_map/ppermute | solution.py:43
  137.4 18.1 %collective-permute-start.3 = (bf16[16,64,128]{2,1,0:T(8,128)(2,1)S(1)}, bf16[16,64,128]{2,1,0:T(8,128)(2,1)S(1)}, u32[]{:S(2)}, u32[]{:S(2)}) collective-permute-start(bf16[16,64,128]{2,1,0:T(8,128)(2,1)S(1)} %get-tuple-element.16.refs_0_), channel_id=1, source_target_pairs={{0,8},{1,9},{2,10},{3,11},{4,12},{5,13},{6,14},{7,15},{8,16},{9,17... | collective-permute-start | bytes 786440 | tf_op jit(solution)/shard_map/ppermute | solution.py:43
  146.7 13.2 %copy-start = (bf16[64,512]{1,0:T(8,128)(2,1)S(1)}, bf16[64,512]{1,0:T(8,128)(2,1)}, u32[]{:S(2)}) copy-start(bf16[64,512]{1,0:T(8,128)(2,1)} %refs_8_.1) | copy-start | bytes 196612
  146.7 13.2 %all-to-all-start.5 = ((bf16[8,16,8,128]{3,2,1,0:T(8,128)(2,1)}), bf16[8,16,8,128]{3,2,1,0:T(8,128)(2,1)S(1)}, u32[]{:S(2)}, u32[]{:S(2)}) async-start(bf16[8,16,8,128]{3,2,1,0:T(8,128)(2,1)} %broadcast_in_dim.10), calls=%async_computation.5 | async-start | bytes 524288 | tf_op jit(solution)/shard_map/all_to_all | solution.py:32

commit v11 on v9

--- a/solution.py
+++ b/solution.py
@@ -308,14 +308,14 @@
         return moved(block, lambda z, y, x, c: (z, (y - k) % 4, x, c))
 
     other = moved(own, lambda z, y, x, c: (z ^ 2, y, x, c))
-    next_own = from_y(own, 1)
+    last_own = from_y(own, 3)
     attended, own, other = call(
         combine_kernel,
         [jax.ShapeDtypeStruct((ROWS, HEAD_DIM), bf16), held, held],
         [VMEM] * 3,
         "combine",
     )(parts, own, other)
-    weights = [own, next_own, from_y(next_own, 1), from_y(own, 3)]
+    weights = [own, from_y(own, 1), from_y(last_own, 3), last_own]
     weights += [other] + [from_y(other, k) for k in (1, 2, 3)]
 
     back = exchange(attended.reshape(planes, EACH, HEAD_DIM), PLANES)

time: 162 us -> 162 us (level)
  starting transfers between devices: 79.7 us -> 77.8 us
  waiting for transfers between devices: 19.6 us -> 21.5 us
    ppermute x8, starting transfers between devices: 30.4 us -> 28.5 us  [moved(): lax.ppermute(block, names, [(flat(*p), flat(*where(*p))) for p in places])]
  transfers between devices with their start and end apart: 13 -> 13, of which waited for: 7 -> 6; matrix products, arithmetic and copies ran while one was open for 1% -> 1% of each run, Pallas kernels for 3% -> 3%
where the time goes in v11:
time: 162 us; the launch traced here: 161 us
  starting transfers between devices  77.8 us (48%)
  blocking collectives  51 us (31%)
  waiting for transfers between devices  21.5 us (13%)
  Pallas kernels  7.28 us (4%)
    all_to_all x5, starting transfers between devices, exchange(): return lax.all_to_all(tiles, axes, split_axis=0, concat_axis=0, tiled=True)  49.3 us
    all_to_all x1, blocking collectives, exchange(): return lax.all_to_all(tiles, axes, split_axis=0, concat_axis=0, tiled=True)  40.5 us
    ppermute x8, starting transfers between devices, moved(): lax.ppermute(block, names, [(flat(*p), flat(*where(*p))) for p in places])  28.5 us
    all_to_all x5, waiting for transfers between devices, exchange(): return lax.all_to_all(tiles, axes, split_axis=0, concat_axis=0, tiled=True)  20.2 us
    all_gather x1, blocking collectives, shards(): queries = lax.all_gather(queries, QUERY_AXES)  10.6 us
    pallas_call x1, Pallas kernels, shards(): call(attend_kernel, jax.ShapeDtypeStruct((spread, ROWS + 16, LANES), bf16...  3.38 us
  transfers between devices with their start and end apart: 13, of which 6 were waited for; matrix products, arithmetic and copies ran while one was open for 1% of the time, Pallas kernels for 3%

profile of v11, /device:TPU:1, one launch (start us, length us, event | category | flops | bytes accessed | tf_op | source)
XLA Modules:
  0.0 160.9 jit_solution(12502798521744570932)
XLA Ops:
  0.0 1.4 pad_maximum_fusion
  1.4 17.4 %all-to-all-start = ((bf16[8,24,256]{2,1,0:T(8,128)(2,1)}), bf16[8,24,256]{2,1,0:T(8,128)(2,1)S(1)}, u32[]{:S(2)}, u32[]{:S(2)}) async-start(bf16[8,24,256]{2,1,0:T(8,128)(2,1)} %pad_maximum_fusion), calls=%async_computation | async-start | bytes 196608 | tf_op jit(solution)/shard_map/all_to_all | solution.py:32
  18.8 0.0 copy-start.2
  18.8 0.0 copy-start.1
  18.9 0.7 copy-done.2
  19.5 0.1 pad_add_fusion
  19.6 0.1 dynamic-slice_convert_fusion
  19.7 0.1 tile.10
  19.8 0.0 copy-done.1
  19.8 4.1 %all-to-all-done.rows_ref = bf16[8,24,256]{2,1,0:T(8,128)(2,1)S(1)} async-done(((bf16[8,24,256]{2,1,0:T(8,128)(2,1)}), bf16[8,24,256]{2,1,0:T(8,128)(2,1)S(1)}, u32[]{:S(2)}, u32[]{:S(2)}) %all-to-all-start) | async-done | bytes 98336 | tf_op jit(solution)/shard_map/all_to_all | solution.py:32
  23.9 40.5 %all_to_all.30.came_ref = bf16[16,64,128]{2,1,0:T(8,128)(2,1)S(1)} all-to-all(bf16[16,64,128]{2,1,0:T(8,128)(2,1)S(1)} %send.1), channel_id=1, replica_groups=mesh['zh'=8,'zp'=2,'z2'=2,'y'=4,'x'=4,'c'=2] {'zh','zp'}, dimensions={0} | all-to-all | bytes 524288 | tf_op jit(solution)/shard_map/all_to_all | solution.py:32
  64.4 1.0 spread.1
  65.4 14.6 %all-to-all-start.2 = ((bf16[16,208,128]{2,1,0:T(8,128)(2,1)}), bf16[16,208,128]{2,1,0:T(8,128)(2,1)S(1)}, u32[]{:S(2)}, u32[]{:S(2)}) async-start(bf16[16,208,128]{2,1,0:T(8,128)(2,1)} %get-tuple-element.13), calls=%async_computation.2 | async-start | bytes 1703936 | tf_op jit(solution)/shard_map/all_to_all | solution.py:32
  79.9 10.6 %all-gather = bf16[576,128]{1,0:T(8,128)(2,1)S(1)} all-gather(bf16[144,128]{1,0:T(8,128)(2,1)S(1)} %get-tuple-element.12), channel_id=2, replica_groups=mesh['zh'=8,'zp'=2,'z2'=2,'y'=4,'x'=4,'c'=2] {'y'}, dimensions={0}, use_global_device_ids=true | all-gather | bytes 184320 | tf_op jit(solution)/shard_map/all_gather | solution.py:283
  90.5 3.1 %all-to-all-done.2.key_ref = bf16[16,208,128]{2,1,0:T(8,128)(2,1)S(1)} async-done(((bf16[16,208,128]{2,1,0:T(8,128)(2,1)}), bf16[16,208,128]{2,1,0:T(8,128)(2,1)S(1)}, u32[]{:S(2)}, u32[]{:S(2)}) %all-to-all-start.2) | async-done | bytes 852000 | tf_op jit(solution)/shard_map/all_to_all | solution.py:32
  93.6 0.1 columns.1
  93.7 2.8 %collective-permute-start = (bf16[16,128,128]{2,1,0:T(8,128)(2,1)S(1)}, bf16[16,128,128]{2,1,0:T(8,128)(2,1)S(1)}, u32[]{:S(2)}, u32[]{:S(2)}) collective-permute-start(bf16[16,128,128]{2,1,0:T(8,128)(2,1)S(1)} %get-tuple-element.14), channel_id=1, source_target_pairs={{0,1},{1,0},{2,3},{3,2},{4,5},{5,4},{6,7},{7,6},{8,9},{9,8},{10,11... | collective-permute-start | bytes 1572872 | tf_op jit(solution)/shard_map/ppermute | solution.py:43
  96.5 7.5 %collective-permute-start.1 = (bf16[16,64,128]{2,1,0:T(8,128)(2,1)S(1)}, bf16[16,64,128]{2,1,0:T(8,128)(2,1)S(1)}, u32[]{:S(2)}, u32[]{:S(2)}) collective-permute-start(bf16[16,64,128]{2,1,0:T(8,128)(2,1)S(1)} %get-tuple-element.15.own_ref), channel_id=1, source_target_pairs={{0,64},{1,65},{2,66},{3,67},{4,68},{5,69},{6,70},{7,71},{8,72},{9,... | collective-permute-start | bytes 786440 | tf_op jit(solution)/shard_map/ppermute | solution.py:43
  104.0 0.1 stack.23.place_ref
  104.1 0.0 collective-permute-done.swapped_ref
  104.1 3.4 %attend.1 = bf16[4,144,128]{2,1,0:T(8,128)(2,1)} custom-call(s32[5]{0:T(128)S(1)} %stack.23.place_ref, bf16[4,144,128]{2,1,0:T(8,128)(2,1)S(1)} %bitcast.12, bf16[16,208,128]{2,1,0:T(8,128)(2,1)S(1)} %all-to-all-done.2.key_ref, bf16[16,128,128]{2,1,0:T(8,128)(2,1)S(1)} %collective-permute-done.swapped_ref), custom_call_target="tpu_custom_call" | custom-call | flops 536870912 | bytes 2097152 | tf_op jit(solution)/shard_map/attend/pallas_call | solution.py:292
  107.5 4.2 %all-to-all-start.3 = ((bf16[4,144,128]{2,1,0:T(8,128)(2,1)}), bf16[4,144,128]{2,1,0:T(8,128)(2,1)S(1)}, u32[]{:S(2)}, u32[]{:S(2)}) async-start(bf16[4,144,128]{2,1,0:T(8,128)(2,1)} %attend.1), calls=%async_computation.3 | async-start | bytes 294912 | tf_op jit(solution)/shard_map/all_to_all | solution.py:32
  111.7 3.4 %collective-permute-start.3 = (bf16[16,64,128]{2,1,0:T(8,128)(2,1)S(1)}, bf16[16,64,128]{2,1,0:T(8,128)(2,1)S(1)}, u32[]{:S(2)}, u32[]{:S(2)}) collective-permute-start(bf16[16,64,128]{2,1,0:T(8,128)(2,1)S(1)} %get-tuple-element.15.own_ref), channel_id=1, source_target_pairs={{0,8},{1,9},{2,10},{3,11},{4,12},{5,13},{6,14},{7,15},{8,16},{9,17... | collective-permute-start | bytes 786440 | tf_op jit(solution)/shard_map/ppermute | solution.py:43
  115.0 1.4 collective-permute-done.1.other_ref
  116.4 0.2 all-to-all-done.3.part_ref
  116.6 0.8 combine.1
  117.4 7.0 %all-to-all-start.4 = ((bf16[16,8,128]{2,1,0:T(8,128)(2,1)}), bf16[16,8,128]{2,1,0:T(8,128)(2,1)S(1)}, u32[]{:S(2)}, u32[]{:S(2)}) async-start(bf16[16,8,128]{2,1,0:T(8,128)(2,1)} %bitcast.10), calls=%async_computation.4 | async-start | bytes 65536 | tf_op jit(solution)/shard_map/all_to_all | solution.py:32
  124.4 0.0 collective-permute-done.3.refs_3_
  124.4 3.2 %collective-permute-start.4 = (bf16[16,64,128]{2,1,0:T(8,128)(2,1)S(1)}, bf16[16,64,128]{2,1,0:T(8,128)(2,1)S(1)}, u32[]{:S(2)}, u32[]{:S(2)}) collective-permute-start(bf16[16,64,128]{2,1,0:T(8,128)(2,1)S(1)} %collective-permute-done.3.refs_3_), channel_id=1, source_target_pairs={{0,8},{1,9},{2,10},{3,11},{4,12},{5,13},{6,14},{7,15},{8,16},{9,17... | collective-permute-start | bytes 786440 | tf_op jit(solution)/shard_map/ppermute | solution.py:43
  127.6 3.4 %collective-permute-start.2 = (bf16[16,64,128]{2,1,0:T(8,128)(2,1)S(1)}, bf16[16,64,128]{2,1,0:T(8,128)(2,1)S(1)}, u32[]{:S(2)}, u32[]{:S(2)}) collective-permute-start(bf16[16,64,128]{2,1,0:T(8,128)(2,1)S(1)} %get-tuple-element.17.refs_0_), channel_id=1, source_target_pairs={{0,24},{1,25},{2,26},{3,27},{4,28},{5,29},{6,30},{7,31},{8,0},{9,1... | collective-permute-start | bytes 786440 | tf_op jit(solution)/shard_map/ppermute | solution.py:43
  130.9 3.4 %collective-permute-start.5 = (bf16[16,64,128]{2,1,0:T(8,128)(2,1)S(1)}, bf16[16,64,128]{2,1,0:T(8,128)(2,1)S(1)}, u32[]{:S(2)}, u32[]{:S(2)}) collective-permute-start(bf16[16,64,128]{2,1,0:T(8,128)(2,1)S(1)} %get-tuple-element.18.refs_4_), channel_id=1, source_target_pairs={{0,24},{1,25},{2,26},{3,27},{4,28},{5,29},{6,30},{7,31},{8,0},{9,1... | collective-permute-start | bytes 786440 | tf_op jit(solution)/shard_map/ppermute | solution.py:43
  134.3 2.3 %collective-permute-start.6 = (bf16[16,64,128]{2,1,0:T(8,128)(2,1)S(1)}, bf16[16,64,128]{2,1,0:T(8,128)(2,1)S(1)}, u32[]{:S(2)}, u32[]{:S(2)}) collective-permute-start(bf16[16,64,128]{2,1,0:T(8,128)(2,1)S(1)} %get-tuple-element.18.refs_4_), channel_id=1, source_target_pairs={{0,16},{1,17},{2,18},{3,19},{4,20},{5,21},{6,22},{7,23},{8,24},{9,... | collective-permute-start | bytes 786440 | tf_op jit(solution)/shard_map/ppermute | solution.py:43
  136.6 2.6 %collective-permute-start.7 = (bf16[16,64,128]{2,1,0:T(8,128)(2,1)S(1)}, bf16[16,64,128]{2,1,0:T(8,128)(2,1)S(1)}, u32[]{:S(2)}, u32[]{:S(2)}) collective-permute-start(bf16[16,64,128]{2,1,0:T(8,128)(2,1)S(1)} %get-tuple-element.18.refs_4_), channel_id=1, source_target_pairs={{0,8},{1,9},{2,10},{3,11},{4,12},{5,13},{6,14},{7,15},{8,16},{9,17... | collective-permute-start | bytes 786440 | tf_op jit(solution)/shard_map/ppermute | solution.py:43
  139.2 6.3 %all-to-all-done.4 = bf16[16,8,128]{2,1,0:T(8,128)(2,1)S(1)} async-done(((bf16[16,8,128]{2,1,0:T(8,128)(2,1)}), bf16[16,8,128]{2,1,0:T(8,128)(2,1)S(1)}, u32[]{:S(2)}, u32[]{:S(2)}) %all-to-all-start.4) | async-done | bytes 32800 | tf_op jit(solution)/shard_map/all_to_all | solution.py:32
  145.5 0.7 broadcast_in_dim.10
  146.2 0.0 copy-start
  146.2 6.2 %all-to-all-start.5 = ((bf16[8,16,8,128]{3,2,1,0:T(8,128)(2,1)}), bf16[8,16,8,128]{3,2,1,0:T(8,128)(2,1)S(1)}, u32[]{:S(2)}, u32[]{:S(2)}) async-start(bf16[8,16,8,128]{3,2,1,0:T(8,128)(2,1)} %broadcast_in_dim.10), calls=%async_computation.5 | async-start | bytes 524288 | tf_op jit(solution)/shard_map/all_to_all | solution.py:32
  152.4 0.0 collective-permute-done.4.refs_2_
  152.4 0.0 collective-permute-done.2.refs_1_
  152.4 0.0 collective-permute-done.5.refs_5_
  152.4 0.0 collective-permute-done.6.refs_6_
  152.4 0.0 collective-permute-done.7.refs_7_
  152.4 6.5 %all-to-all-done.5.attended_ref = bf16[8,16,8,128]{3,2,1,0:T(8,128)(2,1)S(1)} async-done(((bf16[8,16,8,128]{3,2,1,0:T(8,128)(2,1)}), bf16[8,16,8,128]{3,2,1,0:T(8,128)(2,1)S(1)}, u32[]{:S(2)}, u32[]{:S(2)}) %all-to-all-start.5) | async-done | bytes 262176 | tf_op jit(solution)/shard_map/all_to_all | solution.py:32
  158.9 0.0 copy-done
  158.9 2.0 %product.1 = bf16[64,512]{1,0:T(8,128)(2,1)} custom-call(s32[5]{0:T(128)S(1)} %stack.23.place_ref, bf16[8,16,8,128]{3,2,1,0:T(8,128)(2,1)S(1)} %all-to-all-done.5.attended_ref, bf16[16,64,128]{2,1,0:T(8,128)(2,1)S(1)} %get-tuple-element.17.refs_0_, bf16[16,64,128]{2,1,0:T(8,128)(2,1)S(1)} %collective-permute-done.2.refs_1_, ...), custom_call_target="tpu_custom_call" | custom-call | flops 134217728 | bytes 3145728 | tf_op jit(solution)/shard_map/product/pallas_call | solution.py:323
  (4 shorter events, 0.1 us)
Async XLA Ops:
  1.4 22.4 %all-to-all-start = ((bf16[8,24,256]{2,1,0:T(8,128)(2,1)}), bf16[8,24,256]{2,1,0:T(8,128)(2,1)S(1)}, u32[]{:S(2)}, u32[]{:S(2)}) async-start(bf16[8,24,256]{2,1,0:T(8,128)(2,1)} %pad_maximum_fusion), calls=%async_computation | async-start | bytes 196608 | tf_op jit(solution)/shard_map/all_to_all | solution.py:32
  18.8 0.7 copy-start.2
  18.8 0.9 copy-start.1
  65.4 28.3 %all-to-all-start.2 = ((bf16[16,208,128]{2,1,0:T(8,128)(2,1)}), bf16[16,208,128]{2,1,0:T(8,128)(2,1)S(1)}, u32[]{:S(2)}, u32[]{:S(2)}) async-start(bf16[16,208,128]{2,1,0:T(8,128)(2,1)} %get-tuple-element.13), calls=%async_computation.2 | async-start | bytes 1703936 | tf_op jit(solution)/shard_map/all_to_all | solution.py:32
  93.7 10.4 %collective-permute-start = (bf16[16,128,128]{2,1,0:T(8,128)(2,1)S(1)}, bf16[16,128,128]{2,1,0:T(8,128)(2,1)S(1)}, u32[]{:S(2)}, u32[]{:S(2)}) collective-permute-start(bf16[16,128,128]{2,1,0:T(8,128)(2,1)S(1)} %get-tuple-element.14), channel_id=1, source_target_pairs={{0,1},{1,0},{2,3},{3,2},{4,5},{5,4},{6,7},{7,6},{8,9},{9,8},{10,11... | collective-permute-start | bytes 1572872 | tf_op jit(solution)/shard_map/ppermute | solution.py:43
  96.5 19.9 %collective-permute-start.1 = (bf16[16,64,128]{2,1,0:T(8,128)(2,1)S(1)}, bf16[16,64,128]{2,1,0:T(8,128)(2,1)S(1)}, u32[]{:S(2)}, u32[]{:S(2)}) collective-permute-start(bf16[16,64,128]{2,1,0:T(8,128)(2,1)S(1)} %get-tuple-element.15.own_ref), channel_id=1, source_target_pairs={{0,64},{1,65},{2,66},{3,67},{4,68},{5,69},{6,70},{7,71},{8,72},{9,... | collective-permute-start | bytes 786440 | tf_op jit(solution)/shard_map/ppermute | solution.py:43
  107.5 9.1 %all-to-all-start.3 = ((bf16[4,144,128]{2,1,0:T(8,128)(2,1)}), bf16[4,144,128]{2,1,0:T(8,128)(2,1)S(1)}, u32[]{:S(2)}, u32[]{:S(2)}) async-start(bf16[4,144,128]{2,1,0:T(8,128)(2,1)} %attend.1), calls=%async_computation.3 | async-start | bytes 294912 | tf_op jit(solution)/shard_map/all_to_all | solution.py:32
  111.7 12.7 %collective-permute-start.3 = (bf16[16,64,128]{2,1,0:T(8,128)(2,1)S(1)}, bf16[16,64,128]{2,1,0:T(8,128)(2,1)S(1)}, u32[]{:S(2)}, u32[]{:S(2)}) collective-permute-start(bf16[16,64,128]{2,1,0:T(8,128)(2,1)S(1)} %get-tuple-element.15.own_ref), channel_id=1, source_target_pairs={{0,8},{1,9},{2,10},{3,11},{4,12},{5,13},{6,14},{7,15},{8,16},{9,17... | collective-permute-start | bytes 786440 | tf_op jit(solution)/shard_map/ppermute | solution.py:43
  117.4 28.1 %all-to-all-start.4 = ((bf16[16,8,128]{2,1,0:T(8,128)(2,1)}), bf16[16,8,128]{2,1,0:T(8,128)(2,1)S(1)}, u32[]{:S(2)}, u32[]{:S(2)}) async-start(bf16[16,8,128]{2,1,0:T(8,128)(2,1)} %bitcast.10), calls=%async_computation.4 | async-start | bytes 65536 | tf_op jit(solution)/shard_map/all_to_all | solution.py:32
  124.4 28.0 %collective-permute-start.4 = (bf16[16,64,128]{2,1,0:T(8,128)(2,1)S(1)}, bf16[16,64,128]{2,1,0:T(8,128)(2,1)S(1)}, u32[]{:S(2)}, u32[]{:S(2)}) collective-permute-start(bf16[16,64,128]{2,1,0:T(8,128)(2,1)S(1)} %collective-permute-done.3.refs_3_), channel_id=1, source_target_pairs={{0,8},{1,9},{2,10},{3,11},{4,12},{5,13},{6,14},{7,15},{8,16},{9,17... | collective-permute-start | bytes 786440 | tf_op jit(solution)/shard_map/ppermute | solution.py:43
  127.6 24.8 %collective-permute-start.2 = (bf16[16,64,128]{2,1,0:T(8,128)(2,1)S(1)}, bf16[16,64,128]{2,1,0:T(8,128)(2,1)S(1)}, u32[]{:S(2)}, u32[]{:S(2)}) collective-permute-start(bf16[16,64,128]{2,1,0:T(8,128)(2,1)S(1)} %get-tuple-element.17.refs_0_), channel_id=1, source_target_pairs={{0,24},{1,25},{2,26},{3,27},{4,28},{5,29},{6,30},{7,31},{8,0},{9,1... | collective-permute-start | bytes 786440 | tf_op jit(solution)/shard_map/ppermute | solution.py:43
  130.9 21.5 %collective-permute-start.5 = (bf16[16,64,128]{2,1,0:T(8,128)(2,1)S(1)}, bf16[16,64,128]{2,1,0:T(8,128)(2,1)S(1)}, u32[]{:S(2)}, u32[]{:S(2)}) collective-permute-start(bf16[16,64,128]{2,1,0:T(8,128)(2,1)S(1)} %get-tuple-element.18.refs_4_), channel_id=1, source_target_pairs={{0,24},{1,25},{2,26},{3,27},{4,28},{5,29},{6,30},{7,31},{8,0},{9,1... | collective-permute-start | bytes 786440 | tf_op jit(solution)/shard_map/ppermute | solution.py:43
  134.3 18.1 %collective-permute-start.6 = (bf16[16,64,128]{2,1,0:T(8,128)(2,1)S(1)}, bf16[16,64,128]{2,1,0:T(8,128)(2,1)S(1)}, u32[]{:S(2)}, u32[]{:S(2)}) collective-permute-start(bf16[16,64,128]{2,1,0:T(8,128)(2,1)S(1)} %get-tuple-element.18.refs_4_), channel_id=1, source_target_pairs={{0,16},{1,17},{2,18},{3,19},{4,20},{5,21},{6,22},{7,23},{8,24},{9,... | collective-permute-start | bytes 786440 | tf_op jit(solution)/shard_map/ppermute | solution.py:43
  136.6 15.9 %collective-permute-start.7 = (bf16[16,64,128]{2,1,0:T(8,128)(2,1)S(1)}, bf16[16,64,128]{2,1,0:T(8,128)(2,1)S(1)}, u32[]{:S(2)}, u32[]{:S(2)}) collective-permute-start(bf16[16,64,128]{2,1,0:T(8,128)(2,1)S(1)} %get-tuple-element.18.refs_4_), channel_id=1, source_target_pairs={{0,8},{1,9},{2,10},{3,11},{4,12},{5,13},{6,14},{7,15},{8,16},{9,17... | collective-permute-start | bytes 786440 | tf_op jit(solution)/shard_map/ppermute | solution.py:43
  146.2 12.7 %copy-start = (bf16[64,512]{1,0:T(8,128)(2,1)S(1)}, bf16[64,512]{1,0:T(8,128)(2,1)}, u32[]{:S(2)}) copy-start(bf16[64,512]{1,0:T(8,128)(2,1)} %refs_8_.1) | copy-start | bytes 196612
  146.2 12.7 %all-to-all-start.5 = ((bf16[8,16,8,128]{3,2,1,0:T(8,128)(2,1)}), bf16[8,16,8,128]{3,2,1,0:T(8,128)(2,1)S(1)}, u32[]{:S(2)}, u32[]{:S(2)}) async-start(bf16[8,16,8,128]{3,2,1,0:T(8,128)(2,1)} %broadcast_in_dim.10), calls=%async_computation.5 | async-start | bytes 524288 | tf_op jit(solution)/shard_map/all_to_all | solution.py:32
